TPU v7x, 128 devices: a whole 4x4x4 slice. The times are simulated.
128 devices in a mesh: leaf: 32 (over y, z, core), sub: 4 (over x).
Axes of the slice: x: 4, y: 4, z: 4, core: 2. Of those that a mesh axis runs over, the one named last changes fastest.
Arguments:
- loads: bfloat16 [16, 1048576], P(None, ('leaf', 'sub')), may hold values from -6 to 6
- col_basis: bfloat16 [8192, 128, 64], P(('leaf', 'sub')), may hold values from -0.5 to 0.5
- row_basis: bfloat16 [8192, 128, 64], P(('leaf', 'sub')), may hold values from -0.75 to 0.75
- near_blocks: bfloat16 [8192, 6, 128, 128], P(('leaf', 'sub')), may hold values from -0.21875 to 0.21875
- near_src: int32 [8192, 6], P(('leaf', 'sub')), may hold values from 0 to 8191, as said below
- up_leaf: bfloat16 [8192, 64, 64], P(('leaf', 'sub')), may hold values from -0.25 to 0.25
- down_leaf: bfloat16 [8192, 64, 64], P(('leaf', 'sub')), may hold values from -0.75 to 0.75
- up_node: bfloat16 [1024, 64, 64], P(('leaf', 'sub')), may hold values from -0.25 to 0.25
- down_node: bfloat16 [1024, 64, 64], P(('leaf', 'sub')), may hold values from -0.75 to 0.75
- up_group: bfloat16 [128, 64, 64], P(('leaf', 'sub')), may hold values from -0.375 to 0.375
- down_group: bfloat16 [128, 64, 64], P(('leaf', 'sub')), may hold values from -0.75 to 0.75
- up_top: bfloat16 [32, 64, 64], replicated, may hold values from -0.375 to 0.375
- downward_top_transfer: bfloat16 [32, 64, 64], replicated, may hold values from -0.75 to 0.75
- coupling: bfloat16 [316, 64, 64], replicated, may hold values from -0.25 to 0.25
- send_table: int32 [128, 21, 48], P(('leaf', 'sub')), may hold values from 0 to 63
- distant_leaf_slot_index: int32 [8192, 8], P(('leaf', 'sub')), may hold values from 0 to 1007, as said below
- far_leaf_type: int32 [8192, 8], P(('leaf', 'sub')), may hold values from 0 to 315
- far_group_src: int32 [32, 8], P('leaf'), may hold values from 0 to 31
- far_group_type: int32 [32, 8], P('leaf'), may hold values from 0 to 315
- far_top_src: int32 [8, 8], replicated, may hold values from 0 to 7
- far_top_type: int32 [8, 8], replicated, may hold values from 0 to 315
Outputs:
- potential: float32 [16, 1048576], P(None, ('leaf', 'sub'))
Inputs may be any that keep to these rules, and one draw needn't show every extreme that they name: `near_src`: the first three entries of row t are t, t - 32 and t + 32, clipped to the leaves; every entry lies within 32 of t. `distant_leaf_slot_index`: for a leaf on device e, entry s names a device e + s // 48 - 10 that exists.
All inputs are finite; a program needn't handle non-finite values.
Results may differ from a plain program's by a relative error of at most 0.025.
Values may be sent and summed in bfloat16 or wider, within the bound.
No kernel may reach another device: no remote copies, remote signals or barrier semaphores. Data moves between devices by JAX's collectives and lax.ppermute only.
A program may use at most 128 MiB of HBM per device.

v0:
```python
import jax
import jax.numpy as jnp
from jax import lax
from jax.sharding import PartitionSpec as P

HALO = 32


def passed_along(value, axis, steps):
    count = lax.axis_size(axis)
    leading, last = (max(0, -steps), min(count, count - steps))
    return lax.ppermute(value, axis, [(source, source + steps) for source in range(leading, last)])


def padded(block, sides, width):
    for axis, dim in sides:
        count = lax.axis_size(axis)
        forward = [(i, i + 1) for i in range(count - 1)]
        backward = [(target, source) for source, target in forward]
        low = lax.ppermute(
            lax.slice_in_dim(block, block.shape[dim] - width, None, axis=dim), axis, forward
        )
        high = lax.ppermute(lax.slice_in_dim(block, 0, width, axis=dim), axis, backward)
        block = jnp.concatenate([low, block, high], axis=dim)
    return block


def couple(expansion_weights, source_charges, interaction_kinds, coupling):
    terms = jnp.einsum(
        "lxbd,lxdp->lxbp",
        expansion_weights[source_charges],
        coupling[interaction_kinds],
        preferred_element_type=jnp.float32,
    )
    return jnp.sum(terms, axis=1)


def per_device(
    loads,
    col_basis,
    row_basis,
    near_blocks,
    near_src,
    up_leaf,
    down_leaf,
    up_node,
    down_node,
    up_group,
    down_group,
    up_top,
    downward_top_transfer,
    coupling,
    send_table,
    distant_leaf_slot_index,
    far_leaf_type,
    far_group_src,
    far_group_type,
    far_top_src,
    far_top_type,
):
    leaf_count, panels, rank = col_basis.shape
    vectors = loads.shape[0]
    nodes = leaf_count // 8
    leaf_size = lax.axis_size("leaf")
    sub_size = lax.axis_size("sub")
    group_index = lax.axis_index("leaf")
    position = group_index * sub_size + lax.axis_index("sub")
    leaf_first = jnp.transpose(loads.reshape(vectors, leaf_count, panels), (1, 0, 2))
    leaf_coeff = jnp.einsum(
        "lvp,lpr->lvr", leaf_first, col_basis, preferred_element_type=jnp.float32
    ).astype(jnp.bfloat16)
    flat_coeff = leaf_coeff.reshape(leaf_count, vectors * rank)
    width = send_table.shape[1]
    reach = (width - 1) // 2
    slot_count = send_table.shape[2]
    outgoing = flat_coeff[send_table[0].reshape(width * slot_count)].reshape(
        width, slot_count, vectors * rank
    )
    pieces = [None] * width
    pieces[reach] = outgoing[reach]
    for offset_pos in range(width):
        if offset_pos != reach:
            pieces[offset_pos] = passed_along(
                outgoing[offset_pos], ("leaf", "sub"), reach - offset_pos
            )
    received = jnp.concatenate(pieces, axis=0).reshape(width * slot_count, vectors, rank)
    rimmed = padded(leaf_first, ((("leaf", "sub"), 0),), HALO)
    local_ids = near_src - (position * leaf_count - HALO)
    gathered = rimmed[local_ids]
    nearby_contributions = jnp.einsum(
        "lkvq,lkpq->lkvp", gathered, near_blocks, preferred_element_type=jnp.float32
    )
    near_field = jnp.sum(nearby_contributions, axis=1)
    node_coeff = jnp.einsum(
        "ncvr,ncrs->nvs",
        leaf_coeff.reshape(nodes, 8, vectors, rank),
        up_leaf.reshape(nodes, 8, rank, rank),
        preferred_element_type=jnp.float32,
    ).astype(jnp.bfloat16)
    mid_coeff = jnp.einsum(
        "nvr,nrs->vs", node_coeff, up_node, preferred_element_type=jnp.float32
    ).astype(jnp.bfloat16)
    group_term = jnp.dot(mid_coeff, up_group[0], preferred_element_type=jnp.float32)
    group_own = lax.psum(group_term, "sub").astype(jnp.bfloat16)
    group_coeff = lax.all_gather(group_own[None], "leaf", axis=0, tiled=True)
    far_part = couple(received, distant_leaf_slot_index, far_leaf_type, coupling)
    tops = leaf_size // 4
    top_coeff = jnp.einsum(
        "gcvr,gcrs->gvs",
        group_coeff.reshape(tops, 4, vectors, rank),
        up_top.reshape(tops, 4, rank, rank),
        preferred_element_type=jnp.float32,
    ).astype(jnp.bfloat16)
    parent = group_index // 4
    top_local = couple(top_coeff, far_top_src[parent][None], far_top_type[parent][None], coupling)[
        0
    ].astype(jnp.bfloat16)
    group_local = (
        couple(group_coeff, far_group_src, far_group_type, coupling)[0]
        + jnp.dot(top_local, downward_top_transfer[group_index], preferred_element_type=jnp.float32)
    ).astype(jnp.bfloat16)
    mid_local = jnp.dot(group_local, down_group[0], preferred_element_type=jnp.float32).astype(
        jnp.bfloat16
    )
    node_local = jnp.einsum(
        "vr,nrs->nvs", mid_local, down_node, preferred_element_type=jnp.float32
    ).astype(jnp.bfloat16)
    inherited = jnp.einsum(
        "nvr,ncrs->ncvs",
        node_local,
        down_leaf.reshape(nodes, 8, rank, rank),
        preferred_element_type=jnp.float32,
    ).reshape(leaf_count, vectors, rank)
    leaf_local = (far_part + inherited).astype(jnp.bfloat16)
    far_field = jnp.einsum(
        "lvr,lpr->lvp", leaf_local, row_basis, preferred_element_type=jnp.float32
    )
    return jnp.transpose(far_field + near_field, (1, 0, 2)).reshape(vectors, leaf_count * panels)


def solution(mesh):
    return jax.shard_map(
        per_device,
        mesh=mesh,
        in_specs=(
            P(None, ("leaf", "sub")),
            P(("leaf", "sub"), None, None),
            P(("leaf", "sub"), None, None),
            P(("leaf", "sub"), None, None, None),
            P(("leaf", "sub"), None),
            P(("leaf", "sub"), None, None),
            P(("leaf", "sub"), None, None),
            P(("leaf", "sub"), None, None),
            P(("leaf", "sub"), None, None),
            P(("leaf", "sub"), None, None),
            P(("leaf", "sub"), None, None),
            P(),
            P(),
            P(),
            P(("leaf", "sub"), None, None),
            P(("leaf", "sub"), None),
            P(("leaf", "sub"), None),
            P("leaf", None),
            P("leaf", None),
            P(),
            P(),
        ),
        out_specs=P(None, ("leaf", "sub")),
        check_vma=False,
    )
```

profile of v0, /device:TPU:16, one launch (start us, length us, event | category | flops | bytes accessed | tf_op | source)
XLA Modules:
  0.0 217.6 jit_solution(13943304838873244237)
XLA Ops:
  0.0 2.0 convolution_convert_fusion
  2.3 0.7 compare_select_fusion.2
  3.1 0.7 reduce.4
  4.0 4.2 %gather_fusion = bf16[1008,1024]{1,0:T(8,128)(2,1)S(1)} fusion(bf16[64,1024]{1,0:T(8,128)(2,1)S(1)} %reshape.141, s32[1024]{0:T(1024)S(1)} %get-tuple-element.33), kind=kCustom, calls=%fused_computation | custom fusion | bytes 4132800 | tf_op jit(solution)/shard_map/gather | solution.py:76
  8.2 1.3 fusion.25
  9.5 3.8 %collective-permute-start.2 = (bf16[48,1024]{1,0:T(8,128)(2,1)}, bf16[48,1024]{1,0:T(8,128)(2,1)}, u32[]{:S(2)}, u32[]{:S(2)}) collective-permute-start(bf16[48,1024]{1,0:T(8,128)(2,1)} %get-tuple-element.23), channel_id=1, source_target_pairs={{0,8},{1,9},{2,10},{3,11},{4,12},{5,13},{6,14},{7,15},{8,16},{9,17... | collective-permute-start | bytes 294920 | tf_op jit(solution)/shard_map/ppermute | solution.py:12
  13.3 0.7 fusion.26
  14.0 6.3 %collective-permute-start = (bf16[48,1024]{1,0:T(8,128)(2,1)}, bf16[48,1024]{1,0:T(8,128)(2,1)}, u32[]{:S(2)}, u32[]{:S(2)}) collective-permute-start(bf16[48,1024]{1,0:T(8,128)(2,1)} %get-tuple-element.25), channel_id=1, source_target_pairs={{0,10},{1,11},{2,12},{3,13},{4,14},{5,15},{6,16},{7,17},{8,18},{9,... | collective-permute-start | bytes 294920 | tf_op jit(solution)/shard_map/ppermute | solution.py:12
  20.3 3.6 %collective-permute-start.1 = (bf16[48,1024]{1,0:T(8,128)(2,1)}, bf16[48,1024]{1,0:T(8,128)(2,1)}, u32[]{:S(2)}, u32[]{:S(2)}) collective-permute-start(bf16[48,1024]{1,0:T(8,128)(2,1)} %get-tuple-element.24), channel_id=1, source_target_pairs={{0,9},{1,10},{2,11},{3,12},{4,13},{5,14},{6,15},{7,16},{8,17},{9,1... | collective-permute-start | bytes 294920 | tf_op jit(solution)/shard_map/ppermute | solution.py:12
  23.9 4.3 %collective-permute-start.3 = (bf16[48,1024]{1,0:T(8,128)(2,1)}, bf16[48,1024]{1,0:T(8,128)(2,1)}, u32[]{:S(2)}, u32[]{:S(2)}) collective-permute-start(bf16[48,1024]{1,0:T(8,128)(2,1)} %get-tuple-element.22), channel_id=1, source_target_pairs={{0,7},{1,8},{2,9},{3,10},{4,11},{5,12},{6,13},{7,14},{8,15},{9,16}... | collective-permute-start | bytes 294920 | tf_op jit(solution)/shard_map/ppermute | solution.py:12
  28.2 1.9 collective-permute-start.4
  30.1 1.0 bitcast_bitcast_fusion
  31.5 0.7 fusion.22
  32.3 10.1 %copy.26 = bf16[316,64,64]{2,1,0:T(8,128)(2,1)} copy(bf16[316,64,64]{0,2,1:T(8,128)(2,1)} %param.34) | data formatting | bytes 5177344 | tf_op args[13]
  42.4 0.7 fusion.21
  43.8 10.8 %psum.7 = bf16[16,64]{1,0:T(8,128)(2,1)S(1)} all-reduce(f32[16,64]{1,0:T(8,128)S(1)} %fusion.17), channel_id=1, replica_groups=mesh['leaf'=32,'sub'=4] {'sub'}, use_global_device_ids=true, to_apply=%region_0.0 | all-reduce | flops 1024 | bytes 6144 | tf_op jit(solution)/shard_map/psum | solution.py:104
  54.6 22.8 %all-gather = bf16[512,64]{1,0:T(8,128)(2,1)S(1)} all-gather(bf16[16,64]{1,0:T(8,128)(2,1)S(1)} %psum.7), channel_id=2, replica_groups=mesh['leaf'=32,'sub'=4] {'leaf'}, dimensions={0}, use_global_device_ids=true | all-gather | bytes 67584 | tf_op jit(solution)/shard_map/all_gather | solution.py:105
  77.4 3.0 %gather_fusion.4 = bf16[8,64,64]{2,1,0:T(8,128)(2,1)S(1)} fusion(bf16[316,64,64]{2,1,0:T(8,128)(2,1)} %copy.26, s32[1024]{0:T(1024)S(1)} %pad_clamp_fusion.3), kind=kCustom, calls=%fused_computation.4 | custom fusion | bytes 131104 | tf_op jit(solution)/shard_map/gather | solution.py:32
  80.4 3.0 %gather_fusion.6 = bf16[8,64,64]{2,1,0:T(8,128)(2,1)S(1)} fusion(bf16[316,64,64]{2,1,0:T(8,128)(2,1)} %copy.26, s32[1024]{0:T(1024)S(1)} %pad_clamp_fusion.1), kind=kCustom, calls=%fused_computation.6 | custom fusion | bytes 131104 | tf_op jit(solution)/shard_map/gather | solution.py:32
  83.5 22.2 %gather_fusion.2 = bf16[512,64,64]{2,1,0:T(8,128)(2,1)} fusion(bf16[316,64,64]{2,1,0:T(8,128)(2,1)} %copy.26, s32[1024]{0:T(1024)S(1)} %get-tuple-element.32), kind=kCustom, calls=%fused_computation.2 | custom fusion | bytes 8390656 | tf_op jit(solution)/shard_map/gather | solution.py:32
  108.2 1.0 fusion.11
  109.4 1.2 fusion.14
  110.6 3.0 %collective-permute-start.5 = (bf16[48,1024]{1,0:T(8,128)(2,1)}, bf16[48,1024]{1,0:T(8,128)(2,1)S(1)}, u32[]{:S(2)}, u32[]{:S(2)}) collective-permute-start(bf16[48,1024]{1,0:T(8,128)(2,1)} %get-tuple-element.20), channel_id=1, source_target_pairs={{0,5},{1,6},{2,7},{3,8},{4,9},{5,10},{6,11},{7,12},{8,13},{9,14},{... | collective-permute-start | bytes 294920 | tf_op jit(solution)/shard_map/ppermute | solution.py:12
  113.6 1.1 concatenate.49
  114.7 0.7 constant_dynamic-update-slice_fusion.20
  115.4 1.9 collective-permute-start.6
  117.3 1.1 concatenate.50
  119.1 4.3 %collective-permute-start.7 = (bf16[48,1024]{1,0:T(8,128)(2,1)}, bf16[48,1024]{1,0:T(8,128)(2,1)S(1)}, u32[]{:S(2)}, u32[]{:S(2)}) collective-permute-start(bf16[48,1024]{1,0:T(8,128)(2,1)} %get-tuple-element.18), channel_id=1, source_target_pairs={{0,3},{1,4},{2,5},{3,6},{4,7},{5,8},{6,9},{7,10},{8,11},{9,12},{10... | collective-permute-start | bytes 294920 | tf_op jit(solution)/shard_map/ppermute | solution.py:12
  123.5 1.1 concatenate.51
  124.6 0.7 constant_dynamic-update-slice_fusion.18
  125.3 1.9 collective-permute-start.8
  127.2 1.1 concatenate.52
  128.3 0.7 constant_dynamic-update-slice_fusion.17
  129.0 2.8 %collective-permute-start.9 = (bf16[48,1024]{1,0:T(8,128)(2,1)}, bf16[48,1024]{1,0:T(8,128)(2,1)S(1)}, u32[]{:S(2)}, u32[]{:S(2)}) collective-permute-start(bf16[48,1024]{1,0:T(8,128)(2,1)} %get-tuple-element.16), channel_id=1, source_target_pairs={{0,1},{1,2},{2,3},{3,4},{4,5},{5,6},{6,7},{7,8},{8,9},{9,10},{10,1... | collective-permute-start | bytes 294920 | tf_op jit(solution)/shard_map/ppermute | solution.py:12
  131.8 1.1 concatenate.53
  132.9 0.7 constant_dynamic-update-slice_fusion.16
  133.6 7.0 %collective-permute-start.10 = (bf16[48,1024]{1,0:T(8,128)(2,1)}, bf16[48,1024]{1,0:T(8,128)(2,1)S(1)}, u32[]{:S(2)}, u32[]{:S(2)}) collective-permute-start(bf16[48,1024]{1,0:T(8,128)(2,1)} %get-tuple-element.14), channel_id=1, source_target_pairs={{1,0},{2,1},{3,2},{4,3},{5,4},{6,5},{7,6},{8,7},{9,8},{10,9},{11,1... | collective-permute-start | bytes 294920 | tf_op jit(solution)/shard_map/ppermute | solution.py:12
  141.4 3.6 %collective-permute-start.11 = (bf16[48,1024]{1,0:T(8,128)(2,1)S(1)}, bf16[48,1024]{1,0:T(8,128)(2,1)S(1)}, u32[]{:S(2)}, u32[]{:S(2)}) collective-permute-start(bf16[48,1024]{1,0:T(8,128)(2,1)S(1)} %copy-done.15), channel_id=1, source_target_pairs={{2,0},{3,1},{4,2},{5,3},{6,4},{7,5},{8,6},{9,7},{10,8},{11,9},{12,... | collective-permute-start | bytes 294920 | tf_op jit(solution)/shard_map/ppermute | solution.py:12
  146.0 1.9 collective-permute-start.12
  148.1 0.7 constant_dynamic-update-slice_fusion.13
  148.8 3.0 %collective-permute-start.13 = (bf16[48,1024]{1,0:T(8,128)(2,1)S(1)}, bf16[48,1024]{1,0:T(8,128)(2,1)S(1)}, u32[]{:S(2)}, u32[]{:S(2)}) collective-permute-start(bf16[48,1024]{1,0:T(8,128)(2,1)S(1)} %copy-done.13), channel_id=1, source_target_pairs={{4,0},{5,1},{6,2},{7,3},{8,4},{9,5},{10,6},{11,7},{12,8},{13,9},{1... | collective-permute-start | bytes 294920 | tf_op jit(solution)/shard_map/ppermute | solution.py:12
  151.9 0.7 constant_dynamic-update-slice_fusion.12
  152.6 5.6 %collective-permute-start.14 = (bf16[48,1024]{1,0:T(8,128)(2,1)S(1)}, bf16[48,1024]{1,0:T(8,128)(2,1)S(1)}, u32[]{:S(2)}, u32[]{:S(2)}) collective-permute-start(bf16[48,1024]{1,0:T(8,128)(2,1)S(1)} %copy-done.12), channel_id=1, source_target_pairs={{5,0},{6,1},{7,2},{8,3},{9,4},{10,5},{11,6},{12,7},{13,8},{14,9},{... | collective-permute-start | bytes 294920 | tf_op jit(solution)/shard_map/ppermute | solution.py:12
  158.4 0.7 constant_dynamic-update-slice_fusion.11
  159.1 0.7 constant_dynamic-update-slice_fusion.10
  159.8 1.9 collective-permute-start.15
  162.6 2.1 collective-permute-start.16
  165.7 3.6 %collective-permute-start.17 = (bf16[48,1024]{1,0:T(8,128)(2,1)S(1)}, bf16[48,1024]{1,0:T(8,128)(2,1)S(1)}, u32[]{:S(2)}, u32[]{:S(2)}) collective-permute-start(bf16[48,1024]{1,0:T(8,128)(2,1)S(1)} %copy-done.9), channel_id=1, source_target_pairs={{8,0},{9,1},{10,2},{11,3},{12,4},{13,5},{14,6},{15,7},{16,8},{17,9... | collective-permute-start | bytes 294920 | tf_op jit(solution)/shard_map/ppermute | solution.py:12
  170.1 5.9 %collective-permute-start.18 = (bf16[48,1024]{1,0:T(8,128)(2,1)S(1)}, bf16[48,1024]{1,0:T(8,128)(2,1)S(1)}, u32[]{:S(2)}, u32[]{:S(2)}) collective-permute-start(bf16[48,1024]{1,0:T(8,128)(2,1)S(1)} %copy-done.8), channel_id=1, source_target_pairs={{9,0},{10,1},{11,2},{12,3},{13,4},{14,5},{15,6},{16,7},{17,8},{18,... | collective-permute-start | bytes 294920 | tf_op jit(solution)/shard_map/ppermute | solution.py:12
  176.2 0.7 constant_dynamic-update-slice_fusion.6
  176.9 4.1 %collective-permute-start.19 = (bf16[48,1024]{1,0:T(8,128)(2,1)S(1)}, bf16[48,1024]{1,0:T(8,128)(2,1)S(1)}, u32[]{:S(2)}, u32[]{:S(2)}) collective-permute-start(bf16[48,1024]{1,0:T(8,128)(2,1)S(1)} %copy-done.7), channel_id=1, source_target_pairs={{10,0},{11,1},{12,2},{13,3},{14,4},{15,5},{16,6},{17,7},{18,8},{19... | collective-permute-start | bytes 294920 | tf_op jit(solution)/shard_map/ppermute | solution.py:12
  181.9 2.1 collective-permute-start.20
  184.2 0.7 constant_dynamic-update-slice_fusion.4
  184.9 7.9 %collective-permute-start.21 = (bf16[32,16,128]{2,1,0:T(8,128)(2,1)S(1)}, bf16[32,16,128]{2,1,0:T(8,128)(2,1)}, u32[]{:S(2)}, u32[]{:S(2)}) collective-permute-start(bf16[32,16,128]{2,1,0:T(8,128)(2,1)S(1)} %get-tuple-element.27), channel_id=1, source_target_pairs={{1,0},{2,1},{3,2},{4,3},{5,4},{6,5},{7,6},{8,7},{9,8},{10,9},{11,1... | collective-permute-start | bytes 393224 | tf_op jit(solution)/shard_map/ppermute | solution.py:23
  192.9 0.7 constant_dynamic-update-slice_fusion.3
  193.8 0.7 constant_dynamic-update-slice_fusion.2
  194.7 0.7 constant_dynamic-update-slice_fusion.1
  195.5 0.7 constant_dynamic-update-slice_fusion
  196.2 3.4 %gather_fusion.1 = bf16[512,16,64]{2,1,0:T(8,128)(2,1)S(1)} fusion(bf16[1008,16,64]{2,1,0:T(8,128)(2,1)} %constant_dynamic-update-slice_fusion, s32[1024]{0:T(1024)S(1)} %pad_clamp_fusion.6), kind=kCustom, calls=%fused_computation.1 | custom fusion | bytes 2099200 | tf_op jit(solution)/shard_map/gather | solution.py:31
  199.6 6.2 %fusion.4 = f32[64,16,128]{2,1,0:T(8,128)} fusion(bf16[64,128,64]{1,2,0:T(8,128)(2,1)} %param.23, f32[64,16,64]{2,1,0:T(8,128)} %bitcast.127, bf16[64,8,16,64]{3,2,1,0:T(8,128)(2,1)S(1)} %bitcast.124, bf16[64,8,64,64]{3,2,1,0:T(8,128)(2,1)} %bitcast.123), kind=kOutput, calls=%fused_computation.15 | convolution fusion | flops 84017152 | bytes 7077888 | tf_op jit(solution)/shard_map/lvr,lpr->lvp/dot_general | solution.py:135
  205.8 1.0 pad_maximum_fusion
  206.9 1.9 gather_fusion.7
  208.8 8.0 %fusion.1 = f32[64,2,8,128]{3,2,1,0:T(8,128)S(1)} fusion(f32[64,16,128]{2,1,0:T(8,128)} %fusion.4, bf16[64,6,16,128]{3,2,1,0:T(8,128)(2,1)S(1)} %bitcast.125, bf16[64,6,128,128]{3,2,1,0:T(8,128)(2,1)} %param.24), kind=kOutput, calls=%fused_computation.10 | convolution fusion | flops 201457664 | bytes 15204352 | tf_op jit(solution)/shard_map/lkvq,lkpq->lkvp/dot_general | solution.py:90
  216.8 0.8 copy.41
  (115 shorter events, 11.6 us)
Async XLA Ops:
  0.0 109.4 %copy-start = (bf16[64,64,64]{2,1,0:T(8,128)(2,1)S(1)}, bf16[64,64,64]{2,1,0:T(8,128)(2,1)}, u32[]{:S(2)}) copy-start(bf16[64,64,64]{2,1,0:T(8,128)(2,1)} %param.27) | copy-start | bytes 1572868
  2.0 2.0 copy-start.1
  8.2 23.1 %copy-start.18 = (s32[64,8]{0,1:T(8,128)S(1)}, s32[64,8]{0,1:T(8,128)}, u32[]{:S(2)}) copy-start(s32[64,8]{0,1:T(8,128)} %param.36) | copy-start | bytes 6148
  8.2 23.3 %copy-start.20 = (s32[1,8]{1,0:T(1,128)S(1)}, s32[1,8]{1,0:T(1,128)}, u32[]{:S(2)}) copy-start(s32[1,8]{1,0:T(1,128)} %param.39) | copy-start | bytes 100
  9.5 109.6 %collective-permute-start.2 = (bf16[48,1024]{1,0:T(8,128)(2,1)}, bf16[48,1024]{1,0:T(8,128)(2,1)}, u32[]{:S(2)}, u32[]{:S(2)}) collective-permute-start(bf16[48,1024]{1,0:T(8,128)(2,1)} %get-tuple-element.23), channel_id=1, source_target_pairs={{0,8},{1,9},{2,10},{3,11},{4,12},{5,13},{6,14},{7,15},{8,16},{9,17... | collective-permute-start | bytes 294920 | tf_op jit(solution)/shard_map/ppermute | solution.py:12
  14.0 96.6 %collective-permute-start = (bf16[48,1024]{1,0:T(8,128)(2,1)}, bf16[48,1024]{1,0:T(8,128)(2,1)}, u32[]{:S(2)}, u32[]{:S(2)}) collective-permute-start(bf16[48,1024]{1,0:T(8,128)(2,1)} %get-tuple-element.25), channel_id=1, source_target_pairs={{0,10},{1,11},{2,12},{3,13},{4,14},{5,15},{6,16},{7,17},{8,18},{9,... | collective-permute-start | bytes 294920 | tf_op jit(solution)/shard_map/ppermute | solution.py:12
  20.3 95.1 %collective-permute-start.1 = (bf16[48,1024]{1,0:T(8,128)(2,1)}, bf16[48,1024]{1,0:T(8,128)(2,1)}, u32[]{:S(2)}, u32[]{:S(2)}) collective-permute-start(bf16[48,1024]{1,0:T(8,128)(2,1)} %get-tuple-element.24), channel_id=1, source_target_pairs={{0,9},{1,10},{2,11},{3,12},{4,13},{5,14},{6,15},{7,16},{8,17},{9,1... | collective-permute-start | bytes 294920 | tf_op jit(solution)/shard_map/ppermute | solution.py:12
  23.9 101.4 %collective-permute-start.3 = (bf16[48,1024]{1,0:T(8,128)(2,1)}, bf16[48,1024]{1,0:T(8,128)(2,1)}, u32[]{:S(2)}, u32[]{:S(2)}) collective-permute-start(bf16[48,1024]{1,0:T(8,128)(2,1)} %get-tuple-element.22), channel_id=1, source_target_pairs={{0,7},{1,8},{2,9},{3,10},{4,11},{5,12},{6,13},{7,14},{8,15},{9,16}... | collective-permute-start | bytes 294920 | tf_op jit(solution)/shard_map/ppermute | solution.py:12
  28.2 100.8 %collective-permute-start.4 = (bf16[48,1024]{1,0:T(8,128)(2,1)}, bf16[48,1024]{1,0:T(8,128)(2,1)}, u32[]{:S(2)}, u32[]{:S(2)}) collective-permute-start(bf16[48,1024]{1,0:T(8,128)(2,1)} %get-tuple-element.21), channel_id=1, source_target_pairs={{0,6},{1,7},{2,8},{3,9},{4,10},{5,11},{6,12},{7,13},{8,14},{9,15},... | collective-permute-start | bytes 294920 | tf_op jit(solution)/shard_map/ppermute | solution.py:12
  32.3 10.2 %copy-start.21 = (s32[1,8]{1,0:T(1,128)S(1)}, s32[1,8]{1,0:T(1,128)}, u32[]{:S(2)}) copy-start(s32[1,8]{1,0:T(1,128)} %param.38) | copy-start | bytes 100
  32.3 10.9 %copy-start.2 = (bf16[64,16,64]{2,1,0:T(8,128)(2,1)S(1)}, bf16[64,16,64]{2,1,0:T(8,128)(2,1)}, u32[]{:S(2)}) copy-start(bf16[64,16,64]{2,1,0:T(8,128)(2,1)} %copy-done.1) | copy-start | bytes 393220
  32.3 10.9 %copy-start.3 = (bf16[64,64,64]{2,1,0:T(8,128)(2,1)S(1)}, bf16[64,64,64]{2,1,0:T(8,128)(2,1)}, u32[]{:S(2)}) copy-start(bf16[64,64,64]{2,1,0:T(8,128)(2,1)} %param.26) | copy-start | bytes 1572868
  32.3 10.9 %copy-start.5 = (bf16[8,64,64]{2,1,0:T(8,128)(2,1)S(1)}, bf16[8,64,64]{2,1,0:T(8,128)(2,1)}, u32[]{:S(2)}) copy-start(bf16[8,64,64]{2,1,0:T(8,128)(2,1)} %param.28) | copy-start | bytes 196612
  32.3 11.4 %copy-start.16 = (bf16[1,64,64]{2,1,0:T(8,128)(2,1)S(1)}, bf16[1,64,64]{2,1,0:T(8,128)(2,1)}, u32[]{:S(2)}) copy-start(bf16[1,64,64]{2,1,0:T(8,128)(2,1)} %param.30) | copy-start | bytes 24580
  83.5 22.3 %copy-start.19 = (s32[64,6]{0,1:T(8,128)S(1)}, s32[64,6]{0,1:T(8,128)}, u32[]{:S(2)}) copy-start(s32[64,6]{0,1:T(8,128)} %param.25) | copy-start | bytes 4612
  83.5 23.9 %copy-start.4 = (bf16[32,64,64]{2,1,0:T(8,128)(2,1)S(1)}, bf16[32,64,64]{2,1,0:T(8,128)(2,1)}, u32[]{:S(2)}) copy-start(bf16[32,64,64]{2,1,0:T(8,128)(2,1)} %param.32) | copy-start | bytes 786436
  83.5 25.8 %copy-start.17 = (bf16[1,64,64]{2,1,0:T(8,128)(2,1)S(1)}, bf16[1,64,64]{2,1,0:T(8,128)(2,1)}, u32[]{:S(2)}) copy-start(bf16[1,64,64]{2,1,0:T(8,128)(2,1)} %param.31) | copy-start | bytes 24580
  83.5 25.9 %copy-start.6 = (bf16[8,64,64]{2,1,0:T(8,128)(2,1)S(1)}, bf16[8,64,64]{2,1,0:T(8,128)(2,1)}, u32[]{:S(2)}) copy-start(bf16[8,64,64]{2,1,0:T(8,128)(2,1)} %param.29) | copy-start | bytes 196612
  105.7 35.7 %copy-start.15 = (bf16[48,1024]{1,0:T(8,128)(2,1)S(1)}, bf16[48,1024]{1,0:T(8,128)(2,1)}, u32[]{:S(2)}) copy-start(bf16[48,1024]{1,0:T(8,128)(2,1)} %get-tuple-element.13) | copy-start | bytes 294916
  106.0 40.0 %copy-start.14 = (bf16[48,1024]{1,0:T(8,128)(2,1)S(1)}, bf16[48,1024]{1,0:T(8,128)(2,1)}, u32[]{:S(2)}) copy-start(bf16[48,1024]{1,0:T(8,128)(2,1)} %get-tuple-element.12) | copy-start | bytes 294916
  107.4 41.4 %copy-start.13 = (bf16[48,1024]{1,0:T(8,128)(2,1)S(1)}, bf16[48,1024]{1,0:T(8,128)(2,1)}, u32[]{:S(2)}) copy-start(bf16[48,1024]{1,0:T(8,128)(2,1)} %get-tuple-element.11) | copy-start | bytes 294916
  107.7 45.0 %copy-start.12 = (bf16[48,1024]{1,0:T(8,128)(2,1)S(1)}, bf16[48,1024]{1,0:T(8,128)(2,1)}, u32[]{:S(2)}) copy-start(bf16[48,1024]{1,0:T(8,128)(2,1)} %get-tuple-element.10) | copy-start | bytes 294916
  109.4 50.5 %copy-start.11 = (bf16[48,1024]{1,0:T(8,128)(2,1)S(1)}, bf16[48,1024]{1,0:T(8,128)(2,1)}, u32[]{:S(2)}) copy-start(bf16[48,1024]{1,0:T(8,128)(2,1)} %get-tuple-element.9) | copy-start | bytes 294916
  110.6 52.1 %copy-start.10 = (bf16[48,1024]{1,0:T(8,128)(2,1)S(1)}, bf16[48,1024]{1,0:T(8,128)(2,1)}, u32[]{:S(2)}) copy-start(bf16[48,1024]{1,0:T(8,128)(2,1)} %get-tuple-element.8) | copy-start | bytes 294916
  110.6 23.0 %collective-permute-start.5 = (bf16[48,1024]{1,0:T(8,128)(2,1)}, bf16[48,1024]{1,0:T(8,128)(2,1)S(1)}, u32[]{:S(2)}, u32[]{:S(2)}) collective-permute-start(bf16[48,1024]{1,0:T(8,128)(2,1)} %get-tuple-element.20), channel_id=1, source_target_pairs={{0,5},{1,6},{2,7},{3,8},{4,9},{5,10},{6,11},{7,12},{8,13},{9,14},{... | collective-permute-start | bytes 294920 | tf_op jit(solution)/shard_map/ppermute | solution.py:12
  114.7 51.0 %copy-start.9 = (bf16[48,1024]{1,0:T(8,128)(2,1)S(1)}, bf16[48,1024]{1,0:T(8,128)(2,1)}, u32[]{:S(2)}) copy-start(bf16[48,1024]{1,0:T(8,128)(2,1)} %get-tuple-element.7) | copy-start | bytes 294916
  115.4 26.0 %collective-permute-start.6 = (bf16[48,1024]{1,0:T(8,128)(2,1)}, bf16[48,1024]{1,0:T(8,128)(2,1)S(1)}, u32[]{:S(2)}, u32[]{:S(2)}) collective-permute-start(bf16[48,1024]{1,0:T(8,128)(2,1)} %get-tuple-element.19), channel_id=1, source_target_pairs={{0,4},{1,5},{2,6},{3,7},{4,8},{5,9},{6,10},{7,11},{8,12},{9,13},{1... | collective-permute-start | bytes 294920 | tf_op jit(solution)/shard_map/ppermute | solution.py:12
  118.4 51.7 %copy-start.8 = (bf16[48,1024]{1,0:T(8,128)(2,1)S(1)}, bf16[48,1024]{1,0:T(8,128)(2,1)}, u32[]{:S(2)}) copy-start(bf16[48,1024]{1,0:T(8,128)(2,1)} %get-tuple-element.6) | copy-start | bytes 294916
  119.1 26.8 %collective-permute-start.7 = (bf16[48,1024]{1,0:T(8,128)(2,1)}, bf16[48,1024]{1,0:T(8,128)(2,1)S(1)}, u32[]{:S(2)}, u32[]{:S(2)}) collective-permute-start(bf16[48,1024]{1,0:T(8,128)(2,1)} %get-tuple-element.18), channel_id=1, source_target_pairs={{0,3},{1,4},{2,5},{3,6},{4,7},{5,8},{6,9},{7,10},{8,11},{9,12},{10... | collective-permute-start | bytes 294920 | tf_op jit(solution)/shard_map/ppermute | solution.py:12
  124.6 52.3 %copy-start.7 = (bf16[48,1024]{1,0:T(8,128)(2,1)S(1)}, bf16[48,1024]{1,0:T(8,128)(2,1)}, u32[]{:S(2)}) copy-start(bf16[48,1024]{1,0:T(8,128)(2,1)} %get-tuple-element.5) | copy-start | bytes 294916
  125.3 23.5 %collective-permute-start.8 = (bf16[48,1024]{1,0:T(8,128)(2,1)}, bf16[48,1024]{1,0:T(8,128)(2,1)S(1)}, u32[]{:S(2)}, u32[]{:S(2)}) collective-permute-start(bf16[48,1024]{1,0:T(8,128)(2,1)} %get-tuple-element.17), channel_id=1, source_target_pairs={{0,2},{1,3},{2,4},{3,5},{4,6},{5,7},{6,8},{7,9},{8,10},{9,11},{10,... | collective-permute-start | bytes 294920 | tf_op jit(solution)/shard_map/ppermute | solution.py:12
  129.0 23.6 %collective-permute-start.9 = (bf16[48,1024]{1,0:T(8,128)(2,1)}, bf16[48,1024]{1,0:T(8,128)(2,1)S(1)}, u32[]{:S(2)}, u32[]{:S(2)}) collective-permute-start(bf16[48,1024]{1,0:T(8,128)(2,1)} %get-tuple-element.16), channel_id=1, source_target_pairs={{0,1},{1,2},{2,3},{3,4},{4,5},{5,6},{6,7},{7,8},{8,9},{9,10},{10,1... | collective-permute-start | bytes 294920 | tf_op jit(solution)/shard_map/ppermute | solution.py:12
  133.6 26.3 %collective-permute-start.10 = (bf16[48,1024]{1,0:T(8,128)(2,1)}, bf16[48,1024]{1,0:T(8,128)(2,1)S(1)}, u32[]{:S(2)}, u32[]{:S(2)}) collective-permute-start(bf16[48,1024]{1,0:T(8,128)(2,1)} %get-tuple-element.14), channel_id=1, source_target_pairs={{1,0},{2,1},{3,2},{4,3},{5,4},{6,5},{7,6},{8,7},{9,8},{10,9},{11,1... | collective-permute-start | bytes 294920 | tf_op jit(solution)/shard_map/ppermute | solution.py:12
  141.4 21.2 %collective-permute-start.11 = (bf16[48,1024]{1,0:T(8,128)(2,1)S(1)}, bf16[48,1024]{1,0:T(8,128)(2,1)S(1)}, u32[]{:S(2)}, u32[]{:S(2)}) collective-permute-start(bf16[48,1024]{1,0:T(8,128)(2,1)S(1)} %copy-done.15), channel_id=1, source_target_pairs={{2,0},{3,1},{4,2},{5,3},{6,4},{7,5},{8,6},{9,7},{10,8},{11,9},{12,... | collective-permute-start | bytes 294920 | tf_op jit(solution)/shard_map/ppermute | solution.py:12
  146.0 19.7 %collective-permute-start.12 = (bf16[48,1024]{1,0:T(8,128)(2,1)S(1)}, bf16[48,1024]{1,0:T(8,128)(2,1)S(1)}, u32[]{:S(2)}, u32[]{:S(2)}) collective-permute-start(bf16[48,1024]{1,0:T(8,128)(2,1)S(1)} %copy-done.14), channel_id=1, source_target_pairs={{3,0},{4,1},{5,2},{6,3},{7,4},{8,5},{9,6},{10,7},{11,8},{12,9},{13... | collective-permute-start | bytes 294920 | tf_op jit(solution)/shard_map/ppermute | solution.py:12
  148.8 21.3 %collective-permute-start.13 = (bf16[48,1024]{1,0:T(8,128)(2,1)S(1)}, bf16[48,1024]{1,0:T(8,128)(2,1)S(1)}, u32[]{:S(2)}, u32[]{:S(2)}) collective-permute-start(bf16[48,1024]{1,0:T(8,128)(2,1)S(1)} %copy-done.13), channel_id=1, source_target_pairs={{4,0},{5,1},{6,2},{7,3},{8,4},{9,5},{10,6},{11,7},{12,8},{13,9},{1... | collective-permute-start | bytes 294920 | tf_op jit(solution)/shard_map/ppermute | solution.py:12
  152.6 24.3 %collective-permute-start.14 = (bf16[48,1024]{1,0:T(8,128)(2,1)S(1)}, bf16[48,1024]{1,0:T(8,128)(2,1)S(1)}, u32[]{:S(2)}, u32[]{:S(2)}) collective-permute-start(bf16[48,1024]{1,0:T(8,128)(2,1)S(1)} %copy-done.12), channel_id=1, source_target_pairs={{5,0},{6,1},{7,2},{8,3},{9,4},{10,5},{11,6},{12,7},{13,8},{14,9},{... | collective-permute-start | bytes 294920 | tf_op jit(solution)/shard_map/ppermute | solution.py:12
  159.8 22.0 %collective-permute-start.15 = (bf16[48,1024]{1,0:T(8,128)(2,1)S(1)}, bf16[48,1024]{1,0:T(8,128)(2,1)S(1)}, u32[]{:S(2)}, u32[]{:S(2)}) collective-permute-start(bf16[48,1024]{1,0:T(8,128)(2,1)S(1)} %copy-done.11), channel_id=1, source_target_pairs={{6,0},{7,1},{8,2},{9,3},{10,4},{11,5},{12,6},{13,7},{14,8},{15,9},... | collective-permute-start | bytes 294920 | tf_op jit(solution)/shard_map/ppermute | solution.py:12
  162.6 22.2 %collective-permute-start.16 = (bf16[48,1024]{1,0:T(8,128)(2,1)S(1)}, bf16[48,1024]{1,0:T(8,128)(2,1)S(1)}, u32[]{:S(2)}, u32[]{:S(2)}) collective-permute-start(bf16[48,1024]{1,0:T(8,128)(2,1)S(1)} %copy-done.10), channel_id=1, source_target_pairs={{7,0},{8,1},{9,2},{10,3},{11,4},{12,5},{13,6},{14,7},{15,8},{16,9}... | collective-permute-start | bytes 294920 | tf_op jit(solution)/shard_map/ppermute | solution.py:12
  165.7 28.0 %collective-permute-start.17 = (bf16[48,1024]{1,0:T(8,128)(2,1)S(1)}, bf16[48,1024]{1,0:T(8,128)(2,1)S(1)}, u32[]{:S(2)}, u32[]{:S(2)}) collective-permute-start(bf16[48,1024]{1,0:T(8,128)(2,1)S(1)} %copy-done.9), channel_id=1, source_target_pairs={{8,0},{9,1},{10,2},{11,3},{12,4},{13,5},{14,6},{15,7},{16,8},{17,9... | collective-permute-start | bytes 294920 | tf_op jit(solution)/shard_map/ppermute | solution.py:12
  170.1 24.4 %collective-permute-start.18 = (bf16[48,1024]{1,0:T(8,128)(2,1)S(1)}, bf16[48,1024]{1,0:T(8,128)(2,1)S(1)}, u32[]{:S(2)}, u32[]{:S(2)}) collective-permute-start(bf16[48,1024]{1,0:T(8,128)(2,1)S(1)} %copy-done.8), channel_id=1, source_target_pairs={{9,0},{10,1},{11,2},{12,3},{13,4},{14,5},{15,6},{16,7},{17,8},{18,... | collective-permute-start | bytes 294920 | tf_op jit(solution)/shard_map/ppermute | solution.py:12
  176.9 18.5 %collective-permute-start.19 = (bf16[48,1024]{1,0:T(8,128)(2,1)S(1)}, bf16[48,1024]{1,0:T(8,128)(2,1)S(1)}, u32[]{:S(2)}, u32[]{:S(2)}) collective-permute-start(bf16[48,1024]{1,0:T(8,128)(2,1)S(1)} %copy-done.7), channel_id=1, source_target_pairs={{10,0},{11,1},{12,2},{13,3},{14,4},{15,5},{16,6},{17,7},{18,8},{19... | collective-permute-start | bytes 294920 | tf_op jit(solution)/shard_map/ppermute | solution.py:12
  181.9 24.0 %collective-permute-start.20 = (bf16[32,16,128]{2,1,0:T(8,128)(2,1)}, bf16[32,16,128]{2,1,0:T(8,128)(2,1)}, u32[]{:S(2)}, u32[]{:S(2)}) collective-permute-start(bf16[32,16,128]{2,1,0:T(8,128)(2,1)} %get-tuple-element.26), channel_id=1, source_target_pairs={{0,1},{1,2},{2,3},{3,4},{4,5},{5,6},{6,7},{7,8},{8,9},{9,10},{10,1... | collective-permute-start | bytes 393224 | tf_op jit(solution)/shard_map/ppermute | solution.py:20
  184.9 20.9 %collective-permute-start.21 = (bf16[32,16,128]{2,1,0:T(8,128)(2,1)S(1)}, bf16[32,16,128]{2,1,0:T(8,128)(2,1)}, u32[]{:S(2)}, u32[]{:S(2)}) collective-permute-start(bf16[32,16,128]{2,1,0:T(8,128)(2,1)S(1)} %get-tuple-element.27), channel_id=1, source_target_pairs={{1,0},{2,1},{3,2},{4,3},{5,4},{6,5},{7,6},{8,7},{9,8},{10,9},{11,1... | collective-permute-start | bytes 393224 | tf_op jit(solution)/shard_map/ppermute | solution.py:23
where the time goes:
time: 219 us; the launch traced here: 218 us
  starting transfers between devices  82.6 us (38%)
  local copies, waits for them, and re-layouts  77.2 us (35%)
  blocking collectives  33.5 us (15%)
  matrix products  19.6 us (9%)
  other arithmetic  3.91 us (2%)
    ppermute x20, starting transfers between devices, passed_along(): lax.ppermute(value, axis, [(source, source + steps) for source in range(l...  72.6 us
    gather x3, local copies, waits for them, and re-layouts, couple(): coupling[interaction_kinds]  28.3 us
    unnamed x65, local copies, waits for them, and re-layouts  24.1 us
    all_gather x1, blocking collectives, per_device(): group_coeff = lax.all_gather(group_own[None], 'leaf', axis=0, tiled=True)  22.8 us
    psum x1, blocking collectives, per_device(): group_own = lax.psum(group_term, 'sub').astype(jnp.bfloat16)  10.8 us
    concatenate x22, local copies, waits for them, and re-layouts, per_device(): jnp.concatenate(pieces, axis=0).reshape(width * slot_count, vectors, rank)  8.91 us
    dot_general x1, matrix products, per_device(): jnp.einsum('lkvq,lkpq->lkvp', gathered, near_blocks, preferred_element_ty...  7.99 us
    ppermute x1, starting transfers between devices, padded(): lax.ppermute(lax.slice_in_dim(block, 0, width, axis=dim), axis, backward)  7.85 us
  transfers between devices with their start and end apart: 22, of which 0 were waited for; matrix products, arithmetic and copies ran while one was open for 36% of the time, Pallas kernels for 0%

commit v1 on v0

v1 whole, which is shorter than its diff:
```python
import functools

import jax
import jax.numpy as jnp
from jax import lax
from jax.experimental import pallas as pl
from jax.experimental.pallas import tpu as pltpu
from jax.sharding import PartitionSpec as P

AXES = ("leaf", "sub")
DEVICES = 128
RANK = 64
PANEL = 128
LEAVES = 64
FAR = 8
NEAR = 6
HALO = 32
OFFSETS = 21
SLOTS = 48
TYPES = 316
TYPE_ROWS = 320
TERM_ROW = 512
TABLE_ROW = 528
BLOCK = 560
KP_ROWS = 576
NT = (((1,), (1,)), ((), ()))


def dot(a, b):
    return jnp.dot(a, b, preferred_element_type=jnp.float32)


def dot_nt(a, b):
    return lax.dot_general(a, b, NT, preferred_element_type=jnp.float32)


def lane_index(rows):
    return lax.broadcasted_iota(jnp.int32, (rows, 128), 1)


def moved(value, pairs):
    return lax.ppermute(value, AXES, pairs)


def line_shift(steps):
    return [(s, s + steps) for s in range(max(0, -steps), min(DEVICES, DEVICES - steps))]


def x_shift(d):
    return [(p, (p & ~3) | ((p + d) & 3)) for p in range(DEVICES)]


def z_shift(d):
    return [(p, (p & ~24) | ((p + 8 * d) & 24)) for p in range(DEVICES)]


def y_shift(d):
    return [(p, (p + 32 * d) % DEVICES) for p in range(DEVICES)]


CORE_SWAP = [(p, p ^ 4) for p in range(DEVICES)]


def two_blocks_away(near_edge, steps):
    pairs = []
    for e in range(DEVICES):
        i = e % 8
        if i < near_edge and e >= steps:
            pairs.append((e - steps, e))
        if i >= 8 - near_edge and e + steps < DEVICES:
            pairs.append((e + steps, e))
    return pairs


def up_kernel(x_ref, cb_ref, ul_ref, un_ref, ug_ref, table_ref, out_ref, mid_ref):
    step = pl.program_id(0)
    nodes = ul_ref.shape[0]
    left = lane_index(16) < RANK

    @pl.when(step == 0)
    def _():
        mid_ref[...] = jnp.zeros_like(mid_ref)

    mid = mid_ref[...]
    for n in range(nodes):
        blocks = []
        for q in range(4):
            i = n * 4 + q
            lhs = jnp.concatenate(
                [x_ref[:, 2 * i * PANEL : (2 * i + 1) * PANEL], x_ref[:, (2 * i + 1) * PANEL : (2 * i + 2) * PANEL]],
                axis=0,
            )
            both = dot_nt(lhs, cb_ref[i])
            block = jnp.where(left, both[:16], both[16:]).astype(jnp.bfloat16)
            row = pl.multiple_of(step * (nodes * 64) + i * 16, 16)
            out_ref[pl.ds(row, 16), :] = block
            blocks.append(block)
        node = dot(jnp.concatenate(blocks, axis=1), ul_ref[n]).astype(jnp.bfloat16)
        mid = mid + dot(node, un_ref[n])
    mid_ref[...] = mid

    @pl.when(step == pl.num_programs(0) - 1)
    def _():
        term = dot(mid.astype(jnp.bfloat16), ug_ref[...])
        high = term.astype(jnp.bfloat16).astype(jnp.float32)
        parts = jnp.concatenate([high, term - high], axis=1)
        out_ref[TERM_ROW : TERM_ROW + 16, :] = parts.astype(jnp.bfloat16)
        out_ref[TABLE_ROW:BLOCK, :] = table_ref[...].astype(jnp.bfloat16)


def up_sweep(loads, col_basis, up_leaf, up_node, up_group, table):
    steps = 4
    return pl.pallas_call(
        up_kernel,
        grid=(steps,),
        in_specs=[
            pl.BlockSpec((16, 8192 // steps), lambda i: (0, i)),
            pl.BlockSpec((32 // steps, 128, 128), lambda i: (i, 0, 0)),
            pl.BlockSpec((8 // steps, 512, RANK), lambda i: (i, 0, 0)),
            pl.BlockSpec((8 // steps, RANK, RANK), lambda i: (i, 0, 0)),
            pl.BlockSpec((RANK, RANK), lambda i: (0, 0)),
            pl.BlockSpec((32, 128), lambda i: (0, 0)),
        ],
        out_specs=pl.BlockSpec((BLOCK, 128), lambda i: (0, 0)),
        out_shape=jax.ShapeDtypeStruct((BLOCK, 128), jnp.bfloat16),
        scratch_shapes=[pltpu.VMEM((16, RANK), jnp.float32)],
        compiler_params=pltpu.CompilerParams(vmem_limit_bytes=32 << 20),
        cost_estimate=pl.CostEstimate(flops=40_000_000, bytes_accessed=2_600_000, transcendentals=0),
        name="up_sweep",
    )(loads, col_basis, up_leaf, up_node, up_group, table)


def pick_kernel(place, leaf_type, group_type, top_type, k2_ref, down_ref, out_ref, table):
    step = pl.program_id(0)
    per_step = k2_ref.shape[0] // RANK
    eye = (
        lax.broadcasted_iota(jnp.int32, (TYPE_ROWS, TYPES), 0)
        == lax.broadcasted_iota(jnp.int32, (TYPE_ROWS, TYPES), 1)
    ).astype(jnp.bfloat16)
    for r in range(0, per_step, 2):
        one = k2_ref[r * RANK : (r + 1) * RANK, :]
        two = k2_ref[(r + 1) * RANK : (r + 2) * RANK, :]
        turned = dot_nt(eye, jnp.concatenate([one, one, two, two], axis=0))
        row = pl.multiple_of((step * per_step + r) * TYPE_ROWS, 8)
        table[pl.ds(row, TYPE_ROWS), :] = turned[:, :128]
        table[pl.ds(row + TYPE_ROWS, TYPE_ROWS), :] = turned[:, 128:]

    @pl.when(step == pl.num_programs(0) - 1)
    def _():
        left = lane_index(RANK) < RANK

        def pair(i, first, second):
            one = table[pl.ds(first, RANK, stride=TYPE_ROWS), :]
            two = table[pl.ds(second, RANK, stride=TYPE_ROWS), :]
            return jnp.where(left, one, two).astype(jnp.bfloat16)

        @pl.loop(0, LEAVES // 2)
        def _(i):
            base = pl.multiple_of(i * KP_ROWS, 64)
            for k in range(FAR):
                out_ref[pl.ds(base + k * RANK, RANK), :] = pair(i, leaf_type[k, 2 * i], leaf_type[k, 2 * i + 1])
            out_ref[pl.ds(base + FAR * RANK, RANK), :] = jnp.concatenate(
                [down_ref[2 * i], down_ref[2 * i + 1]], axis=1
            )

        base = LEAVES // 2 * KP_ROWS
        parent = place[5]
        for k in range(FAR):
            out_ref[base + k * RANK : base + (k + 1) * RANK, :] = pair(0, group_type[0, k], top_type[parent, k])
        out_ref[base + FAR * RANK : base + KP_ROWS, :] = jnp.zeros((RANK, 128), jnp.bfloat16)


def picked_couplings(place, leaf_type, group_type, top_type, coupling, down_leaf):
    steps = 8
    rows = (LEAVES // 2 + 1) * KP_ROWS
    smem = pl.BlockSpec(memory_space=pltpu.SMEM)
    return pl.pallas_call(
        pick_kernel,
        grid=(steps,),
        in_specs=[
            smem,
            smem,
            smem,
            smem,
            pl.BlockSpec((RANK * RANK // steps, TYPES), lambda i: (i, 0)),
            pl.BlockSpec((LEAVES, RANK, RANK), lambda i: (0, 0, 0)),
        ],
        out_specs=pl.BlockSpec((rows, 128), lambda i: (0, 0)),
        out_shape=jax.ShapeDtypeStruct((rows, 128), jnp.bfloat16),
        scratch_shapes=[pltpu.VMEM((RANK * TYPE_ROWS, 128), jnp.float32)],
        compiler_params=pltpu.CompilerParams(vmem_limit_bytes=48 << 20),
        cost_estimate=pl.CostEstimate(flops=3_200_000_000, bytes_accessed=9_000_000, transcendentals=0),
        name="pick_couplings",
    )(place, leaf_type, group_type, top_type, coupling, down_leaf)


def near_kernel(first, per_step, place, src, low_ref, own_ref, high_ref, blocks_ref, out_ref, all_x):
    step = pl.program_id(0)

    @pl.when(step == 0)
    def _():
        all_x[:, : HALO * PANEL] = low_ref[...]
        all_x[:, HALO * PANEL : (HALO + LEAVES) * PANEL] = own_ref[...]
        all_x[:, (HALO + LEAVES) * PANEL :] = high_ref[...]

    start = place[0] * LEAVES - HALO
    for t in range(per_step):
        total = jnp.zeros((16, PANEL), jnp.float32)
        for k in range(NEAR):
            i = src[k, first + step * per_step + t] - start
            x = all_x[:, pl.ds(pl.multiple_of(i * PANEL, PANEL), PANEL)]
            total = total + dot_nt(x, blocks_ref[t, k])
        out_ref[:, t * PANEL : (t + 1) * PANEL] = total


def near_field(place, src, low, own, high, blocks, first, count):
    per_step = 8
    smem = pl.BlockSpec(memory_space=pltpu.SMEM)
    begin = first // per_step
    return pl.pallas_call(
        functools.partial(near_kernel, first, per_step),
        grid=(count // per_step,),
        in_specs=[
            smem,
            smem,
            pl.BlockSpec(low.shape, lambda i: (0, 0)),
            pl.BlockSpec(own.shape, lambda i: (0, 0)),
            pl.BlockSpec(high.shape, lambda i: (0, 0)),
            pl.BlockSpec((per_step, NEAR, PANEL, PANEL), lambda i: (begin + i, 0, 0, 0)),
        ],
        out_specs=pl.BlockSpec((16, per_step * PANEL), lambda i: (0, i)),
        out_shape=jax.ShapeDtypeStruct((16, count * PANEL), jnp.float32),
        scratch_shapes=[pltpu.VMEM((16, (2 * HALO + LEAVES) * PANEL), jnp.bfloat16)],
        compiler_params=pltpu.CompilerParams(vmem_limit_bytes=32 << 20),
        cost_estimate=pl.CostEstimate(flops=count * 3_200_000, bytes_accessed=count * 200_000, transcendentals=0),
        name="near_field",
    )(place, src, low, own, high, blocks)


def group_sum_kernel(own_ref, other_ref, place, out_ref):
    def total(ref):
        parts = [ref[d, TERM_ROW : TERM_ROW + 16, :].astype(jnp.float32) for d in range(4)]
        both = (parts[0] + parts[1]) + (parts[2] + parts[3])
        return (both + pltpu.roll(both, RANK, 1)).astype(jnp.bfloat16)

    own, other = total(own_ref), total(other_ref)
    left = lane_index(16) < RANK
    first_core = jnp.full((16, 128), place[3], jnp.int32) == 0
    out_ref[...] = jnp.where(left == first_core, own, other)


def group_sums(own, other, place):
    return pl.pallas_call(
        group_sum_kernel,
        in_specs=[
            pl.BlockSpec(own.shape, lambda: (0, 0, 0)),
            pl.BlockSpec(other.shape, lambda: (0, 0, 0)),
            pl.BlockSpec(memory_space=pltpu.SMEM),
        ],
        out_shape=jax.ShapeDtypeStruct((16, 128), jnp.bfloat16),
        name="group_sums",
    )(own, other, place)


def down_kernel(place, far_src, top_src, groups_ref, ut_ref, dt_ref, kp_ref, dg_ref, dn_ref, out_ref, tops):
    y, z, parent, group = place[1], place[2], place[5], place[6]
    left = lane_index(16) < RANK

    def block(yy, zz):
        at = ((z - zz) & 3) * 4 + ((y - yy) & 3)
        return groups_ref[pl.ds(pl.multiple_of(at * 16, 16), 16), :]

    for h in range(8):
        yy, zz = h // 2, 2 * (h % 2)
        four = jnp.concatenate([block(yy, zz), block(yy, zz + 1)], axis=1)
        tops[h] = dot(four, ut_ref[h]).astype(jnp.bfloat16)
    by_group = jnp.zeros((16, 128), jnp.float32)
    by_top = jnp.zeros((16, 128), jnp.float32)
    for k in range(FAR):
        g = far_src[0, k]
        pair = block(g >> 3, (g >> 1) & 3).astype(jnp.float32)
        pair = jnp.where(jnp.full((16, 128), g & 1, jnp.int32) == 1, pltpu.roll(pair, RANK, 1), pair)
        both = kp_ref[k * RANK : (k + 1) * RANK, :]
        by_group = by_group + dot(pair[:, :RANK].astype(jnp.bfloat16), both)
        by_top = by_top + dot(tops[top_src[parent, k]], both)
    top_local = by_top[:, RANK:].astype(jnp.bfloat16)
    group_local = (by_group[:, :RANK] + dot(top_local, dt_ref[group])).astype(jnp.bfloat16)
    mid_local = dot(group_local, dg_ref[...]).astype(jnp.bfloat16)
    for n in range(8):
        out_ref[n * 16 : (n + 1) * 16, :] = dot(mid_local, dn_ref[n]).astype(jnp.bfloat16)


def down_sweep(place, far_src, top_src, groups, up_top, down_top, picked, down_group, down_node):
    smem = pl.BlockSpec(memory_space=pltpu.SMEM)
    last = LEAVES // 2
    return pl.pallas_call(
        down_kernel,
        grid=(1,),
        in_specs=[
            smem,
            smem,
            smem,
            pl.BlockSpec((256, 128), lambda i: (0, 0)),
            pl.BlockSpec((8, 256, RANK), lambda i: (0, 0, 0)),
            pl.BlockSpec((32, RANK, RANK), lambda i: (0, 0, 0)),
            pl.BlockSpec((KP_ROWS, 128), lambda i: (last, 0)),
            pl.BlockSpec((RANK, RANK), lambda i: (0, 0)),
            pl.BlockSpec((8, RANK, RANK), lambda i: (0, 0, 0)),
        ],
        out_specs=pl.BlockSpec((128, RANK), lambda i: (0, 0)),
        out_shape=jax.ShapeDtypeStruct((128, RANK), jnp.bfloat16),
        scratch_shapes=[pltpu.VMEM((8, 16, RANK), jnp.bfloat16)],
        compiler_params=pltpu.CompilerParams(vmem_limit_bytes=32 << 20),
        cost_estimate=pl.CostEstimate(flops=20_000_000, bytes_accessed=1_500_000, transcendentals=0),
        name="down_sweep",
    )(place, far_src, top_src, groups, up_top, down_top, picked, down_group, down_node)


def far_kernel(
    place, slot_ref, g0, g1, z0, z1, z2, z3, e0, e1, picked, rows_ref, node_ref, near0, near1, out_ref,
    table, kp, found, scalars, sems, kp_sems, scalar_sem,
):
    copies = []
    for j, ref in enumerate((g0, g1, z0, z1, z2, z3)):
        copies.append(pltpu.make_async_copy(ref, table.at[pl.ds(j * 4 * BLOCK, 4 * BLOCK), :], sems.at[j]))
    for j, ref in enumerate((e0, e1)):
        copies.append(pltpu.make_async_copy(ref, table.at[pl.ds((24 + j) * BLOCK, BLOCK), :], sems.at[6 + j]))
    for c in copies:
        c.start()
    chunks = kp_sems.shape[0]
    size = LEAVES // 2 * KP_ROWS // chunks
    kp_copies = [
        pltpu.make_async_copy(
            picked.at[pl.ds(j * size, size), :], kp.at[pl.ds(j * size, size), :], kp_sems.at[j]
        )
        for j in range(chunks)
    ]
    for c in kp_copies:
        c.start()

    x, core = place[4], place[3]
    i_in_block = core * 4 + x

    def slot_of(offset):
        at = i_in_block + offset
        away = at >> 3
        d = (x - at) & 3
        same = jnp.where(((at >> 2) & 1) == core, 0, 4)
        base = jnp.where(away == 0, 0, jnp.where(away < 0, 8, 16))
        inside = base + same + d
        far = jnp.where((offset == 10) | (offset == -10), 24, 25)
        return jnp.where((away > 1) | (away < -1), far, inside)

    slots = slot_ref[...]
    j_of = (slots * 1366) >> 16
    c_of = slots - j_of * SLOTS
    row_of = slot_of(j_of - 10) * BLOCK
    for c in copies:
        c.wait()
    leaf = jnp.zeros_like(slots)
    for j in range(OFFSETS):
        row = slot_of(jnp.int32(j - 10)) * BLOCK + TABLE_ROW + (j // 16) * 16
        rows = table[pl.ds(pl.multiple_of(row, 16), 16), :].astype(jnp.float32)
        line = jnp.broadcast_to(rows[j % 16 : j % 16 + 1, :], (8, 128)).astype(jnp.int32)
        here = jnp.take_along_axis(line, c_of, axis=1)
        leaf = jnp.where(j_of == j, here, leaf)
    leaf = leaf & (LEAVES - 1)
    found[...] = (row_of + (leaf >> 1) * 16) * 2 + (leaf & 1)
    to_scalars = pltpu.make_async_copy(found, scalars, scalar_sem)
    to_scalars.start()
    to_scalars.wait()

    left = lane_index(16) < RANK
    left_pair = lane_index(32) < RANK
    top_half = lax.broadcasted_iota(jnp.int32, (32, 128), 0) < 16

    def source(k, t, want):
        code = scalars[k, t]
        block = table[pl.ds(pl.multiple_of((code >> 1), 16), 16), :].astype(jnp.float32)
        return pltpu.roll(block, ((code & 1) ^ want) * RANK, 1)

    def coefficients(t):
        parts = []
        for m in range(FAR // 2):
            parts.append(jnp.where(left, source(2 * m, t, 0), source(2 * m + 1, t, 1)).astype(jnp.bfloat16))
        return jnp.concatenate(parts, axis=1)

    pairs = LEAVES // 2 // chunks
    for j in range(chunks):
        kp_copies[j].wait()

        @pl.loop(0, pairs)
        def _(q):
            i = j * pairs + q
            two = jnp.concatenate([coefficients(2 * i), coefficients(2 * i + 1)], axis=0)
            node = node_ref[pl.ds(pl.multiple_of((i // 4) * 16, 16), 16), :]
            node = jnp.concatenate([node, node], axis=0)
            base = pl.multiple_of(i * KP_ROWS, 64)
            local = dot(two, kp[pl.ds(base, FAR * RANK), :]) + dot(node, kp[pl.ds(base + FAR * RANK, RANK), :])
            local = jnp.where(left_pair == top_half, local, 0.0).astype(jnp.bfloat16)
            both = dot(local, rows_ref[i])
            near_ref = near0 if j < chunks // 2 else near1
            shift = 0 if j < chunks // 2 else LEAVES // 2 * PANEL
            at = pl.multiple_of(i * (2 * PANEL), 2 * PANEL)
            near_at = pl.multiple_of(i * (2 * PANEL) - shift, 2 * PANEL)
            near = near_ref[:, pl.ds(near_at, 2 * PANEL)]
            out_ref[:, pl.ds(at, 2 * PANEL)] = jnp.concatenate([both[:16], both[16:]], axis=1) + near


def far_field(place, slots, pieces, extras, picked, row_basis, node_local, near):
    smem = pl.BlockSpec(memory_space=pltpu.SMEM)
    hbm = pl.BlockSpec(memory_space=pl.ANY)
    chunks = 4
    return pl.pallas_call(
        far_kernel,
        grid=(1,),
        in_specs=[smem, pl.BlockSpec((8, 128), lambda i: (0, 0))]
        + [hbm] * 9
        + [
            pl.BlockSpec((LEAVES // 2, 128, 128), lambda i: (0, 0, 0)),
            pl.BlockSpec((128, RANK), lambda i: (0, 0)),
            pl.BlockSpec((16, LEAVES // 2 * PANEL), lambda i: (0, 0)),
            pl.BlockSpec((16, LEAVES // 2 * PANEL), lambda i: (0, 0)),
        ],
        out_specs=pl.BlockSpec((16, LEAVES * PANEL), lambda i: (0, 0)),
        out_shape=jax.ShapeDtypeStruct((16, LEAVES * PANEL), jnp.float32),
        scratch_shapes=[
            pltpu.VMEM((26 * BLOCK, 128), jnp.bfloat16),
            pltpu.VMEM((LEAVES // 2 * KP_ROWS, 128), jnp.bfloat16),
            pltpu.VMEM((8, 128), jnp.int32),
            pltpu.SMEM((8, 128), jnp.int32),
            pltpu.SemaphoreType.DMA((8,)),
            pltpu.SemaphoreType.DMA((chunks,)),
            pltpu.SemaphoreType.DMA,
        ],
        compiler_params=pltpu.CompilerParams(vmem_limit_bytes=48 << 20),
        cost_estimate=pl.CostEstimate(flops=300_000_000, bytes_accessed=11_000_000, transcendentals=0),
        name="far_field",
    )(place, slots, *pieces, *extras, picked, row_basis, node_local, *near)


def per_device(
    loads,
    col_basis,
    row_basis,
    near_blocks,
    near_src,
    up_leaf,
    down_leaf,
    up_node,
    down_node,
    up_group,
    down_group,
    up_top,
    downward_top_transfer,
    coupling,
    send_table,
    distant_leaf_slot_index,
    far_leaf_type,
    far_group_src,
    far_group_type,
    far_top_src,
    far_top_type,
):
    group = lax.axis_index("leaf")
    sub = lax.axis_index("sub")
    pos = group * 4 + sub
    place = jnp.stack([pos, group >> 3, (group >> 1) & 3, group & 1, sub, group >> 2, group, group]).astype(jnp.int32)
    table = jnp.pad(send_table[0], ((0, 32 - OFFSETS), (0, 128 - SLOTS)))
    slots = jnp.pad(distant_leaf_slot_index.T, ((0, 0), (0, 128 - LEAVES)))

    half = HALO * PANEL
    low = moved(loads[:, half:], line_shift(1))
    high = moved(loads[:, :half], line_shift(-1))

    own = up_sweep(
        loads,
        jnp.swapaxes(col_basis, 1, 2).reshape(LEAVES // 2, 128, PANEL),
        up_leaf.reshape(8, 8 * RANK, RANK),
        up_node,
        up_group[0],
        table,
    )
    extra = [moved(own, two_blocks_away(2, 10)), moved(own, two_blocks_away(1, 9))]
    along_x = [moved(own, x_shift(d)) for d in (1, 2, 3)]
    mine = jnp.concatenate([own] + along_x, axis=0)
    theirs = moved(mine, CORE_SWAP)
    below = moved(mine, line_shift(8))
    above = moved(mine, line_shift(-8))

    picked = picked_couplings(
        place,
        far_leaf_type.T,
        far_group_type,
        far_top_type,
        jnp.transpose(coupling, (1, 2, 0)).reshape(RANK * RANK, TYPES),
        down_leaf,
    )
    near = [near_field(place, near_src.T, low, loads, high, near_blocks, f, LEAVES // 2) for f in (0, LEAVES // 2)]

    pair = group_sums(mine.reshape(4, BLOCK, 128), theirs.reshape(4, BLOCK, 128), place)
    column = jnp.concatenate([pair] + [moved(pair, y_shift(d)) for d in (1, 2, 3)], axis=0)
    groups = jnp.concatenate([column] + [moved(column, z_shift(d)) for d in (1, 2, 3)], axis=0)
    node_local = down_sweep(
        place,
        far_group_src,
        far_top_src,
        groups,
        up_top.reshape(8, 4 * RANK, RANK),
        downward_top_transfer,
        picked,
        down_group[0],
        down_node,
    )
    pieces = [mine, theirs, below, moved(below, CORE_SWAP), above, moved(above, CORE_SWAP)]
    return far_field(
        place,
        slots,
        pieces,
        extra,
        picked,
        jnp.swapaxes(row_basis, 1, 2).reshape(LEAVES // 2, 2 * RANK, PANEL),
        node_local,
        near,
    )


def solution(mesh):
    whole, split = P(), P(AXES)
    return jax.shard_map(
        per_device,
        mesh=mesh,
        in_specs=(
            P(None, AXES),
            split, split, split, split, split, split, split, split, split, split,
            whole, whole, whole,
            split, split, split,
            P("leaf"), P("leaf"),
            whole, whole,
        ),
        out_specs=P(None, AXES),
        check_vma=False,
    )
```

time: 219 us -> 135 us (0.62)
  the two profiles are of different devices: /device:TPU:16 before, /device:TPU:10 now
where the time goes in v1:
time: 135 us; the launch traced here: 134 us
  Pallas kernels  55.4 us (41%)
  starting transfers between devices  38.2 us (28%)
  local copies, waits for them, and re-layouts  19.6 us (15%)
  waiting for transfers between devices  19.5 us (14%)
    ppermute x18, starting transfers between devices, moved(): return lax.ppermute(value, AXES, pairs)  38.2 us
    pallas_call x1, Pallas kernels, picked_couplings(): pl.pallas_call(pick_kernel, grid=(steps,), in_specs=[smem, smem, smem, sm...  25.5 us
    ppermute x18, waiting for transfers between devices, moved(): return lax.ppermute(value, AXES, pairs)  19.5 us
    unnamed x63, local copies, waits for them, and re-layouts  19.5 us
    pallas_call x1, Pallas kernels, far_field(): pl.pallas_call(far_kernel, grid=(1,), in_specs=[smem, pl.BlockSpec((8, 12...  14.7 us
    pallas_call x2, Pallas kernels, near_field(): pl.pallas_call(functools.partial(near_kernel, first, per_step), grid=(cou...  8.79 us
    pallas_call x1, Pallas kernels, up_sweep(): pl.pallas_call(up_kernel, grid=(steps,), in_specs=[pl.BlockSpec((16, 8192...  3.07 us
  transfers between devices with their start and end apart: 18, of which 6 were waited for; matrix products, arithmetic and copies ran while one was open for 1% of the time, Pallas kernels for 28%

profile of v1, /device:TPU:10, one launch (start us, length us, event | category | flops | bytes accessed | tf_op | source)
XLA Modules:
  0.0 133.7 jit_solution(9810274520648118549)
XLA Ops:
  0.0 0.7 copy.24
  0.7 0.9 copy-done.4
  1.7 1.2 copy-done.9
  2.9 1.2 copy-done.10
  4.1 0.9 copy-done.14
  5.0 0.7 copy-done.18
  5.7 3.1 %up_sweep.1 = bf16[560,128]{1,0:T(8,128)(2,1)S(1)} custom-call(bf16[16,8192]{1,0:T(8,128)(2,1)S(1)} %copy-done.4, bf16[32,128,128]{2,1,0:T(8,128)(2,1)S(1)} %bitcast.31, bf16[8,512,64]{2,1,0:T(8,128)(2,1)S(1)} %bitcast.32, bf16[8,64,64]{2,1,0:T(8,128)(2,1)S(1)} %copy-done.14, bf16[64,64]{1,0:T(8,128)(2,1)S(1)} %bitcast.36, s32[32,128]{1,0:T(8,128)S(1)} %pad.9.table_ref), custom_call_target="tpu_custom_call" | custom-call | flops 40000000 | bytes 2600000 | tf_op jit(solution)/shard_map/up_sweep/pallas_call | solution.py:113
  8.8 0.6 collective-permute-start.2
  9.4 2.4 %collective-permute-start.1 = (bf16[560,128]{1,0:T(8,128)(2,1)S(1)}, bf16[560,128]{1,0:T(8,128)(2,1)S(1)}, u32[]{:S(2)}, u32[]{:S(2)}) collective-permute-start(bf16[560,128]{1,0:T(8,128)(2,1)S(1)} %up_sweep.1), channel_id=1, source_target_pairs={{0,2},{1,3},{2,0},{3,1},{4,6},{5,7},{6,4},{7,5},{8,10},{9,11},{10,... | collective-permute-start | bytes 430088 | tf_op jit(solution)/shard_map/ppermute | solution.py:42
  11.9 1.8 %collective-permute-start = (bf16[560,128]{1,0:T(8,128)(2,1)S(1)}, bf16[560,128]{1,0:T(8,128)(2,1)S(1)}, u32[]{:S(2)}, u32[]{:S(2)}) collective-permute-start(bf16[560,128]{1,0:T(8,128)(2,1)S(1)} %up_sweep.1), channel_id=1, source_target_pairs={{0,1},{1,2},{2,3},{3,0},{4,5},{5,6},{6,7},{7,4},{8,9},{9,10},{10,1... | collective-permute-start | bytes 430088 | tf_op jit(solution)/shard_map/ppermute | solution.py:42
  13.7 1.0 collective-permute-done.2
  14.6 3.8 %collective-permute-done.1 = bf16[560,128]{1,0:T(8,128)(2,1)S(1)} collective-permute-done((bf16[560,128]{1,0:T(8,128)(2,1)S(1)}, bf16[560,128]{1,0:T(8,128)(2,1)S(1)}, u32[]{:S(2)}, u32[]{:S(2)}) %collective-permute-start.1) | collective-permute-done | bytes 143392 | tf_op jit(solution)/shard_map/ppermute | solution.py:42
  18.4 0.9 collective-permute-done
  19.3 5.8 %collective-permute-start.6 = (bf16[2240,128]{1,0:T(8,128)(2,1)S(1)}, bf16[2240,128]{1,0:T(8,128)(2,1)S(1)}, u32[]{:S(2)}, u32[]{:S(2)}) collective-permute-start(bf16[2240,128]{1,0:T(8,128)(2,1)S(1)} %pad_maximum_fusion.g0), channel_id=1, source_target_pairs={{8,0},{9,1},{10,2},{11,3},{12,4},{13,5},{14,6},{15,7},{16,8},{17,9... | collective-permute-start | bytes 1720328 | tf_op jit(solution)/shard_map/ppermute | solution.py:42
  25.2 1.9 %collective-permute-start.4 = (bf16[2240,128]{1,0:T(8,128)(2,1)S(1)}, bf16[2240,128]{1,0:T(8,128)(2,1)S(1)}, u32[]{:S(2)}, u32[]{:S(2)}) collective-permute-start(bf16[2240,128]{1,0:T(8,128)(2,1)S(1)} %pad_maximum_fusion.g0), channel_id=1, source_target_pairs={{0,8},{1,9},{2,10},{3,11},{4,12},{5,13},{6,14},{7,15},{8,16},{9,17... | collective-permute-start | bytes 1720328 | tf_op jit(solution)/shard_map/ppermute | solution.py:42
  27.1 0.1 collective-permute-start.3
  27.2 4.6 %collective-permute-start.17 = (bf16[16,4096]{1,0:T(8,128)(2,1)S(1)}, bf16[16,4096]{1,0:T(8,128)(2,1)S(1)}, u32[]{:S(2)}, u32[]{:S(2)}) collective-permute-start(bf16[16,4096]{1,0:T(8,128)(2,1)S(1)} %get-tuple-element.5), channel_id=1, source_target_pairs={{1,0},{2,1},{3,2},{4,3},{5,4},{6,5},{7,6},{8,7},{9,8},{10,9},{11,1... | collective-permute-start | bytes 393224 | tf_op jit(solution)/shard_map/ppermute | solution.py:42
  31.9 1.9 %collective-permute-start.16 = (bf16[16,4096]{1,0:T(8,128)(2,1)S(1)}, bf16[16,4096]{1,0:T(8,128)(2,1)S(1)}, u32[]{:S(2)}, u32[]{:S(2)}) collective-permute-start(bf16[16,4096]{1,0:T(8,128)(2,1)S(1)} %get-tuple-element.6), channel_id=1, source_target_pairs={{0,1},{1,2},{2,3},{3,4},{4,5},{5,6},{6,7},{7,8},{8,9},{9,10},{10,1... | collective-permute-start | bytes 393224 | tf_op jit(solution)/shard_map/ppermute | solution.py:42
  33.8 0.1 stack.32.place
  33.9 0.0 copy-start.22
  33.9 1.9 %copy-done.22 = bf16[316,64,64]{0,2,1:T(8,128)(2,1)S(1)} copy-done((bf16[316,64,64]{0,2,1:T(8,128)(2,1)S(1)}, bf16[316,64,64]{0,2,1:T(8,128)(2,1)}, u32[]{:S(2)}) %copy-start.22) | copy-done | bytes 2588696
  35.8 1.2 copy-done.23
  37.0 25.5 %pick_couplings.1.kp_ref.picked = bf16[19008,128]{1,0:T(8,128)(2,1)} custom-call(s32[8]{0:T(128)S(1)} %stack.32.place, s32[8,64]{1,0:T(8,128)S(1)} %bitcast.39, s32[1,8]{1,0:T(1,128)S(1)} %copy-done.26, s32[8,8]{1,0:T(8,128)S(1)} %copy-done.25, bf16[4096,316]{1,0:T(8,128)(2,1)S(1)} %bitcast.38, bf16[64,64,64]{2,1,0:T(8,128)(2,1)S(1)} %copy-done.23), custom_call_target="tpu_custom_call" | custom-call | flops 3200000000 | bytes 9000000 | tf_op jit(solution)/shard_map/pick_couplings/pallas_call | solution.py:177
  62.5 0.0 collective-permute-done.17.high_ref
  62.5 0.0 collective-permute-done.16.low_ref
  62.6 0.0 copy-start
  62.6 4.6 %copy-done = bf16[64,6,128,128]{3,2,1,0:T(8,128)(2,1)S(1)} copy-done((bf16[64,6,128,128]{3,2,1,0:T(8,128)(2,1)S(1)}, bf16[64,6,128,128]{3,2,1,0:T(8,128)(2,1)}, u32[]{:S(2)}) %copy-start) | copy-done | bytes 12582936
  67.2 4.4 %near_field.3.near1 = f32[16,4096]{1,0:T(8,128)S(1)} custom-call(s32[8]{0:T(128)S(1)} %stack.32.place, s32[6,64]{1,0:T(8,128)S(1)} %bitcast.34, bf16[16,4096]{1,0:T(8,128)(2,1)S(1)} %collective-permute-done.16.low_ref, bf16[16,8192]{1,0:T(8,128)(2,1)S(1)} %copy-done.5, bf16[16,4096]{1,0:T(8,128)(2,1)S(1)} %collective-permute-done.17.high_ref, ...), custom_call_target="tpu_custom_call" | custom-call | flops 102400000 | bytes 6400000 | tf_op jit(solution)/shard_map/near_field/pallas_call | solution.py:220
  71.5 4.4 %near_field.2.near0 = f32[16,4096]{1,0:T(8,128)S(1)} custom-call(s32[8]{0:T(128)S(1)} %stack.32.place, s32[6,64]{1,0:T(8,128)S(1)} %bitcast.35, bf16[16,4096]{1,0:T(8,128)(2,1)S(1)} %collective-permute-done.16.low_ref, bf16[16,8192]{1,0:T(8,128)(2,1)S(1)} %copy-done.5, bf16[16,4096]{1,0:T(8,128)(2,1)S(1)} %collective-permute-done.17.high_ref, ...), custom_call_target="tpu_custom_call" | custom-call | flops 102400000 | bytes 6400000 | tf_op jit(solution)/shard_map/near_field/pallas_call | solution.py:220
  76.0 0.0 copy-start.19
  76.0 0.0 copy-start.20
  76.0 0.0 copy-start.21
  76.0 0.0 collective-permute-done.3.g1
  76.0 0.8 copy-done.6
  76.8 1.9 %group_sums.1 = bf16[16,128]{1,0:T(8,128)(2,1)} custom-call(bf16[4,560,128]{2,1,0:T(8,128)(2,1)} %bitcast.28, bf16[4,560,128]{2,1,0:T(8,128)(2,1)} %bitcast.29, s32[8]{0:T(128)} %copy-done.15), custom_call_target="tpu_custom_call" | custom-call | tf_op jit(solution)/shard_map/group_sums/pallas_call | solution.py:253
  78.8 0.0 collective-permute-start.12
  78.8 3.0 %collective-permute-start.11 = (bf16[16,128]{1,0:T(8,128)(2,1)}, bf16[16,128]{1,0:T(8,128)(2,1)S(1)}, u32[]{:S(2)}, u32[]{:S(2)}) collective-permute-start(bf16[16,128]{1,0:T(8,128)(2,1)} %group_sums.1), channel_id=1, source_target_pairs={{0,64},{1,65},{2,66},{3,67},{4,68},{5,69},{6,70},{7,71},{8,72},{9,... | collective-permute-start | bytes 12296 | tf_op jit(solution)/shard_map/ppermute | solution.py:42
  81.8 2.2 %collective-permute-start.10 = (bf16[16,128]{1,0:T(8,128)(2,1)}, bf16[16,128]{1,0:T(8,128)(2,1)S(1)}, u32[]{:S(2)}, u32[]{:S(2)}) collective-permute-start(bf16[16,128]{1,0:T(8,128)(2,1)} %group_sums.1), channel_id=1, source_target_pairs={{0,32},{1,33},{2,34},{3,35},{4,36},{5,37},{6,38},{7,39},{8,40},{9,... | collective-permute-start | bytes 12296 | tf_op jit(solution)/shard_map/ppermute | solution.py:42
  84.0 0.7 constant_dynamic-update-slice_fusion.6
  84.7 0.0 collective-permute-done.6.z2
  84.7 0.7 collective-permute-start.9
  85.4 0.0 collective-permute-done.4.z0
  85.4 12.5 %collective-permute-start.8 = (bf16[560,128]{1,0:T(8,128)(2,1)S(1)}, bf16[560,128]{1,0:T(8,128)(2,1)S(1)}, u32[]{:S(2)}, u32[]{:S(2)}) collective-permute-start(bf16[560,128]{1,0:T(8,128)(2,1)S(1)} %up_sweep.1), channel_id=1, source_target_pairs={{16,6},{17,7},{24,14},{25,15},{6,16},{7,17},{32,22},{33,23},{14,24... | collective-permute-start | bytes 430088 | tf_op jit(solution)/shard_map/ppermute | solution.py:42
  97.8 0.0 collective-permute-done.12
  97.8 0.1 collective-permute-start.7
  97.9 0.0 collective-permute-done.11
  98.0 0.5 collective-permute-start.5
  98.4 0.0 collective-permute-done.10
  98.4 0.7 pad_maximum_fusion.1
  99.1 0.0 collective-permute-start.13
  99.2 4.9 %collective-permute-done.13 = bf16[64,128]{1,0:T(8,128)(2,1)S(1)} collective-permute-done((bf16[64,128]{1,0:T(8,128)(2,1)S(1)}, bf16[64,128]{1,0:T(8,128)(2,1)S(1)}, u32[]{:S(2)}, u32[]{:S(2)}) %collective-permute-start.13) | collective-permute-done | bytes 16416 | tf_op jit(solution)/shard_map/ppermute | solution.py:42
  104.1 0.0 collective-permute-start.14
  104.1 5.2 %collective-permute-done.14 = bf16[64,128]{1,0:T(8,128)(2,1)S(1)} collective-permute-done((bf16[64,128]{1,0:T(8,128)(2,1)S(1)}, bf16[64,128]{1,0:T(8,128)(2,1)S(1)}, u32[]{:S(2)}, u32[]{:S(2)}) %collective-permute-start.14) | collective-permute-done | bytes 16416 | tf_op jit(solution)/shard_map/ppermute | solution.py:42
  109.3 0.0 collective-permute-start.15
  109.3 3.7 %collective-permute-done.15 = bf16[64,128]{1,0:T(8,128)(2,1)S(1)} collective-permute-done((bf16[64,128]{1,0:T(8,128)(2,1)S(1)}, bf16[64,128]{1,0:T(8,128)(2,1)S(1)}, u32[]{:S(2)}, u32[]{:S(2)}) %collective-permute-start.15) | collective-permute-done | bytes 16416 | tf_op jit(solution)/shard_map/ppermute | solution.py:42
  113.1 2.4 %copy-done.1 = bf16[19008,128]{1,0:T(8,128)(2,1)S(1)} copy-done((bf16[19008,128]{1,0:T(8,128)(2,1)S(1)}, bf16[19008,128]{1,0:T(8,128)(2,1)}, u32[]{:S(2)}) %copy-start.1) | copy-done | bytes 4866072
  115.5 1.0 copy-done.12
  116.5 0.9 copy-done.13
  117.4 1.4 %down_sweep.1.node_ref = bf16[128,64]{1,0:T(8,128)(2,1)S(1)} custom-call(s32[8]{0:T(128)S(1)} %copy-done.16, s32[1,8]{1,0:T(1,128)S(1)} %copy-done.21, s32[8,8]{1,0:T(8,128)S(1)} %copy-done.20, bf16[256,128]{1,0:T(8,128)(2,1)S(1)} %constant_dynamic-update-slice_fusion.groups_ref, bf16[8,256,64]{2,1,0:T(8,128)(2,1)S(1)} %bitcast.33, ...), custom_call_target="tpu_custom_call" | custom-call | flops 20000000 | bytes 1500000 | tf_op jit(solution)/shard_map/down_sweep/pallas_call | solution.py:296
  118.9 0.0 collective-permute-done.8.e0
  118.9 0.0 collective-permute-done.7.z3
  118.9 0.0 collective-permute-done.5.z1
  118.9 0.1 copy-done.8
  119.0 14.7 %far_field.1 = f32[16,8192]{1,0:T(8,128)} custom-call(s32[8]{0:T(128)S(1)} %copy-done.16, s32[8,128]{1,0:T(8,128)S(1)} %pad.8.slot_ref, bf16[2240,128]{1,0:T(8,128)(2,1)S(1)} %copy-done.3, bf16[2240,128]{1,0:T(8,128)(2,1)S(1)} %copy-done.7, bf16[2240,128]{1,0:T(8,128)(2,1)S(1)} %collective-permute-done.4.z0, ...), custom_call_target="tpu_custom_call" | custom-call | flops 300000000 | bytes 11000000 | tf_op jit(solution)/shard_map/far_field/pallas_call | solution.py:414
  (49 shorter events, 0.2 us)
Async XLA Ops:
  0.7 0.9 copy-start.4
  1.7 1.2 copy-start.9
  2.9 1.2 copy-start.10
  4.1 0.9 copy-start.14
  5.0 0.7 copy-start.18
  8.8 25.1 %copy-start.24 = (s32[64,8]{0,1:T(8,128)S(1)}, s32[64,8]{0,1:T(8,128)}, u32[]{:S(2)}) copy-start(s32[64,8]{0,1:T(8,128)} %param.37) | copy-start | bytes 6148
  8.8 25.1 %copy-start.25 = (s32[8,8]{1,0:T(8,128)S(1)}, s32[8,8]{1,0:T(8,128)}, u32[]{:S(2)}) copy-start(s32[8,8]{1,0:T(8,128)} %top_type.1) | copy-start | bytes 772
  8.8 25.1 %copy-start.26 = (s32[1,8]{1,0:T(1,128)S(1)}, s32[1,8]{1,0:T(1,128)}, u32[]{:S(2)}) copy-start(s32[1,8]{1,0:T(1,128)} %group_type.1) | copy-start | bytes 100
  8.8 5.8 %collective-permute-start.2 = (bf16[560,128]{1,0:T(8,128)(2,1)S(1)}, bf16[560,128]{1,0:T(8,128)(2,1)S(1)}, u32[]{:S(2)}, u32[]{:S(2)}) collective-permute-start(bf16[560,128]{1,0:T(8,128)(2,1)S(1)} %up_sweep.1), channel_id=1, source_target_pairs={{0,3},{1,0},{2,1},{3,2},{4,7},{5,4},{6,5},{7,6},{8,11},{9,8},{10,9... | collective-permute-start | bytes 430088 | tf_op jit(solution)/shard_map/ppermute | solution.py:42
  9.4 9.0 %collective-permute-start.1 = (bf16[560,128]{1,0:T(8,128)(2,1)S(1)}, bf16[560,128]{1,0:T(8,128)(2,1)S(1)}, u32[]{:S(2)}, u32[]{:S(2)}) collective-permute-start(bf16[560,128]{1,0:T(8,128)(2,1)S(1)} %up_sweep.1), channel_id=1, source_target_pairs={{0,2},{1,3},{2,0},{3,1},{4,6},{5,7},{6,4},{7,5},{8,10},{9,11},{10,... | collective-permute-start | bytes 430088 | tf_op jit(solution)/shard_map/ppermute | solution.py:42
  11.9 7.4 %collective-permute-start = (bf16[560,128]{1,0:T(8,128)(2,1)S(1)}, bf16[560,128]{1,0:T(8,128)(2,1)S(1)}, u32[]{:S(2)}, u32[]{:S(2)}) collective-permute-start(bf16[560,128]{1,0:T(8,128)(2,1)S(1)} %up_sweep.1), channel_id=1, source_target_pairs={{0,1},{1,2},{2,3},{3,0},{4,5},{5,6},{6,7},{7,4},{8,9},{9,10},{10,1... | collective-permute-start | bytes 430088 | tf_op jit(solution)/shard_map/ppermute | solution.py:42
  19.3 43.2 %copy-start.2 = (bf16[2240,128]{1,0:T(8,128)(2,1)}, bf16[2240,128]{1,0:T(8,128)(2,1)S(1)}, u32[]{:S(2)}) copy-start(bf16[2240,128]{1,0:T(8,128)(2,1)S(1)} %pad_maximum_fusion.g0) | copy-start | bytes 1720324
  19.3 65.4 %collective-permute-start.6 = (bf16[2240,128]{1,0:T(8,128)(2,1)S(1)}, bf16[2240,128]{1,0:T(8,128)(2,1)S(1)}, u32[]{:S(2)}, u32[]{:S(2)}) collective-permute-start(bf16[2240,128]{1,0:T(8,128)(2,1)S(1)} %pad_maximum_fusion.g0), channel_id=1, source_target_pairs={{8,0},{9,1},{10,2},{11,3},{12,4},{13,5},{14,6},{15,7},{16,8},{17,9... | collective-permute-start | bytes 1720328 | tf_op jit(solution)/shard_map/ppermute | solution.py:42
  25.2 60.2 %collective-permute-start.4 = (bf16[2240,128]{1,0:T(8,128)(2,1)S(1)}, bf16[2240,128]{1,0:T(8,128)(2,1)S(1)}, u32[]{:S(2)}, u32[]{:S(2)}) collective-permute-start(bf16[2240,128]{1,0:T(8,128)(2,1)S(1)} %pad_maximum_fusion.g0), channel_id=1, source_target_pairs={{0,8},{1,9},{2,10},{3,11},{4,12},{5,13},{6,14},{7,15},{8,16},{9,17... | collective-permute-start | bytes 1720328 | tf_op jit(solution)/shard_map/ppermute | solution.py:42
  27.1 48.9 %collective-permute-start.3 = (bf16[2240,128]{1,0:T(8,128)(2,1)S(1)}, bf16[2240,128]{1,0:T(8,128)(2,1)S(1)}, u32[]{:S(2)}, u32[]{:S(2)}) collective-permute-start(bf16[2240,128]{1,0:T(8,128)(2,1)S(1)} %pad_maximum_fusion.g0), channel_id=1, source_target_pairs={{0,4},{1,5},{2,6},{3,7},{4,0},{5,1},{6,2},{7,3},{8,12},{9,13},{10,... | collective-permute-start | bytes 1720328 | tf_op jit(solution)/shard_map/ppermute | solution.py:42
  27.2 35.3 %collective-permute-start.17 = (bf16[16,4096]{1,0:T(8,128)(2,1)S(1)}, bf16[16,4096]{1,0:T(8,128)(2,1)S(1)}, u32[]{:S(2)}, u32[]{:S(2)}) collective-permute-start(bf16[16,4096]{1,0:T(8,128)(2,1)S(1)} %get-tuple-element.5), channel_id=1, source_target_pairs={{1,0},{2,1},{3,2},{4,3},{5,4},{6,5},{7,6},{8,7},{9,8},{10,9},{11,1... | collective-permute-start | bytes 393224 | tf_op jit(solution)/shard_map/ppermute | solution.py:42
  31.9 30.7 %collective-permute-start.16 = (bf16[16,4096]{1,0:T(8,128)(2,1)S(1)}, bf16[16,4096]{1,0:T(8,128)(2,1)S(1)}, u32[]{:S(2)}, u32[]{:S(2)}) collective-permute-start(bf16[16,4096]{1,0:T(8,128)(2,1)S(1)} %get-tuple-element.6), channel_id=1, source_target_pairs={{0,1},{1,2},{2,3},{3,4},{4,5},{5,6},{6,7},{7,8},{8,9},{9,10},{10,1... | collective-permute-start | bytes 393224 | tf_op jit(solution)/shard_map/ppermute | solution.py:42
  33.9 37.7 %copy-start.15 = (s32[8]{0:T(128)}, s32[8]{0:T(128)S(1)}, u32[]{:S(2)}) copy-start(s32[8]{0:T(128)S(1)} %stack.32.place) | copy-start | bytes 100
  33.9 1.9 %copy-start.22 = (bf16[316,64,64]{0,2,1:T(8,128)(2,1)S(1)}, bf16[316,64,64]{0,2,1:T(8,128)(2,1)}, u32[]{:S(2)}) copy-start(bf16[316,64,64]{0,2,1:T(8,128)(2,1)} %param.34) | copy-start | bytes 7766020
  35.8 1.2 copy-start.23
  37.0 25.5 %copy-start.27 = (s32[64,8]{0,1:T(8,128)S(1)}, s32[64,8]{0,1:T(8,128)}, u32[]{:S(2)}) copy-start(s32[64,8]{0,1:T(8,128)} %param.36) | copy-start | bytes 6148
  37.0 25.5 %copy-start.5 = (bf16[16,8192]{1,0:T(8,128)(2,1)S(1)}, bf16[16,8192]{1,0:T(8,128)(2,1)}, u32[]{:S(2)}) copy-start(bf16[16,8192]{1,0:T(8,128)(2,1)} %own_ref.3) | copy-start | bytes 786436
  37.0 25.5 %copy-start.17 = (s32[64,6]{0,1:T(8,128)S(1)}, s32[64,6]{0,1:T(8,128)}, u32[]{:S(2)}) copy-start(s32[64,6]{0,1:T(8,128)} %param.25) | copy-start | bytes 4612
  62.6 4.6 %copy-start = (bf16[64,6,128,128]{3,2,1,0:T(8,128)(2,1)S(1)}, bf16[64,6,128,128]{3,2,1,0:T(8,128)(2,1)}, u32[]{:S(2)}) copy-start(bf16[64,6,128,128]{3,2,1,0:T(8,128)(2,1)} %blocks_ref.3) | copy-start | bytes 37748740
  75.9 37.1 %copy-start.11 = (bf16[32,64,64]{2,1,0:T(8,128)(2,1)S(1)}, bf16[32,64,64]{2,1,0:T(8,128)(2,1)}, u32[]{:S(2)}) copy-start(bf16[32,64,64]{2,1,0:T(8,128)(2,1)} %param.32) | copy-start | bytes 786436
  75.9 37.1 %copy-start.16 = (s32[8]{0:T(128)S(1)}, s32[8]{0:T(128)}, u32[]{:S(2)}) copy-start(s32[8]{0:T(128)} %copy-done.15) | copy-start | bytes 100
  76.0 37.1 %copy-start.19 = (bf16[1,64,64]{2,1,0:T(8,128)(2,1)S(1)}, bf16[1,64,64]{2,1,0:T(8,128)(2,1)}, u32[]{:S(2)}) copy-start(bf16[1,64,64]{2,1,0:T(8,128)(2,1)} %param.31) | copy-start | bytes 24580
  76.0 37.1 %copy-start.20 = (s32[8,8]{1,0:T(8,128)S(1)}, s32[8,8]{1,0:T(8,128)}, u32[]{:S(2)}) copy-start(s32[8,8]{1,0:T(8,128)} %top_src.1) | copy-start | bytes 772
  76.0 37.1 %copy-start.21 = (s32[1,8]{1,0:T(1,128)S(1)}, s32[1,8]{1,0:T(1,128)}, u32[]{:S(2)}) copy-start(s32[1,8]{1,0:T(1,128)} %far_src.1) | copy-start | bytes 100
  76.0 0.8 copy-start.6
  78.8 19.1 %collective-permute-start.12 = (bf16[16,128]{1,0:T(8,128)(2,1)}, bf16[16,128]{1,0:T(8,128)(2,1)S(1)}, u32[]{:S(2)}, u32[]{:S(2)}) collective-permute-start(bf16[16,128]{1,0:T(8,128)(2,1)} %group_sums.1), channel_id=1, source_target_pairs={{0,96},{1,97},{2,98},{3,99},{4,100},{5,101},{6,102},{7,103},{8,104... | collective-permute-start | bytes 12296 | tf_op jit(solution)/shard_map/ppermute | solution.py:42
  78.8 19.2 %collective-permute-start.11 = (bf16[16,128]{1,0:T(8,128)(2,1)}, bf16[16,128]{1,0:T(8,128)(2,1)S(1)}, u32[]{:S(2)}, u32[]{:S(2)}) collective-permute-start(bf16[16,128]{1,0:T(8,128)(2,1)} %group_sums.1), channel_id=1, source_target_pairs={{0,64},{1,65},{2,66},{3,67},{4,68},{5,69},{6,70},{7,71},{8,72},{9,... | collective-permute-start | bytes 12296 | tf_op jit(solution)/shard_map/ppermute | solution.py:42
  81.8 16.7 %collective-permute-start.10 = (bf16[16,128]{1,0:T(8,128)(2,1)}, bf16[16,128]{1,0:T(8,128)(2,1)S(1)}, u32[]{:S(2)}, u32[]{:S(2)}) collective-permute-start(bf16[16,128]{1,0:T(8,128)(2,1)} %group_sums.1), channel_id=1, source_target_pairs={{0,32},{1,33},{2,34},{3,35},{4,36},{5,37},{6,38},{7,39},{8,40},{9,... | collective-permute-start | bytes 12296 | tf_op jit(solution)/shard_map/ppermute | solution.py:42
  84.7 34.2 %collective-permute-start.9 = (bf16[560,128]{1,0:T(8,128)(2,1)S(1)}, bf16[560,128]{1,0:T(8,128)(2,1)S(1)}, u32[]{:S(2)}, u32[]{:S(2)}) collective-permute-start(bf16[560,128]{1,0:T(8,128)(2,1)S(1)} %up_sweep.1), channel_id=1, source_target_pairs={{16,7},{24,15},{7,16},{32,23},{15,24},{40,31},{23,32},{48,39},{31,... | collective-permute-start | bytes 430088 | tf_op jit(solution)/shard_map/ppermute | solution.py:42
  85.4 33.5 %collective-permute-start.8 = (bf16[560,128]{1,0:T(8,128)(2,1)S(1)}, bf16[560,128]{1,0:T(8,128)(2,1)S(1)}, u32[]{:S(2)}, u32[]{:S(2)}) collective-permute-start(bf16[560,128]{1,0:T(8,128)(2,1)S(1)} %up_sweep.1), channel_id=1, source_target_pairs={{16,6},{17,7},{24,14},{25,15},{6,16},{7,17},{32,22},{33,23},{14,24... | collective-permute-start | bytes 430088 | tf_op jit(solution)/shard_map/ppermute | solution.py:42
  97.8 21.0 %collective-permute-start.7 = (bf16[2240,128]{1,0:T(8,128)(2,1)S(1)}, bf16[2240,128]{1,0:T(8,128)(2,1)S(1)}, u32[]{:S(2)}, u32[]{:S(2)}) collective-permute-start(bf16[2240,128]{1,0:T(8,128)(2,1)S(1)} %collective-permute-done.6.z2), channel_id=1, source_target_pairs={{0,4},{1,5},{2,6},{3,7},{4,0},{5,1},{6,2},{7,3},{8,12},{9,13},{10,... | collective-permute-start | bytes 1720328 | tf_op jit(solution)/shard_map/ppermute | solution.py:42
  98.0 20.9 %collective-permute-start.5 = (bf16[2240,128]{1,0:T(8,128)(2,1)S(1)}, bf16[2240,128]{1,0:T(8,128)(2,1)S(1)}, u32[]{:S(2)}, u32[]{:S(2)}) collective-permute-start(bf16[2240,128]{1,0:T(8,128)(2,1)S(1)} %collective-permute-done.4.z0), channel_id=1, source_target_pairs={{0,4},{1,5},{2,6},{3,7},{4,0},{5,1},{6,2},{7,3},{8,12},{9,13},{10,... | collective-permute-start | bytes 1720328 | tf_op jit(solution)/shard_map/ppermute | solution.py:42
  99.1 4.9 %collective-permute-start.13 = (bf16[64,128]{1,0:T(8,128)(2,1)S(1)}, bf16[64,128]{1,0:T(8,128)(2,1)S(1)}, u32[]{:S(2)}, u32[]{:S(2)}) collective-permute-start(bf16[64,128]{1,0:T(8,128)(2,1)S(1)} %pad_maximum_fusion.1), channel_id=1, source_target_pairs={{0,8},{1,9},{2,10},{3,11},{4,12},{5,13},{6,14},{7,15},{8,16},{9,17... | collective-permute-start | bytes 49160 | tf_op jit(solution)/shard_map/ppermute | solution.py:42
  104.1 5.2 %collective-permute-start.14 = (bf16[64,128]{1,0:T(8,128)(2,1)S(1)}, bf16[64,128]{1,0:T(8,128)(2,1)S(1)}, u32[]{:S(2)}, u32[]{:S(2)}) collective-permute-start(bf16[64,128]{1,0:T(8,128)(2,1)S(1)} %pad_maximum_fusion.1), channel_id=1, source_target_pairs={{0,16},{1,17},{2,18},{3,19},{4,20},{5,21},{6,22},{7,23},{8,24},{9,... | collective-permute-start | bytes 49160 | tf_op jit(solution)/shard_map/ppermute | solution.py:42
  109.3 3.7 %collective-permute-start.15 = (bf16[64,128]{1,0:T(8,128)(2,1)S(1)}, bf16[64,128]{1,0:T(8,128)(2,1)S(1)}, u32[]{:S(2)}, u32[]{:S(2)}) collective-permute-start(bf16[64,128]{1,0:T(8,128)(2,1)S(1)} %pad_maximum_fusion.1), channel_id=1, source_target_pairs={{0,24},{1,25},{2,26},{3,27},{4,28},{5,29},{6,30},{7,31},{8,0},{9,1... | collective-permute-start | bytes 49160 | tf_op jit(solution)/shard_map/ppermute | solution.py:42
  113.1 2.4 %copy-start.1 = (bf16[19008,128]{1,0:T(8,128)(2,1)S(1)}, bf16[19008,128]{1,0:T(8,128)(2,1)}, u32[]{:S(2)}) copy-start(bf16[19008,128]{1,0:T(8,128)(2,1)} %pick_couplings.1.kp_ref.picked) | copy-start | bytes 14598148
  115.5 1.0 copy-start.12
  116.5 0.9 copy-start.13
  117.4 1.5 %copy-start.3 = (bf16[2240,128]{1,0:T(8,128)(2,1)S(1)}, bf16[2240,128]{1,0:T(8,128)(2,1)}, u32[]{:S(2)}) copy-start(bf16[2240,128]{1,0:T(8,128)(2,1)} %copy-done.2) | copy-start | bytes 1720324
  117.4 1.5 %copy-start.7 = (bf16[2240,128]{1,0:T(8,128)(2,1)S(1)}, bf16[2240,128]{1,0:T(8,128)(2,1)}, u32[]{:S(2)}) copy-start(bf16[2240,128]{1,0:T(8,128)(2,1)} %copy-done.6) | copy-start | bytes 1720324
  117.4 1.6 %copy-start.8 = (bf16[64,128,64]{1,2,0:T(8,128)(2,1)S(1)}, bf16[64,128,64]{1,2,0:T(8,128)(2,1)}, u32[]{:S(2)}) copy-start(bf16[64,128,64]{1,2,0:T(8,128)(2,1)} %param.23) | copy-start | bytes 3145732

commit v2 on v1

v2 whole, which is shorter than its diff:
```python
import functools

import jax
import jax.numpy as jnp
from jax import lax
from jax.experimental import pallas as pl
from jax.experimental.pallas import tpu as pltpu
from jax.sharding import PartitionSpec as P

AXES = ("leaf", "sub")
DEVICES = 128
RANK = 64
PANEL = 128
LEAVES = 64
FAR = 8
NEAR = 6
HALO = 32
OFFSETS = 21
SLOTS = 48
TYPES = 316
HALF = 32
TYPE_ROWS = 328
VMEM = 60 << 20
TERM_ROW = 512
TABLE_ROW = 528
BLOCK = 560
NT = (((1,), (1,)), ((), ()))


def dot(a, b):
    return jnp.dot(a, b, preferred_element_type=jnp.float32)


def dot_nt(a, b):
    return lax.dot_general(a, b, NT, preferred_element_type=jnp.float32)


def lane_index(rows):
    return lax.broadcasted_iota(jnp.int32, (rows, 128), 1)


def place():
    group, sub = lax.axis_index("leaf"), lax.axis_index("sub")
    return group, sub


def moved(value, pairs):
    return lax.ppermute(value, AXES, pairs)


def line_shift(steps):
    return [(s, s + steps) for s in range(max(0, -steps), min(DEVICES, DEVICES - steps))]


def x_shift(d):
    return [(p, (p & ~3) | ((p + d) & 3)) for p in range(DEVICES)]


def z_shift(d):
    return [(p, (p & ~24) | ((p + 8 * d) & 24)) for p in range(DEVICES)]


def y_shift(d):
    return [(p, (p + 32 * d) % DEVICES) for p in range(DEVICES)]


CORE_SWAP = [(p, p ^ 4) for p in range(DEVICES)]


def two_blocks_away(near_edge, steps):
    pairs = []
    for e in range(DEVICES):
        i = e % 8
        if i < near_edge and e >= steps:
            pairs.append((e - steps, e))
        if i >= 8 - near_edge and e + steps < DEVICES:
            pairs.append((e + steps, e))
    return pairs


def up_kernel(x_ref, cb_ref, ul_ref, un_ref, ug_ref, table_ref, out_ref, mid_ref, lines):
    step = pl.program_id(0)
    nodes = un_ref.shape[0]
    quarter = lane_index(16) // HALF

    @pl.when(step == 0)
    def _():
        mid_ref[...] = jnp.zeros_like(mid_ref)

    mid = mid_ref[...]
    for n in range(nodes):
        node = jnp.zeros((16, RANK), jnp.float32)
        for b in range(2):
            four = range(n * 8 + b * 4, n * 8 + b * 4 + 4)
            x = jnp.concatenate([x_ref[:, t * PANEL : (t + 1) * PANEL] for t in four], axis=0)
            halves = []
            for q in range(2):
                rows = slice(q * HALF, (q + 1) * HALF)
                got = dot_nt(x, jnp.concatenate([cb_ref[t, rows, :] for t in four], axis=0))
                block = got[:16]
                for a in range(1, 4):
                    block = jnp.where(quarter == a, got[a * 16 : (a + 1) * 16], block)
                block = block.astype(jnp.bfloat16)
                halves.append(block)
                node = node + dot(block, jnp.concatenate([ul_ref[t, rows, :] for t in four], axis=0))
            row = pl.multiple_of(step * (nodes * 64) + (n * 2 + b) * 32, 32)
            out_ref[pl.ds(row, 32), :] = jnp.concatenate(halves, axis=0)
        mid = mid + dot(node.astype(jnp.bfloat16), un_ref[n])
    mid_ref[...] = mid

    @pl.when(step == pl.num_programs(0) - 1)
    def _():
        term = dot(mid.astype(jnp.bfloat16), ug_ref[...])
        high = term.astype(jnp.bfloat16).astype(jnp.float32)
        parts = jnp.concatenate([high, term - high], axis=1)
        out_ref[TERM_ROW : TERM_ROW + 16, :] = parts.astype(jnp.bfloat16)
        lines[...] = jnp.zeros_like(lines)
        for j in range(OFFSETS):
            lines[j : j + 1, :SLOTS] = table_ref[j].astype(jnp.float32)
        out_ref[TABLE_ROW:BLOCK, :] = lines[...].astype(jnp.bfloat16)


def up_sweep(loads, col_basis, up_leaf, up_node, up_group, table):
    steps = 2
    return pl.pallas_call(
        up_kernel,
        grid=(steps,),
        in_specs=[
            pl.BlockSpec((16, 8192 // steps), lambda i: (0, i)),
            pl.BlockSpec((LEAVES // steps, RANK, PANEL), lambda i: (i, 0, 0)),
            pl.BlockSpec((LEAVES // steps, RANK, RANK), lambda i: (i, 0, 0)),
            pl.BlockSpec((8 // steps, RANK, RANK), lambda i: (i, 0, 0)),
            pl.BlockSpec((RANK, RANK), lambda i: (0, 0)),
            pl.BlockSpec((OFFSETS, 1, SLOTS), lambda i: (0, 0, 0)),
        ],
        out_specs=pl.BlockSpec((BLOCK, 128), lambda i: (0, 0)),
        out_shape=jax.ShapeDtypeStruct((BLOCK, 128), jnp.bfloat16),
        scratch_shapes=[pltpu.VMEM((16, RANK), jnp.float32), pltpu.VMEM((32, 128), jnp.float32)],
        compiler_params=pltpu.CompilerParams(vmem_limit_bytes=VMEM),
        cost_estimate=pl.CostEstimate(flops=40_000_000, bytes_accessed=2_600_000, transcendentals=0),
        name="up_sweep",
    )(loads, col_basis, up_leaf, up_node, up_group, table)


def turn_kernel(k_ref, out_ref, table):
    step = pl.program_id(0)
    per_step = k_ref.shape[1] // RANK
    for r in range(per_step):
        rows = slice(r * RANK, (r + 1) * RANK)
        both = jnp.concatenate([k_ref[0, rows, :], k_ref[1, rows, :]], axis=0).astype(jnp.float32)
        row = pl.multiple_of((step * per_step + r) * TYPE_ROWS, 8)
        table[pl.ds(row, TYPES), :] = both.T

    @pl.when(step == pl.num_programs(0) - 1)
    def _():
        @pl.loop(0, TYPES // 4)
        def _(i):
            for u in range(4):
                t = i * 4 + u
                matrix = table[pl.ds(t, HALF, stride=TYPE_ROWS), :].astype(jnp.bfloat16)
                out_ref[pl.ds(pl.multiple_of(t * HALF, HALF), HALF), :] = matrix


def turned_couplings(coupling):
    steps = 4
    rows = TYPES * HALF
    return pl.pallas_call(
        turn_kernel,
        grid=(steps,),
        in_specs=[pl.BlockSpec((2, HALF * RANK // steps, TYPES), lambda i: (0, i, 0))],
        out_specs=pl.BlockSpec((rows, 128), lambda i: (0, 0)),
        out_shape=jax.ShapeDtypeStruct((rows, 128), jnp.bfloat16),
        scratch_shapes=[pltpu.VMEM((HALF * TYPE_ROWS, 128), jnp.float32)],
        compiler_params=pltpu.CompilerParams(vmem_limit_bytes=VMEM),
        cost_estimate=pl.CostEstimate(flops=0, bytes_accessed=20_000_000, transcendentals=0),
        name="turn_couplings",
    )(coupling)


def near_kernel(first, per_step, src, low_ref, own_ref, high_ref, blocks_ref, out_ref, all_x):
    step = pl.program_id(0)

    @pl.when(step == 0)
    def _():
        all_x[:, : HALO * PANEL] = low_ref[...]
        all_x[:, HALO * PANEL : (HALO + LEAVES) * PANEL] = own_ref[...]
        all_x[:, (HALO + LEAVES) * PANEL :] = high_ref[...]

    group, sub = place()
    start = (group * 4 + sub) * LEAVES - HALO
    for t in range(per_step):
        x = []
        for k in range(NEAR):
            i = src[k, first + step * per_step + t] - start
            x.append(all_x[:, pl.ds(pl.multiple_of(i * PANEL, PANEL), PANEL)])
        blocks = jnp.concatenate([blocks_ref[t, k] for k in range(NEAR)], axis=1)
        out_ref[:, t * PANEL : (t + 1) * PANEL] = dot_nt(jnp.concatenate(x, axis=1), blocks)


def near_field(src, low, own, high, blocks, first, count):
    per_step = 16
    smem = pl.BlockSpec(memory_space=pltpu.SMEM)
    begin = first // per_step
    return pl.pallas_call(
        functools.partial(near_kernel, first, per_step),
        grid=(count // per_step,),
        in_specs=[
            smem,
            pl.BlockSpec(low.shape, lambda i: (0, 0)),
            pl.BlockSpec(own.shape, lambda i: (0, 0)),
            pl.BlockSpec(high.shape, lambda i: (0, 0)),
            pl.BlockSpec((per_step, NEAR, PANEL, PANEL), lambda i: (begin + i, 0, 0, 0)),
        ],
        out_specs=pl.BlockSpec((16, per_step * PANEL), lambda i: (0, i)),
        out_shape=jax.ShapeDtypeStruct((16, count * PANEL), jnp.float32),
        scratch_shapes=[pltpu.VMEM((16, (2 * HALO + LEAVES) * PANEL), jnp.bfloat16)],
        compiler_params=pltpu.CompilerParams(vmem_limit_bytes=VMEM),
        cost_estimate=pl.CostEstimate(flops=count * 3_200_000, bytes_accessed=count * 300_000, transcendentals=0),
        name="near_field",
    )(src, low, own, high, blocks)


def group_sum_kernel(own_ref, other_ref, out_ref):
    def total(ref):
        parts = [ref[d].astype(jnp.float32) for d in range(4)]
        both = (parts[0] + parts[1]) + (parts[2] + parts[3])
        return (both + pltpu.roll(both, RANK, 1)).astype(jnp.bfloat16)

    own, other = total(own_ref), total(other_ref)
    left = lane_index(16) < RANK
    first_core = jnp.full((16, 128), place()[0] & 1, jnp.int32) == 0
    out_ref[...] = jnp.where(left == first_core, own, other)


def group_sums(own, other):
    terms = pl.BlockSpec((4, 16, 128), lambda i: (0, TERM_ROW // 16, 0))
    return pl.pallas_call(
        group_sum_kernel,
        grid=(1,),
        in_specs=[terms, terms],
        out_specs=pl.BlockSpec((16, 128), lambda i: (0, 0)),
        out_shape=jax.ShapeDtypeStruct((16, 128), jnp.bfloat16),
        compiler_params=pltpu.CompilerParams(vmem_limit_bytes=VMEM),
        name="group_sums",
    )(own, other)


def down_kernel(
    far_src, far_type, top_src, top_type, c0, c1, c2, c3, ut_ref, dt_ref, turned_ref, dg_ref, dn_ref, out_ref,
    groups, tops,
):
    group, _ = place()
    y, z, parent = group >> 3, (group >> 1) & 3, group >> 2
    for j, ref in enumerate((c0, c1, c2, c3)):
        groups[j * 64 : (j + 1) * 64, :] = ref[...]

    def block(yy, zz):
        at = ((z - zz) & 3) * 4 + ((y - yy) & 3)
        return groups[pl.ds(pl.multiple_of(at * 16, 16), 16), :]

    def coupling(kind):
        return turned_ref[pl.ds(pl.multiple_of(kind * HALF, HALF), HALF), :]

    def folded(total):
        return (total[:16] + pltpu.roll(total[16:], RANK, 1))[:, :RANK]

    for h in range(8):
        yy, zz = h // 2, 2 * (h % 2)
        four = jnp.concatenate([block(yy, zz), block(yy, zz + 1)], axis=1)
        top = dot(four, ut_ref[h])
        tops[h] = jnp.concatenate([top[:, :HALF], top[:, HALF:]], axis=0).astype(jnp.bfloat16)
    by_group = jnp.zeros((32, 128), jnp.float32)
    by_top = jnp.zeros((32, 128), jnp.float32)
    for k in range(FAR):
        g = far_src[0, k]
        pair = block(g >> 3, (g >> 1) & 3).astype(jnp.float32)
        turn = (g & 1) * RANK
        halves = [pltpu.roll(pair, turn, 1)[:, :HALF], pltpu.roll(pair, turn + 3 * HALF, 1)[:, :HALF]]
        by_group = by_group + dot(jnp.concatenate(halves, axis=0).astype(jnp.bfloat16), coupling(far_type[0, k]))
        by_top = by_top + dot(tops[top_src[parent, k]], coupling(top_type[parent, k]))
    top_local = folded(by_top).astype(jnp.bfloat16)
    group_local = (folded(by_group) + dot(top_local, dt_ref[group])).astype(jnp.bfloat16)
    mid_local = dot(group_local, dg_ref[...]).astype(jnp.bfloat16)
    for n in range(8):
        out_ref[n * 16 : (n + 1) * 16, :] = dot(mid_local, dn_ref[n]).astype(jnp.bfloat16)


def down_sweep(far_src, far_type, top_src, top_type, columns, up_top, down_top, turned, down_group, down_node):
    smem = pl.BlockSpec(memory_space=pltpu.SMEM)
    vmem = pl.BlockSpec(memory_space=pltpu.VMEM)
    return pl.pallas_call(
        down_kernel,
        in_specs=[smem] * 4 + [vmem] * 9,
        out_specs=vmem,
        out_shape=jax.ShapeDtypeStruct((128, RANK), jnp.bfloat16),
        scratch_shapes=[pltpu.VMEM((256, 128), jnp.bfloat16), pltpu.VMEM((8, 32, HALF), jnp.bfloat16)],
        compiler_params=pltpu.CompilerParams(vmem_limit_bytes=VMEM),
        cost_estimate=pl.CostEstimate(flops=20_000_000, bytes_accessed=5_000_000, transcendentals=0),
        name="down_sweep",
    )(far_src, far_type, top_src, top_type, *columns, up_top, down_top, turned, down_group, down_node)


def far_kernel(
    slot_ref, type_ref, g0, g1, z0, z1, z2, z3, e0, e1, turned_hbm, rows_hbm, down_hbm, near0, near1, node_ref,
    out_ref, table, turned, rows_buf, down_buf, near_buf, found, scalars, sems, scalar_sem,
):
    copies = []
    for j, ref in enumerate((g0, g1, z0, z1, z2, z3)):
        copies.append((ref, table.at[pl.ds(j * 4 * BLOCK, 4 * BLOCK), :]))
    for j, ref in enumerate((e0, e1)):
        copies.append((ref, table.at[pl.ds((24 + j) * BLOCK, BLOCK), :]))
    copies += [(turned_hbm, turned), (down_hbm, down_buf), (rows_hbm, rows_buf)]
    copies += [(near0, near_buf.at[0]), (near1, near_buf.at[1])]
    copies = [pltpu.make_async_copy(source, target, sems.at[j]) for j, (source, target) in enumerate(copies)]
    for c in copies:
        c.start()

    group, x = place()
    core = group & 1
    i_in_block = core * 4 + x

    def slot_of(offset):
        at = i_in_block + offset
        away = at >> 3
        d = (x - at) & 3
        same = jnp.where(((at >> 2) & 1) == core, 0, 4)
        base = jnp.where(away == 0, 0, jnp.where(away < 0, 8, 16))
        inside = base + same + d
        far = jnp.where((offset == 10) | (offset == -10), 24, 25)
        return jnp.where((away > 1) | (away < -1), far, inside)

    found[...] = jnp.zeros_like(found)
    found[:, :LEAVES] = slot_ref[...]
    slots = found[...]
    j_of = (slots * 1366) >> 16
    c_of = slots - j_of * SLOTS
    row_of = slot_of(j_of - 10) * BLOCK
    for c in copies[:8]:
        c.wait()
    leaf = jnp.zeros_like(slots)
    for j in range(OFFSETS):
        row = slot_of(jnp.int32(j - 10)) * BLOCK + TABLE_ROW + (j // 16) * 16
        rows = table[pl.ds(pl.multiple_of(row, 16), 16), :].astype(jnp.float32)
        line = jnp.broadcast_to(rows[j % 16 : j % 16 + 1, :], (8, 128)).astype(jnp.int32)
        here = jnp.take_along_axis(line, c_of, axis=1)
        leaf = jnp.where(j_of == j, here, leaf)
    leaf = leaf & (LEAVES - 1)
    found[...] = (row_of + (leaf >> 2) * 32) * 4 + (leaf & 3)
    to_scalars = pltpu.make_async_copy(found, scalars, scalar_sem)
    to_scalars.start()
    for c in copies[8:]:
        c.wait()
    to_scalars.wait()

    quarter = lane_index(32) // HALF

    def source(k, t):
        code = scalars[k, t]
        block = table[pl.ds(pl.multiple_of(code >> 2, 32), 32), :].astype(jnp.float32)
        return pltpu.roll(block, (((k & 3) - code) & 3) * HALF, 1)

    def left_side(t):
        parts = []
        for m in range(2):
            part = source(4 * m, t)
            for a in range(1, 4):
                part = jnp.where(quarter == a, source(4 * m + a, t), part)
            parts.append(part.astype(jnp.bfloat16))
        return jnp.concatenate(parts, axis=1)

    def right_side(t):
        return jnp.concatenate(
            [turned[pl.ds(pl.multiple_of(type_ref[k, t] * HALF, HALF), HALF), :] for k in range(FAR)], axis=0
        )

    for j in range(2):

        @pl.loop(0, LEAVES // 2, step=16)
        def _(i):
            leaves = [j * (LEAVES // 2) + i + u for u in range(16)]
            lefts = [left_side(t) for t in leaves]
            both = [dot(x, right_side(t)) for x, t in zip(lefts, leaves)]
            nodes = [node_ref[pl.ds(pl.multiple_of((t >> 3) * 16, 16), 16), :] for t in leaves[::8]]
            inherited = [dot(nodes[u // 8], down_buf[t]) for u, t in enumerate(leaves)]
            total = [(p[:16] + pltpu.roll(p[16:], RANK, 1))[:, :RANK] + q for p, q in zip(both, inherited)]
            out = [dot(p.astype(jnp.bfloat16), rows_buf[t]) for p, t in zip(total, leaves)]
            near = near_buf[j, :, pl.ds(pl.multiple_of(i * PANEL, 16 * PANEL), 16 * PANEL)]
            at = pl.multiple_of(leaves[0] * PANEL, 16 * PANEL)
            out_ref[:, pl.ds(at, 16 * PANEL)] = jnp.concatenate(out, axis=1) + near


def far_field(slots, types, pieces, extras, turned, row_basis, down_leaf, near, node_local):
    smem = pl.BlockSpec(memory_space=pltpu.SMEM)
    vmem = pl.BlockSpec(memory_space=pltpu.VMEM)
    hbm = pl.BlockSpec(memory_space=pl.ANY)
    return pl.pallas_call(
        far_kernel,
        in_specs=[vmem, smem] + [hbm] * 13 + [vmem],
        out_specs=vmem,
        out_shape=jax.ShapeDtypeStruct((16, LEAVES * PANEL), jnp.float32),
        scratch_shapes=[
            pltpu.VMEM((26 * BLOCK, 128), jnp.bfloat16),
            pltpu.VMEM((TYPES * HALF, 128), jnp.bfloat16),
            pltpu.VMEM((LEAVES, RANK, PANEL), jnp.bfloat16),
            pltpu.VMEM((LEAVES, RANK, RANK), jnp.bfloat16),
            pltpu.VMEM((2, 16, LEAVES // 2 * PANEL), jnp.float32),
            pltpu.VMEM((8, 128), jnp.int32),
            pltpu.SMEM((8, 128), jnp.int32),
            pltpu.SemaphoreType.DMA((13,)),
            pltpu.SemaphoreType.DMA,
        ],
        compiler_params=pltpu.CompilerParams(vmem_limit_bytes=VMEM),
        cost_estimate=pl.CostEstimate(flops=300_000_000, bytes_accessed=11_000_000, transcendentals=0),
        name="far_field",
    )(slots, types, *pieces, *extras, turned, row_basis, down_leaf, *near, node_local)


def per_device(
    loads,
    col_basis,
    row_basis,
    near_blocks,
    near_src,
    up_leaf,
    down_leaf,
    up_node,
    down_node,
    up_group,
    down_group,
    up_top,
    downward_top_transfer,
    coupling,
    send_table,
    distant_leaf_slot_index,
    far_leaf_type,
    far_group_src,
    far_group_type,
    far_top_src,
    far_top_type,
):
    half = HALO * PANEL
    low = moved(loads[:, half:], line_shift(1))
    high = moved(loads[:, :half], line_shift(-1))

    own = up_sweep(loads, jnp.swapaxes(col_basis, 1, 2), up_leaf, up_node, up_group[0], jnp.swapaxes(send_table, 0, 1))
    along_x = [moved(own, x_shift(d)) for d in (1, 2, 3)]
    extra = [moved(own, two_blocks_away(2, 10)), moved(own, two_blocks_away(1, 9))]
    turned = turned_couplings(jnp.transpose(coupling, (1, 2, 0)).reshape(2, HALF * RANK, TYPES))
    *along_x, low, high, turned = lax.optimization_barrier((*along_x, low, high, turned))

    mine = jnp.concatenate([own] + along_x, axis=0)
    theirs = moved(mine, CORE_SWAP)
    below = moved(mine, line_shift(8))
    above = moved(mine, line_shift(-8))
    pair = group_sums(mine.reshape(4, BLOCK, 128), theirs.reshape(4, BLOCK, 128))
    near0 = near_field(near_src.T, low, loads, high, near_blocks, 0, LEAVES // 2)
    along_y = [moved(pair, y_shift(d)) for d in (1, 2, 3)]
    *along_y, near0 = lax.optimization_barrier((*along_y, near0))
    column = jnp.concatenate([pair] + along_y, axis=0)
    along_z = [moved(column, z_shift(d)) for d in (1, 2, 3)]
    near1 = near_field(near_src.T, low, loads, high, near_blocks, LEAVES // 2, LEAVES // 2)
    *along_z, below, above, near1 = lax.optimization_barrier((*along_z, below, above, near1))
    node_local = down_sweep(
        far_group_src,
        far_group_type,
        far_top_src,
        far_top_type,
        [column] + along_z,
        up_top.reshape(8, 4 * RANK, RANK),
        downward_top_transfer,
        turned,
        down_group[0],
        down_node,
    )
    pieces = [mine, theirs, below, moved(below, CORE_SWAP), above, moved(above, CORE_SWAP)]
    return far_field(
        distant_leaf_slot_index.T,
        far_leaf_type.T,
        pieces,
        extra,
        turned,
        jnp.swapaxes(row_basis, 1, 2),
        down_leaf,
        [near0, near1],
        node_local,
    )


def solution(mesh):
    whole, split = P(), P(AXES)
    return jax.shard_map(
        per_device,
        mesh=mesh,
        in_specs=(
            P(None, AXES),
            split, split, split, split, split, split, split, split, split, split,
            whole, whole, whole,
            split, split, split,
            P("leaf"), P("leaf"),
            whole, whole,
        ),
        out_specs=P(None, AXES),
        check_vma=False,
    )
```

time: 135 us -> 87.6 us (0.65)
  the two profiles are of different devices: /device:TPU:10 before, /device:TPU:8 now
where the time goes in v2:
time: 87.6 us; the launch traced here: 87.2 us
  starting transfers between devices  40.7 us (46%)
  Pallas kernels  35.5 us (41%)
  waiting for transfers between devices  8.65 us (10%)
  local copies, waits for them, and re-layouts  1.91 us (2%)
    ppermute x18, starting transfers between devices, moved(): return lax.ppermute(value, AXES, pairs)  40.7 us
    pallas_call x1, Pallas kernels, far_field(): pl.pallas_call(far_kernel, in_specs=[vmem, smem] + [hbm] * 13 + [vmem], o...  9.66 us
    pallas_call x2, Pallas kernels, near_field(): pl.pallas_call(functools.partial(near_kernel, first, per_step), grid=(cou...  9.22 us
    ppermute x18, waiting for transfers between devices, moved(): return lax.ppermute(value, AXES, pairs)  8.65 us
    pallas_call x1, Pallas kernels, turned_couplings(): pl.pallas_call(turn_kernel, grid=(steps,), in_specs=[pl.BlockSpec((2, HAL...  6 us
    pallas_call x1, Pallas kernels, up_sweep(): pl.pallas_call(up_kernel, grid=(steps,), in_specs=[pl.BlockSpec((16, 8192...  5.61 us
    pallas_call x1, Pallas kernels, down_sweep(): pl.pallas_call(down_kernel, in_specs=[smem] * 4 + [vmem] * 9, out_specs=v...  3.65 us
    unnamed x34, local copies, waits for them, and re-layouts  1.89 us
  transfers between devices with their start and end apart: 18, of which 3 were waited for; matrix products, arithmetic and copies ran while one was open for 0% of the time, Pallas kernels for 23%

profile of v2, /device:TPU:8, one launch (start us, length us, event | category | flops | bytes accessed | tf_op | source)
XLA Modules:
  0.0 87.2 jit_solution(9359422599554513664)
XLA Ops:
  0.0 5.6 %up_sweep.1 = bf16[560,128]{1,0:T(8,128)(2,1)} custom-call(bf16[16,8192]{1,0:T(8,128)(2,1)} %own_ref.3, bf16[64,64,128]{2,1,0:T(8,128)(2,1)} %bitcast.17, bf16[64,64,64]{2,1,0:T(8,128)(2,1)} %ul_ref.1, bf16[8,64,64]{2,1,0:T(8,128)(2,1)} %un_ref.1, bf16[64,64]{1,0:T(8,128)(2,1)} %bitcast.20, s32[21,1,48]{2,1,0:T(1,128)} %bitcast.24), custom_call_target="tpu_custom_call" | custom-call | flops 40000000 | bytes 2600000 | tf_op jit(solution)/shard_map/up_sweep/pallas_call | solution.py:125
  5.6 2.8 %collective-permute-start.2 = (bf16[560,128]{1,0:T(8,128)(2,1)}, bf16[560,128]{1,0:T(8,128)(2,1)S(1)}, u32[]{:S(2)}, u32[]{:S(2)}) collective-permute-start(bf16[560,128]{1,0:T(8,128)(2,1)} %up_sweep.1), channel_id=1, source_target_pairs={{0,3},{1,0},{2,1},{3,2},{4,7},{5,4},{6,5},{7,6},{8,11},{9,8},{10,9... | collective-permute-start | bytes 430088 | tf_op jit(solution)/shard_map/ppermute | solution.py:48
  8.4 0.8 collective-permute-start.1
  9.2 0.9 %collective-permute-start = (bf16[560,128]{1,0:T(8,128)(2,1)}, bf16[560,128]{1,0:T(8,128)(2,1)S(1)}, u32[]{:S(2)}, u32[]{:S(2)}) collective-permute-start(bf16[560,128]{1,0:T(8,128)(2,1)} %up_sweep.1), channel_id=1, source_target_pairs={{0,1},{1,2},{2,3},{3,0},{4,5},{5,6},{6,7},{7,4},{8,9},{9,10},{10,1... | collective-permute-start | bytes 430088 | tf_op jit(solution)/shard_map/ppermute | solution.py:48
  10.1 0.0 copy-done.1
  10.1 6.2 %collective-permute-start.4 = (bf16[16,4096]{1,0:T(8,128)(2,1)S(1)}, bf16[16,4096]{1,0:T(8,128)(2,1)S(1)}, u32[]{:S(2)}, u32[]{:S(2)}) collective-permute-start(bf16[16,4096]{1,0:T(8,128)(2,1)S(1)} %get-tuple-element.37), channel_id=1, source_target_pairs={{1,0},{2,1},{3,2},{4,3},{5,4},{6,5},{7,6},{8,7},{9,8},{10,9},{11,1... | collective-permute-start | bytes 393224 | tf_op jit(solution)/shard_map/ppermute | solution.py:48
  16.3 1.9 %collective-permute-start.3 = (bf16[16,4096]{1,0:T(8,128)(2,1)S(1)}, bf16[16,4096]{1,0:T(8,128)(2,1)S(1)}, u32[]{:S(2)}, u32[]{:S(2)}) collective-permute-start(bf16[16,4096]{1,0:T(8,128)(2,1)S(1)} %get-tuple-element.38), channel_id=1, source_target_pairs={{0,1},{1,2},{2,3},{3,4},{4,5},{5,6},{6,7},{7,8},{8,9},{9,10},{10,1... | collective-permute-start | bytes 393224 | tf_op jit(solution)/shard_map/ppermute | solution.py:48
  18.2 0.0 copy-start.7
  18.3 6.0 %turn_couplings.1.turned_ref.turned_hbm = bf16[10112,128]{1,0:T(8,128)(2,1)} custom-call(bf16[2,2048,316]{2,1,0:T(8,128)(2,1)} %bitcast.15), custom_call_target="tpu_custom_call" | custom-call | bytes 20000000 | tf_op jit(solution)/shard_map/turn_couplings/pallas_call | solution.py:167
  24.2 0.0 collective-permute-done.4.high_ref
  24.3 2.7 %collective-permute-done.3.low_ref = bf16[16,4096]{1,0:T(8,128)(2,1)S(1)} collective-permute-done((bf16[16,4096]{1,0:T(8,128)(2,1)S(1)}, bf16[16,4096]{1,0:T(8,128)(2,1)S(1)}, u32[]{:S(2)}, u32[]{:S(2)}) %collective-permute-start.3) | collective-permute-done | bytes 131104 | tf_op jit(solution)/shard_map/ppermute | solution.py:48
  26.9 0.0 collective-permute-done.2
  26.9 0.0 collective-permute-done.1
  26.9 0.0 collective-permute-done
  26.9 0.0 copy-done.7
  27.0 0.0 copy-start
  27.0 0.1 collective-permute-start.5
  27.1 1.9 %collective-permute-start.13 = (bf16[2240,128]{1,0:T(8,128)(2,1)S(1)}, bf16[2240,128]{1,0:T(8,128)(2,1)S(1)}, u32[]{:S(2)}, u32[]{:S(2)}) collective-permute-start(bf16[2240,128]{1,0:T(8,128)(2,1)S(1)} %pad_maximum_fusion.g0), channel_id=1, source_target_pairs={{8,0},{9,1},{10,2},{11,3},{12,4},{13,5},{14,6},{15,7},{16,8},{17,9... | collective-permute-start | bytes 1720328 | tf_op jit(solution)/shard_map/ppermute | solution.py:48
  29.0 3.9 %collective-permute-start.12 = (bf16[2240,128]{1,0:T(8,128)(2,1)S(1)}, bf16[2240,128]{1,0:T(8,128)(2,1)S(1)}, u32[]{:S(2)}, u32[]{:S(2)}) collective-permute-start(bf16[2240,128]{1,0:T(8,128)(2,1)S(1)} %pad_maximum_fusion.g0), channel_id=1, source_target_pairs={{0,8},{1,9},{2,10},{3,11},{4,12},{5,13},{6,14},{7,15},{8,16},{9,17... | collective-permute-start | bytes 1720328 | tf_op jit(solution)/shard_map/ppermute | solution.py:48
  33.0 0.0 collective-permute-done.5.g1
  33.0 0.0 copy-start.2
  33.0 0.0 copy-done
  33.0 0.8 copy-done.2
  33.8 1.4 %group_sums.1 = bf16[16,128]{1,0:T(8,128)(2,1)} custom-call(bf16[4,560,128]{2,1,0:T(8,128)(2,1)} %bitcast.14, bf16[4,560,128]{2,1,0:T(8,128)(2,1)} %bitcast.16), custom_call_target="tpu_custom_call" | custom-call | tf_op jit(solution)/shard_map/group_sums/pallas_call | solution.py:237
  35.2 0.0 copy-done.8
  35.2 0.0 copy-done.9
  35.2 0.0 collective-permute-start.8
  35.2 3.0 %collective-permute-start.7 = (bf16[16,128]{1,0:T(8,128)(2,1)}, bf16[16,128]{1,0:T(8,128)(2,1)S(1)}, u32[]{:S(2)}, u32[]{:S(2)}) collective-permute-start(bf16[16,128]{1,0:T(8,128)(2,1)} %group_sums.1), channel_id=1, source_target_pairs={{0,64},{1,65},{2,66},{3,67},{4,68},{5,69},{6,70},{7,71},{8,72},{9,... | collective-permute-start | bytes 12296 | tf_op jit(solution)/shard_map/ppermute | solution.py:48
  38.2 2.2 %collective-permute-start.6 = (bf16[16,128]{1,0:T(8,128)(2,1)}, bf16[16,128]{1,0:T(8,128)(2,1)S(1)}, u32[]{:S(2)}, u32[]{:S(2)}) collective-permute-start(bf16[16,128]{1,0:T(8,128)(2,1)} %group_sums.1), channel_id=1, source_target_pairs={{0,32},{1,33},{2,34},{3,35},{4,36},{5,37},{6,38},{7,39},{8,40},{9,... | collective-permute-start | bytes 12296 | tf_op jit(solution)/shard_map/ppermute | solution.py:48
  40.4 4.6 %near_field.2.near0 = f32[16,4096]{1,0:T(8,128)} custom-call(s32[6,64]{1,0:T(8,128)} %bitcast.22, bf16[16,4096]{1,0:T(8,128)(2,1)} %copy-done.9, bf16[16,8192]{1,0:T(8,128)(2,1)} %own_ref.3, bf16[16,4096]{1,0:T(8,128)(2,1)} %copy-done.8, bf16[64,6,128,128]{3,2,1,0:T(8,128)(2,1)} %blocks_ref.3), custom_call_target="tpu_custom_call" | custom-call | flops 102400000 | bytes 9600000 | tf_op jit(solution)/shard_map/near_field/pallas_call | solution.py:204
  45.0 0.0 collective-permute-done.8
  45.0 0.4 collective-permute-done.7
  45.4 0.0 collective-permute-done.6
  45.4 0.0 copy-done.16
  45.4 0.0 copy-start.12
  45.4 3.8 %collective-permute-start.11 = (bf16[64,128]{1,0:T(8,128)(2,1)S(1)}, bf16[64,128]{1,0:T(8,128)(2,1)S(1)}, u32[]{:S(2)}, u32[]{:S(2)}) collective-permute-start(bf16[64,128]{1,0:T(8,128)(2,1)S(1)} %pad_maximum_fusion.1.c0), channel_id=1, source_target_pairs={{0,24},{1,25},{2,26},{3,27},{4,28},{5,29},{6,30},{7,31},{8,0},{9,1... | collective-permute-start | bytes 49160 | tf_op jit(solution)/shard_map/ppermute | solution.py:48
  49.2 0.0 collective-permute-start.10
  49.2 0.9 %collective-permute-start.9 = (bf16[64,128]{1,0:T(8,128)(2,1)S(1)}, bf16[64,128]{1,0:T(8,128)(2,1)S(1)}, u32[]{:S(2)}, u32[]{:S(2)}) collective-permute-start(bf16[64,128]{1,0:T(8,128)(2,1)S(1)} %pad_maximum_fusion.1.c0), channel_id=1, source_target_pairs={{0,8},{1,9},{2,10},{3,11},{4,12},{5,13},{6,14},{7,15},{8,16},{9,17... | collective-permute-start | bytes 49160 | tf_op jit(solution)/shard_map/ppermute | solution.py:48
  50.2 4.6 %near_field.3.near1 = f32[16,4096]{1,0:T(8,128)} custom-call(s32[6,64]{1,0:T(8,128)} %bitcast.23, bf16[16,4096]{1,0:T(8,128)(2,1)} %copy-done.9, bf16[16,8192]{1,0:T(8,128)(2,1)} %own_ref.3, bf16[16,4096]{1,0:T(8,128)(2,1)} %copy-done.8, bf16[64,6,128,128]{3,2,1,0:T(8,128)(2,1)} %blocks_ref.3), custom_call_target="tpu_custom_call" | custom-call | flops 102400000 | bytes 9600000 | tf_op jit(solution)/shard_map/near_field/pallas_call | solution.py:204
  54.8 0.0 copy-done.12
  54.8 0.0 collective-permute-done.13.z2
  54.8 0.0 copy-start.3
  54.8 0.0 collective-permute-done.12.z0
  54.8 0.0 copy-start.4
  54.8 0.0 collective-permute-done.11.c3
  54.8 0.0 collective-permute-done.10.c2
  54.8 0.0 copy-start.14
  54.8 0.0 collective-permute-done.9.c1
  54.9 0.1 collective-permute-start.14
  55.0 0.5 collective-permute-start.15
  55.5 9.7 %collective-permute-start.17 = (bf16[560,128]{1,0:T(8,128)(2,1)S(1)}, bf16[560,128]{1,0:T(8,128)(2,1)S(1)}, u32[]{:S(2)}, u32[]{:S(2)}) collective-permute-start(bf16[560,128]{1,0:T(8,128)(2,1)S(1)} %copy-done.7), channel_id=1, source_target_pairs={{16,7},{24,15},{7,16},{32,23},{15,24},{40,31},{23,32},{48,39},{31,... | collective-permute-start | bytes 430088 | tf_op jit(solution)/shard_map/ppermute | solution.py:48
  65.2 1.9 %collective-permute-start.16 = (bf16[560,128]{1,0:T(8,128)(2,1)S(1)}, bf16[560,128]{1,0:T(8,128)(2,1)S(1)}, u32[]{:S(2)}, u32[]{:S(2)}) collective-permute-start(bf16[560,128]{1,0:T(8,128)(2,1)S(1)} %copy-done.7), channel_id=1, source_target_pairs={{16,6},{17,7},{24,14},{25,15},{6,16},{7,17},{32,22},{33,23},{14,24... | collective-permute-start | bytes 430088 | tf_op jit(solution)/shard_map/ppermute | solution.py:48
  67.1 3.6 %down_sweep.1.node_ref = bf16[128,64]{1,0:T(8,128)(2,1)} custom-call(s32[1,8]{1,0:T(1,128)} %far_src.1, s32[1,8]{1,0:T(1,128)} %far_type.1, s32[8,8]{1,0:T(8,128)} %top_src.1, s32[8,8]{1,0:T(8,128)} %top_type.1, bf16[64,128]{1,0:T(8,128)(2,1)} %copy-done.12, bf16[64,128]{1,0:T(8,128)(2,1)} %copy-done.15, bf16[64,128]{1,0:T(8,128)(2,1)} %copy-done.14, ...), custom_call_target="tpu_custom_call" | custom-call | flops 20000000 | bytes 5000000 | tf_op jit(solution)/shard_map/down_sweep/pallas_call | solution.py:291
  70.8 0.0 copy-done.3
  70.8 0.0 collective-permute-done.17.e1
  70.8 5.6 %collective-permute-done.16.e0 = bf16[560,128]{1,0:T(8,128)(2,1)S(1)} collective-permute-done((bf16[560,128]{1,0:T(8,128)(2,1)S(1)}, bf16[560,128]{1,0:T(8,128)(2,1)S(1)}, u32[]{:S(2)}, u32[]{:S(2)}) %collective-permute-start.16) | collective-permute-done | bytes 143392 | tf_op jit(solution)/shard_map/ppermute | solution.py:48
  76.4 0.0 collective-permute-done.14.z1
  76.4 0.0 collective-permute-done.15.z3
  76.4 0.0 copy-start.6
  76.4 0.0 copy-done.10
  76.4 0.6 copy-done.11
  77.1 0.2 copy-done.5
  77.3 0.2 copy-done.6
  77.5 9.7 %far_field.1 = f32[16,8192]{1,0:T(8,128)} custom-call(s32[8,64]{1,0:T(8,128)} %bitcast.25, s32[8,64]{1,0:T(8,128)} %bitcast.26, bf16[2240,128]{1,0:T(8,128)(2,1)} %copy-done, bf16[2240,128]{1,0:T(8,128)(2,1)} %copy-done.2, bf16[2240,128]{1,0:T(8,128)(2,1)} %copy-done.4, bf16[2240,128]{1,0:T(8,128)(2,1)} %copy-done.5, bf16[2240,128]{1,0:T(8,128)(2,1)} %copy-done.3, ...), custom_call_target="tpu_custom_call" | custom-call | flops 300000000 | bytes 11000000 | tf_op jit(solution)/shard_map/far_field/pallas_call | solution.py:396
  (16 shorter events, 0.1 us)
Async XLA Ops:
  0.0 10.1 %copy-start.1 = (bf16[16,8192]{1,0:T(8,128)(2,1)S(1)}, bf16[16,8192]{1,0:T(8,128)(2,1)}, u32[]{:S(2)}) copy-start(bf16[16,8192]{1,0:T(8,128)(2,1)} %own_ref.3) | copy-start | bytes 786436
  5.6 21.3 %collective-permute-start.2 = (bf16[560,128]{1,0:T(8,128)(2,1)}, bf16[560,128]{1,0:T(8,128)(2,1)S(1)}, u32[]{:S(2)}, u32[]{:S(2)}) collective-permute-start(bf16[560,128]{1,0:T(8,128)(2,1)} %up_sweep.1), channel_id=1, source_target_pairs={{0,3},{1,0},{2,1},{3,2},{4,7},{5,4},{6,5},{7,6},{8,11},{9,8},{10,9... | collective-permute-start | bytes 430088 | tf_op jit(solution)/shard_map/ppermute | solution.py:48
  8.4 18.5 %collective-permute-start.1 = (bf16[560,128]{1,0:T(8,128)(2,1)}, bf16[560,128]{1,0:T(8,128)(2,1)S(1)}, u32[]{:S(2)}, u32[]{:S(2)}) collective-permute-start(bf16[560,128]{1,0:T(8,128)(2,1)} %up_sweep.1), channel_id=1, source_target_pairs={{0,2},{1,3},{2,0},{3,1},{4,6},{5,7},{6,4},{7,5},{8,10},{9,11},{10,... | collective-permute-start | bytes 430088 | tf_op jit(solution)/shard_map/ppermute | solution.py:48
  9.2 17.7 %collective-permute-start = (bf16[560,128]{1,0:T(8,128)(2,1)}, bf16[560,128]{1,0:T(8,128)(2,1)S(1)}, u32[]{:S(2)}, u32[]{:S(2)}) collective-permute-start(bf16[560,128]{1,0:T(8,128)(2,1)} %up_sweep.1), channel_id=1, source_target_pairs={{0,1},{1,2},{2,3},{3,0},{4,5},{5,6},{6,7},{7,4},{8,9},{9,10},{10,1... | collective-permute-start | bytes 430088 | tf_op jit(solution)/shard_map/ppermute | solution.py:48
  10.1 14.2 %collective-permute-start.4 = (bf16[16,4096]{1,0:T(8,128)(2,1)S(1)}, bf16[16,4096]{1,0:T(8,128)(2,1)S(1)}, u32[]{:S(2)}, u32[]{:S(2)}) collective-permute-start(bf16[16,4096]{1,0:T(8,128)(2,1)S(1)} %get-tuple-element.37), channel_id=1, source_target_pairs={{1,0},{2,1},{3,2},{4,3},{5,4},{6,5},{7,6},{8,7},{9,8},{10,9},{11,1... | collective-permute-start | bytes 393224 | tf_op jit(solution)/shard_map/ppermute | solution.py:48
  16.3 10.6 %collective-permute-start.3 = (bf16[16,4096]{1,0:T(8,128)(2,1)S(1)}, bf16[16,4096]{1,0:T(8,128)(2,1)S(1)}, u32[]{:S(2)}, u32[]{:S(2)}) collective-permute-start(bf16[16,4096]{1,0:T(8,128)(2,1)S(1)} %get-tuple-element.38), channel_id=1, source_target_pairs={{0,1},{1,2},{2,3},{3,4},{4,5},{5,6},{6,7},{7,8},{8,9},{9,10},{10,1... | collective-permute-start | bytes 393224 | tf_op jit(solution)/shard_map/ppermute | solution.py:48
  18.2 8.7 %copy-start.7 = (bf16[560,128]{1,0:T(8,128)(2,1)S(1)}, bf16[560,128]{1,0:T(8,128)(2,1)}, u32[]{:S(2)}) copy-start(bf16[560,128]{1,0:T(8,128)(2,1)} %up_sweep.1) | copy-start | bytes 430084
  24.3 10.9 %copy-start.8 = (bf16[16,4096]{1,0:T(8,128)(2,1)}, bf16[16,4096]{1,0:T(8,128)(2,1)S(1)}, u32[]{:S(2)}) copy-start(bf16[16,4096]{1,0:T(8,128)(2,1)S(1)} %collective-permute-done.4.high_ref) | copy-start | bytes 393220
  26.9 8.3 %copy-start.9 = (bf16[16,4096]{1,0:T(8,128)(2,1)}, bf16[16,4096]{1,0:T(8,128)(2,1)S(1)}, u32[]{:S(2)}) copy-start(bf16[16,4096]{1,0:T(8,128)(2,1)S(1)} %collective-permute-done.3.low_ref) | copy-start | bytes 393220
  27.0 6.0 %copy-start = (bf16[2240,128]{1,0:T(8,128)(2,1)}, bf16[2240,128]{1,0:T(8,128)(2,1)S(1)}, u32[]{:S(2)}) copy-start(bf16[2240,128]{1,0:T(8,128)(2,1)S(1)} %pad_maximum_fusion.g0) | copy-start | bytes 1720324
  27.0 6.0 %collective-permute-start.5 = (bf16[2240,128]{1,0:T(8,128)(2,1)S(1)}, bf16[2240,128]{1,0:T(8,128)(2,1)S(1)}, u32[]{:S(2)}, u32[]{:S(2)}) collective-permute-start(bf16[2240,128]{1,0:T(8,128)(2,1)S(1)} %pad_maximum_fusion.g0), channel_id=1, source_target_pairs={{0,4},{1,5},{2,6},{3,7},{4,0},{5,1},{6,2},{7,3},{8,12},{9,13},{10,... | collective-permute-start | bytes 1720328 | tf_op jit(solution)/shard_map/ppermute | solution.py:48
  27.1 27.7 %collective-permute-start.13 = (bf16[2240,128]{1,0:T(8,128)(2,1)S(1)}, bf16[2240,128]{1,0:T(8,128)(2,1)S(1)}, u32[]{:S(2)}, u32[]{:S(2)}) collective-permute-start(bf16[2240,128]{1,0:T(8,128)(2,1)S(1)} %pad_maximum_fusion.g0), channel_id=1, source_target_pairs={{8,0},{9,1},{10,2},{11,3},{12,4},{13,5},{14,6},{15,7},{16,8},{17,9... | collective-permute-start | bytes 1720328 | tf_op jit(solution)/shard_map/ppermute | solution.py:48
  29.0 25.8 %collective-permute-start.12 = (bf16[2240,128]{1,0:T(8,128)(2,1)S(1)}, bf16[2240,128]{1,0:T(8,128)(2,1)S(1)}, u32[]{:S(2)}, u32[]{:S(2)}) collective-permute-start(bf16[2240,128]{1,0:T(8,128)(2,1)S(1)} %pad_maximum_fusion.g0), channel_id=1, source_target_pairs={{0,8},{1,9},{2,10},{3,11},{4,12},{5,13},{6,14},{7,15},{8,16},{9,17... | collective-permute-start | bytes 1720328 | tf_op jit(solution)/shard_map/ppermute | solution.py:48
  33.0 0.8 copy-start.2
  35.2 9.8 %collective-permute-start.8 = (bf16[16,128]{1,0:T(8,128)(2,1)}, bf16[16,128]{1,0:T(8,128)(2,1)S(1)}, u32[]{:S(2)}, u32[]{:S(2)}) collective-permute-start(bf16[16,128]{1,0:T(8,128)(2,1)} %group_sums.1), channel_id=1, source_target_pairs={{0,96},{1,97},{2,98},{3,99},{4,100},{5,101},{6,102},{7,103},{8,104... | collective-permute-start | bytes 12296 | tf_op jit(solution)/shard_map/ppermute | solution.py:48
  35.2 10.2 %collective-permute-start.7 = (bf16[16,128]{1,0:T(8,128)(2,1)}, bf16[16,128]{1,0:T(8,128)(2,1)S(1)}, u32[]{:S(2)}, u32[]{:S(2)}) collective-permute-start(bf16[16,128]{1,0:T(8,128)(2,1)} %group_sums.1), channel_id=1, source_target_pairs={{0,64},{1,65},{2,66},{3,67},{4,68},{5,69},{6,70},{7,71},{8,72},{9,... | collective-permute-start | bytes 12296 | tf_op jit(solution)/shard_map/ppermute | solution.py:48
  38.2 7.2 %collective-permute-start.6 = (bf16[16,128]{1,0:T(8,128)(2,1)}, bf16[16,128]{1,0:T(8,128)(2,1)S(1)}, u32[]{:S(2)}, u32[]{:S(2)}) collective-permute-start(bf16[16,128]{1,0:T(8,128)(2,1)} %group_sums.1), channel_id=1, source_target_pairs={{0,32},{1,33},{2,34},{3,35},{4,36},{5,37},{6,38},{7,39},{8,40},{9,... | collective-permute-start | bytes 12296 | tf_op jit(solution)/shard_map/ppermute | solution.py:48
  40.4 5.0 %copy-start.16 = (bf16[16,128]{1,0:T(8,128)(2,1)S(1)}, bf16[16,128]{1,0:T(8,128)(2,1)}, u32[]{:S(2)}) copy-start(bf16[16,128]{1,0:T(8,128)(2,1)} %group_sums.1) | copy-start | bytes 12292
  45.4 9.4 %copy-start.12 = (bf16[64,128]{1,0:T(8,128)(2,1)}, bf16[64,128]{1,0:T(8,128)(2,1)S(1)}, u32[]{:S(2)}) copy-start(bf16[64,128]{1,0:T(8,128)(2,1)S(1)} %pad_maximum_fusion.1.c0) | copy-start | bytes 49156
  45.4 9.4 %collective-permute-start.11 = (bf16[64,128]{1,0:T(8,128)(2,1)S(1)}, bf16[64,128]{1,0:T(8,128)(2,1)S(1)}, u32[]{:S(2)}, u32[]{:S(2)}) collective-permute-start(bf16[64,128]{1,0:T(8,128)(2,1)S(1)} %pad_maximum_fusion.1.c0), channel_id=1, source_target_pairs={{0,24},{1,25},{2,26},{3,27},{4,28},{5,29},{6,30},{7,31},{8,0},{9,1... | collective-permute-start | bytes 49160 | tf_op jit(solution)/shard_map/ppermute | solution.py:48
  49.2 5.6 %collective-permute-start.10 = (bf16[64,128]{1,0:T(8,128)(2,1)S(1)}, bf16[64,128]{1,0:T(8,128)(2,1)S(1)}, u32[]{:S(2)}, u32[]{:S(2)}) collective-permute-start(bf16[64,128]{1,0:T(8,128)(2,1)S(1)} %pad_maximum_fusion.1.c0), channel_id=1, source_target_pairs={{0,16},{1,17},{2,18},{3,19},{4,20},{5,21},{6,22},{7,23},{8,24},{9,... | collective-permute-start | bytes 49160 | tf_op jit(solution)/shard_map/ppermute | solution.py:48
  49.2 5.6 %collective-permute-start.9 = (bf16[64,128]{1,0:T(8,128)(2,1)S(1)}, bf16[64,128]{1,0:T(8,128)(2,1)S(1)}, u32[]{:S(2)}, u32[]{:S(2)}) collective-permute-start(bf16[64,128]{1,0:T(8,128)(2,1)S(1)} %pad_maximum_fusion.1.c0), channel_id=1, source_target_pairs={{0,8},{1,9},{2,10},{3,11},{4,12},{5,13},{6,14},{7,15},{8,16},{9,17... | collective-permute-start | bytes 49160 | tf_op jit(solution)/shard_map/ppermute | solution.py:48
  54.8 16.0 %copy-start.3 = (bf16[2240,128]{1,0:T(8,128)(2,1)}, bf16[2240,128]{1,0:T(8,128)(2,1)S(1)}, u32[]{:S(2)}) copy-start(bf16[2240,128]{1,0:T(8,128)(2,1)S(1)} %collective-permute-done.13.z2) | copy-start | bytes 1720324
  54.8 16.0 %copy-start.4 = (bf16[2240,128]{1,0:T(8,128)(2,1)}, bf16[2240,128]{1,0:T(8,128)(2,1)S(1)}, u32[]{:S(2)}) copy-start(bf16[2240,128]{1,0:T(8,128)(2,1)S(1)} %collective-permute-done.12.z0) | copy-start | bytes 1720324
  54.8 12.3 %copy-start.13 = (bf16[64,128]{1,0:T(8,128)(2,1)}, bf16[64,128]{1,0:T(8,128)(2,1)S(1)}, u32[]{:S(2)}) copy-start(bf16[64,128]{1,0:T(8,128)(2,1)S(1)} %collective-permute-done.11.c3) | copy-start | bytes 49156
  54.8 12.3 %copy-start.14 = (bf16[64,128]{1,0:T(8,128)(2,1)}, bf16[64,128]{1,0:T(8,128)(2,1)S(1)}, u32[]{:S(2)}) copy-start(bf16[64,128]{1,0:T(8,128)(2,1)S(1)} %collective-permute-done.10.c2) | copy-start | bytes 49156
  54.9 12.3 %copy-start.15 = (bf16[64,128]{1,0:T(8,128)(2,1)}, bf16[64,128]{1,0:T(8,128)(2,1)S(1)}, u32[]{:S(2)}) copy-start(bf16[64,128]{1,0:T(8,128)(2,1)S(1)} %collective-permute-done.9.c1) | copy-start | bytes 49156
  54.9 21.5 %collective-permute-start.14 = (bf16[2240,128]{1,0:T(8,128)(2,1)S(1)}, bf16[2240,128]{1,0:T(8,128)(2,1)S(1)}, u32[]{:S(2)}, u32[]{:S(2)}) collective-permute-start(bf16[2240,128]{1,0:T(8,128)(2,1)S(1)} %collective-permute-done.12.z0), channel_id=1, source_target_pairs={{0,4},{1,5},{2,6},{3,7},{4,0},{5,1},{6,2},{7,3},{8,12},{9,13},{10,... | collective-permute-start | bytes 1720328 | tf_op jit(solution)/shard_map/ppermute | solution.py:48
  55.0 21.5 %collective-permute-start.15 = (bf16[2240,128]{1,0:T(8,128)(2,1)S(1)}, bf16[2240,128]{1,0:T(8,128)(2,1)S(1)}, u32[]{:S(2)}, u32[]{:S(2)}) collective-permute-start(bf16[2240,128]{1,0:T(8,128)(2,1)S(1)} %collective-permute-done.13.z2), channel_id=1, source_target_pairs={{0,4},{1,5},{2,6},{3,7},{4,0},{5,1},{6,2},{7,3},{8,12},{9,13},{10,... | collective-permute-start | bytes 1720328 | tf_op jit(solution)/shard_map/ppermute | solution.py:48
  55.5 15.3 %collective-permute-start.17 = (bf16[560,128]{1,0:T(8,128)(2,1)S(1)}, bf16[560,128]{1,0:T(8,128)(2,1)S(1)}, u32[]{:S(2)}, u32[]{:S(2)}) collective-permute-start(bf16[560,128]{1,0:T(8,128)(2,1)S(1)} %copy-done.7), channel_id=1, source_target_pairs={{16,7},{24,15},{7,16},{32,23},{15,24},{40,31},{23,32},{48,39},{31,... | collective-permute-start | bytes 430088 | tf_op jit(solution)/shard_map/ppermute | solution.py:48
  65.2 11.2 %collective-permute-start.16 = (bf16[560,128]{1,0:T(8,128)(2,1)S(1)}, bf16[560,128]{1,0:T(8,128)(2,1)S(1)}, u32[]{:S(2)}, u32[]{:S(2)}) collective-permute-start(bf16[560,128]{1,0:T(8,128)(2,1)S(1)} %copy-done.7), channel_id=1, source_target_pairs={{16,6},{17,7},{24,14},{25,15},{6,16},{7,17},{32,22},{33,23},{14,24... | collective-permute-start | bytes 430088 | tf_op jit(solution)/shard_map/ppermute | solution.py:48
  70.8 5.6 %copy-start.10 = (bf16[560,128]{1,0:T(8,128)(2,1)}, bf16[560,128]{1,0:T(8,128)(2,1)S(1)}, u32[]{:S(2)}) copy-start(bf16[560,128]{1,0:T(8,128)(2,1)S(1)} %collective-permute-done.17.e1) | copy-start | bytes 430084
  76.4 0.7 copy-start.11
  76.4 0.9 %copy-start.5 = (bf16[2240,128]{1,0:T(8,128)(2,1)}, bf16[2240,128]{1,0:T(8,128)(2,1)S(1)}, u32[]{:S(2)}) copy-start(bf16[2240,128]{1,0:T(8,128)(2,1)S(1)} %collective-permute-done.14.z1) | copy-start | bytes 1720324
  76.4 1.1 %copy-start.6 = (bf16[2240,128]{1,0:T(8,128)(2,1)}, bf16[2240,128]{1,0:T(8,128)(2,1)S(1)}, u32[]{:S(2)}) copy-start(bf16[2240,128]{1,0:T(8,128)(2,1)S(1)} %collective-permute-done.15.z3) | copy-start | bytes 1720324

commit v3 on v2

v3 whole, which is shorter than its diff:
```python
import functools

import jax
import jax.numpy as jnp
from jax import lax
from jax.experimental import pallas as pl
from jax.experimental.pallas import tpu as pltpu
from jax.sharding import PartitionSpec as P

AXES = ("leaf", "sub")
DEVICES = 128
RANK = 64
PANEL = 128
LEAVES = 64
FAR = 8
NEAR = 6
HALO = 32
OFFSETS = 21
SLOTS = 48
TYPES = 316
HALF = 32
TYPE_ROWS = 328
VMEM = 60 << 20
UP_CHUNKS = 2
TERM_ROW = 512
TABLE_ROW = 528
BLOCK = 560
NT = (((1,), (1,)), ((), ()))


def dot(a, b):
    return jnp.dot(a, b, preferred_element_type=jnp.float32)


def dot_nt(a, b):
    return lax.dot_general(a, b, NT, preferred_element_type=jnp.float32)


def lane_index(rows):
    return lax.broadcasted_iota(jnp.int32, (rows, 128), 1)


def place():
    group, sub = lax.axis_index("leaf"), lax.axis_index("sub")
    return group, sub


def moved(value, pairs):
    return lax.ppermute(value, AXES, pairs)


def flipped(bits):
    return [(p, p ^ bits) for p in range(DEVICES)]


def line_swap(step, odd):
    low = [p for p in range(DEVICES - step) if (p // step) % 2 == odd]
    return [(p, p + step) for p in low] + [(p + step, p) for p in low]


CORE_SWAP = flipped(4)


def two_blocks_away():
    pairs = []
    for p in range(DEVICES):
        x, core = p & 3, (p >> 2) & 1
        target = p + 12 if core == 1 else p - 12
        if (x < 2) == (core == 1) and 0 <= target < DEVICES:
            pairs.append((p, target))
    return pairs


def up_kernel(
    x_hbm, cb_hbm, ul_hbm, un_hbm, ug_hbm, table_ref, out_ref, halo0, halo1,
    x_ref, cb_ref, ul_ref, un_ref, ug_ref, lines, sems,
):
    quarter = lane_index(16) // HALF
    per = LEAVES // UP_CHUNKS
    first = [pltpu.make_async_copy(x_hbm, x_ref, sems.at[0])]
    chunks = []
    for j in range(UP_CHUNKS):
        part = pl.ds(j * per, per)
        chunks.append(
            [
                pltpu.make_async_copy(cb_hbm.at[part], cb_ref.at[part], sems.at[3 + j]),
                pltpu.make_async_copy(ul_hbm.at[part], ul_ref.at[part], sems.at[3 + UP_CHUNKS + j]),
            ]
        )
    last = [pltpu.make_async_copy(un_hbm, un_ref, sems.at[1]), pltpu.make_async_copy(ug_hbm, ug_ref, sems.at[2])]
    for c in first + [c for chunk in chunks for c in chunk] + last:
        c.start()
    lines[...] = jnp.zeros_like(lines)
    for j in range(OFFSETS):
        lines[j : j + 1, :SLOTS] = table_ref[j].astype(jnp.float32)
    out_ref[TABLE_ROW:BLOCK, :] = lines[...].astype(jnp.bfloat16)
    first[0].wait()
    lower, upper = x_ref[:, : HALO * PANEL], x_ref[:, HALO * PANEL :]
    odd = jnp.full(lower.shape, place()[1] & 1, jnp.int32) == 1
    halo0[...] = jnp.where(odd, lower, upper)
    halo1[...] = jnp.where(odd, upper, lower)
    nodes = []
    for j in range(UP_CHUNKS):
        for c in chunks[j]:
            c.wait()
        for n in range(j * per // 8, (j + 1) * per // 8):
            node = jnp.zeros((16, RANK), jnp.float32)
            for b in range(2):
                four = range(n * 8 + b * 4, n * 8 + b * 4 + 4)
                x = jnp.concatenate([x_ref[:, t * PANEL : (t + 1) * PANEL] for t in four], axis=0)
                halves = []
                for q in range(2):
                    rows = slice(q * HALF, (q + 1) * HALF)
                    got = dot_nt(x, jnp.concatenate([cb_ref[t, rows, :] for t in four], axis=0))
                    block = got[:16]
                    for a in range(1, 4):
                        block = jnp.where(quarter == a, got[a * 16 : (a + 1) * 16], block)
                    block = block.astype(jnp.bfloat16)
                    halves.append(block)
                    node = node + dot(block, jnp.concatenate([ul_ref[t, rows, :] for t in four], axis=0))
                row = (n * 2 + b) * 32
                out_ref[row : row + 32, :] = jnp.concatenate(halves, axis=0)
            nodes.append(node.astype(jnp.bfloat16))
    for c in last:
        c.wait()
    mid = dot(nodes[0], un_ref[0])
    for n in range(1, len(nodes)):
        mid = mid + dot(nodes[n], un_ref[n])
    term = dot(mid.astype(jnp.bfloat16), ug_ref[...])
    high = term.astype(jnp.bfloat16).astype(jnp.float32)
    parts = jnp.concatenate([high, term - high], axis=1)
    out_ref[TERM_ROW : TERM_ROW + 16, :] = parts.astype(jnp.bfloat16)


def up_sweep(loads, col_basis, up_leaf, up_node, up_group, table):
    vmem = pl.BlockSpec(memory_space=pltpu.VMEM)
    hbm = pl.BlockSpec(memory_space=pl.ANY)
    return pl.pallas_call(
        up_kernel,
        in_specs=[hbm] * 5 + [vmem],
        out_specs=[vmem] * 3,
        out_shape=[jax.ShapeDtypeStruct((BLOCK, 128), jnp.bfloat16)]
        + [jax.ShapeDtypeStruct((16, HALO * PANEL), jnp.bfloat16)] * 2,
        scratch_shapes=[
            pltpu.VMEM((16, LEAVES * PANEL), jnp.bfloat16),
            pltpu.VMEM((LEAVES, RANK, PANEL), jnp.bfloat16),
            pltpu.VMEM((LEAVES, RANK, RANK), jnp.bfloat16),
            pltpu.VMEM((8, RANK, RANK), jnp.bfloat16),
            pltpu.VMEM((RANK, RANK), jnp.bfloat16),
            pltpu.VMEM((32, 128), jnp.float32),
            pltpu.SemaphoreType.DMA((3 + 2 * UP_CHUNKS,)),
        ],
        compiler_params=pltpu.CompilerParams(vmem_limit_bytes=VMEM),
        cost_estimate=pl.CostEstimate(flops=1000, bytes_accessed=1000, transcendentals=0),
        name="up_sweep",
    )(loads, col_basis, up_leaf, up_node, up_group, table)


def turn_kernel(k_ref, out_ref, table):
    step = pl.program_id(0)
    per_step = k_ref.shape[1] // RANK
    for r in range(per_step):
        rows = slice(r * RANK, (r + 1) * RANK)
        both = jnp.concatenate([k_ref[0, rows, :], k_ref[1, rows, :]], axis=0).astype(jnp.float32)
        row = pl.multiple_of((step * per_step + r) * TYPE_ROWS, 8)
        table[pl.ds(row, TYPES), :] = both.T

    @pl.when(step == pl.num_programs(0) - 1)
    def _():
        @pl.loop(0, TYPES // 4)
        def _(i):
            for u in range(4):
                t = i * 4 + u
                matrix = table[pl.ds(t, HALF, stride=TYPE_ROWS), :].astype(jnp.bfloat16)
                out_ref[pl.ds(pl.multiple_of(t * HALF, HALF), HALF), :] = matrix


def turned_couplings(coupling):
    steps = 4
    rows = TYPES * HALF
    return pl.pallas_call(
        turn_kernel,
        grid=(steps,),
        in_specs=[pl.BlockSpec((2, HALF * RANK // steps, TYPES), lambda i: (0, i, 0))],
        out_specs=pl.BlockSpec((rows, 128), lambda i: (0, 0)),
        out_shape=jax.ShapeDtypeStruct((rows, 128), jnp.bfloat16),
        scratch_shapes=[pltpu.VMEM((HALF * TYPE_ROWS, 128), jnp.float32)],
        compiler_params=pltpu.CompilerParams(vmem_limit_bytes=16 << 20),
        cost_estimate=pl.CostEstimate(flops=1000, bytes_accessed=1000, transcendentals=0),
        name="turn_couplings",
    )(coupling)


def near_kernel(first, src, halo0, own_ref, halo1, blocks_hbm, out_ref, all_x, blocks, sems):
    chunks = sems.shape[0]
    count = blocks.shape[0]
    per = count // chunks

    def copy(j):
        return pltpu.make_async_copy(
            blocks_hbm.at[pl.ds(first + j * per, per)], blocks.at[pl.ds(j * per, per)], sems.at[j]
        )

    for j in range(chunks):
        copy(j).start()
    group, sub = place()
    one, two = halo0[...], halo1[...]
    odd = jnp.full(one.shape, sub & 1, jnp.int32) == 1
    all_x[:, : HALO * PANEL] = jnp.where(odd, one, two)
    all_x[:, HALO * PANEL : (HALO + LEAVES) * PANEL] = own_ref[...]
    all_x[:, (HALO + LEAVES) * PANEL :] = jnp.where(odd, two, one)
    start = (group * 4 + sub) * LEAVES - HALO

    @pl.loop(0, chunks)
    def _(j):
        copy(j).wait()
        out = []
        for u in range(per):
            t = j * per + u
            x = []
            for k in range(NEAR):
                i = src[k, first + t] - start
                x.append(all_x[:, pl.ds(pl.multiple_of(i * PANEL, PANEL), PANEL)])
            row = jnp.concatenate([blocks[t, k] for k in range(NEAR)], axis=1)
            out.append(dot_nt(jnp.concatenate(x, axis=1), row))
        at = pl.multiple_of(j * (per * PANEL), per * PANEL)
        out_ref[:, pl.ds(at, per * PANEL)] = jnp.concatenate(out, axis=1)


def near_field(src, halo0, own, halo1, blocks, first, count):
    chunks = 4
    vmem = pl.BlockSpec(memory_space=pltpu.VMEM)
    return pl.pallas_call(
        functools.partial(near_kernel, first),
        in_specs=[pl.BlockSpec(memory_space=pltpu.SMEM), vmem, vmem, vmem, pl.BlockSpec(memory_space=pl.ANY)],
        out_specs=vmem,
        out_shape=jax.ShapeDtypeStruct((16, count * PANEL), jnp.float32),
        scratch_shapes=[
            pltpu.VMEM((16, (2 * HALO + LEAVES) * PANEL), jnp.bfloat16),
            pltpu.VMEM((count, NEAR, PANEL, PANEL), jnp.bfloat16),
            pltpu.SemaphoreType.DMA((chunks,)),
        ],
        compiler_params=pltpu.CompilerParams(vmem_limit_bytes=60 << 20),
        cost_estimate=pl.CostEstimate(flops=1000, bytes_accessed=1000, transcendentals=0),
        name="near_field",
    )(src, halo0, own, halo1, blocks)


def join_kernel(own, x1, x2, x3, mine_ref, group_ref):
    total = jnp.zeros((16, 128), jnp.float32)
    for d, ref in enumerate((own, x1, x2, x3)):
        mine_ref[d * BLOCK : (d + 1) * BLOCK, :] = ref[...]
        total = total + ref[TERM_ROW : TERM_ROW + 16, :].astype(jnp.float32)
    group_ref[...] = (total + pltpu.roll(total, RANK, 1)).astype(jnp.bfloat16)


def joined(*blocks):
    vmem = pl.BlockSpec(memory_space=pltpu.VMEM)
    return pl.pallas_call(
        join_kernel,
        in_specs=[vmem] * 4,
        out_specs=[vmem] * 2,
        out_shape=[
            jax.ShapeDtypeStruct((4 * BLOCK, 128), jnp.bfloat16),
            jax.ShapeDtypeStruct((16, 128), jnp.bfloat16),
        ],
        compiler_params=pltpu.CompilerParams(vmem_limit_bytes=8 << 20),
        cost_estimate=pl.CostEstimate(flops=1000, bytes_accessed=1000, transcendentals=0),
        name="join_blocks",
    )(*blocks)


def down_kernel(
    far_src, far_type, top_src, top_type, c0, c1, other_core, ut_ref, dt_ref, turned_ref, dg_ref, dn_ref, out_ref,
    groups, tops, couplings, own_dt, sems,
):
    group, _ = place()
    y, z, parent = group >> 3, (group >> 1) & 3, group >> 2
    left = lax.broadcasted_iota(jnp.int32, (128, 128), 1) < RANK
    first_core = jnp.full((128, 128), group & 1, jnp.int32) == 0
    for j, ref in enumerate((c0, c1)):
        rows = slice(j * 128, (j + 1) * 128)
        groups[rows, :] = jnp.where(left == first_core, ref[...], other_core[rows, :])

    def block(yy, zz):
        at = (y ^ yy) * 4 + (z ^ zz)
        return groups[pl.ds(pl.multiple_of(at * 16, 16), 16), :]

    kinds = [far_type[0, k] for k in range(FAR)] + [top_type[parent, k] for k in range(FAR)]
    copies = [
        pltpu.make_async_copy(
            turned_ref.at[pl.ds(pl.multiple_of(kind * HALF, HALF), HALF), :],
            couplings.at[pl.ds(j * HALF, HALF), :],
            sems.at[j],
        )
        for j, kind in enumerate(kinds)
    ]
    copies.append(pltpu.make_async_copy(dt_ref.at[group], own_dt, sems.at[2 * FAR]))
    for c in copies:
        c.start()

    def coupling(j):
        return couplings[j * HALF : (j + 1) * HALF, :]

    def folded(total):
        return (total[:16] + pltpu.roll(total[16:], RANK, 1))[:, :RANK]

    for h in range(8):
        yy, zz = h // 2, 2 * (h % 2)
        four = jnp.concatenate([block(yy, zz), block(yy, zz + 1)], axis=1)
        top = dot(four, ut_ref[h])
        tops[h] = jnp.concatenate([top[:, :HALF], top[:, HALF:]], axis=0).astype(jnp.bfloat16)
    for c in copies:
        c.wait()
    by_group = jnp.zeros((32, 128), jnp.float32)
    by_top = jnp.zeros((32, 128), jnp.float32)
    for k in range(FAR):
        g = far_src[0, k]
        pair = block(g >> 3, (g >> 1) & 3).astype(jnp.float32)
        turn = (g & 1) * RANK
        halves = [pltpu.roll(pair, turn, 1)[:, :HALF], pltpu.roll(pair, turn + 3 * HALF, 1)[:, :HALF]]
        by_group = by_group + dot(jnp.concatenate(halves, axis=0).astype(jnp.bfloat16), coupling(k))
        by_top = by_top + dot(tops[top_src[parent, k]], coupling(FAR + k))
    top_local = folded(by_top).astype(jnp.bfloat16)
    group_local = (folded(by_group) + dot(top_local, own_dt[...])).astype(jnp.bfloat16)
    mid_local = dot(group_local, dg_ref[...]).astype(jnp.bfloat16)
    for n in range(8):
        out_ref[n * 16 : (n + 1) * 16, :] = dot(mid_local, dn_ref[n]).astype(jnp.bfloat16)


def down_sweep(far_src, far_type, top_src, top_type, groups, up_top, down_top, turned, down_group, down_node):
    smem = pl.BlockSpec(memory_space=pltpu.SMEM)
    vmem = pl.BlockSpec(memory_space=pltpu.VMEM)
    hbm = pl.BlockSpec(memory_space=pl.ANY)
    return pl.pallas_call(
        down_kernel,
        in_specs=[smem] * 4 + [vmem] * 4 + [hbm] * 2 + [vmem] * 2,
        out_specs=vmem,
        out_shape=jax.ShapeDtypeStruct((128, RANK), jnp.bfloat16),
        scratch_shapes=[
            pltpu.VMEM((256, 128), jnp.bfloat16),
            pltpu.VMEM((8, 32, HALF), jnp.bfloat16),
            pltpu.VMEM((2 * FAR * HALF, 128), jnp.bfloat16),
            pltpu.VMEM((RANK, RANK), jnp.bfloat16),
            pltpu.SemaphoreType.DMA((2 * FAR + 1,)),
        ],
        compiler_params=pltpu.CompilerParams(vmem_limit_bytes=8 << 20),
        cost_estimate=pl.CostEstimate(flops=1000, bytes_accessed=1000, transcendentals=0),
        name="down_sweep",
    )(far_src, far_type, top_src, top_type, *groups, up_top, down_top, turned, down_group, down_node)


def far_kernel(
    slot_ref, type_ref, g0, g1, z0, z1, z2, z3, e0, turned, rows_buf, down_buf, near0, near1, node_ref,
    out_ref, table, found, scalars, sems, scalar_sem,
):
    copies = []
    for j, ref in enumerate((g0, g1, z0, z1, z2, z3)):
        copies.append((ref, table.at[pl.ds(j * 4 * BLOCK, 4 * BLOCK), :]))
    copies.append((e0, table.at[pl.ds(24 * BLOCK, 2 * BLOCK), :]))
    copies = [pltpu.make_async_copy(source, target, sems.at[j]) for j, (source, target) in enumerate(copies)]
    for c in copies:
        c.start()

    group, x = place()
    core, block = group & 1, group >> 1
    i_in_block = core * 4 + x

    def slot_of(offset):
        at = i_in_block + offset
        away = at >> 3
        d = (x ^ at) & 3
        same = jnp.where(((at >> 2) & 1) == core, 0, 4)
        first = jnp.where((block & 1) == 0, 1, -1)
        base = jnp.where(away == 0, 0, jnp.where(away == first, 8, 16))
        inside = base + same + d
        return jnp.where((away > 1) | (away < -1), 22 + d, inside)

    found[...] = jnp.zeros_like(found)
    found[:, :LEAVES] = slot_ref[...]
    slots = found[...]
    j_of = (slots * 1366) >> 16
    c_of = slots - j_of * SLOTS
    row_of = slot_of(j_of - 10) * BLOCK
    for c in copies:
        c.wait()
    leaf = jnp.zeros_like(slots)
    for j in range(OFFSETS):
        row = slot_of(jnp.int32(j - 10)) * BLOCK + TABLE_ROW + (j // 16) * 16
        rows = table[pl.ds(pl.multiple_of(row, 16), 16), :].astype(jnp.float32)
        line = jnp.broadcast_to(rows[j % 16 : j % 16 + 1, :], (8, 128)).astype(jnp.int32)
        here = jnp.take_along_axis(line, c_of, axis=1)
        leaf = jnp.where(j_of == j, here, leaf)
    leaf = leaf & (LEAVES - 1)
    found[...] = (row_of + (leaf >> 2) * 32) * 4 + (leaf & 3)
    to_scalars = pltpu.make_async_copy(found, scalars, scalar_sem)
    to_scalars.start()
    to_scalars.wait()

    quarter = lane_index(32) // HALF

    def source(k, t):
        code = scalars[k, t]
        block = table[pl.ds(pl.multiple_of(code >> 2, 32), 32), :].astype(jnp.float32)
        return pltpu.roll(block, (((k & 3) - code) & 3) * HALF, 1)

    def left_side(t):
        parts = []
        for m in range(2):
            part = source(4 * m, t)
            for a in range(1, 4):
                part = jnp.where(quarter == a, source(4 * m + a, t), part)
            parts.append(part.astype(jnp.bfloat16))
        return jnp.concatenate(parts, axis=1)

    def right_side(t):
        return jnp.concatenate(
            [turned[pl.ds(pl.multiple_of(type_ref[k, t] * HALF, HALF), HALF), :] for k in range(FAR)], axis=0
        )

    for j, near_ref in enumerate((near0, near1)):

        @pl.loop(0, LEAVES // 2, step=16)
        def _(i):
            leaves = [j * (LEAVES // 2) + i + u for u in range(16)]
            lefts = [left_side(t) for t in leaves]
            both = [dot(x, right_side(t)) for x, t in zip(lefts, leaves)]
            nodes = [node_ref[pl.ds(pl.multiple_of((t >> 3) * 16, 16), 16), :] for t in leaves[::8]]
            inherited = [dot(nodes[u // 8], down_buf[t]) for u, t in enumerate(leaves)]
            total = [(p[:16] + pltpu.roll(p[16:], RANK, 1))[:, :RANK] + q for p, q in zip(both, inherited)]
            out = [dot(p.astype(jnp.bfloat16), rows_buf[t]) for p, t in zip(total, leaves)]
            near = near_ref[:, pl.ds(pl.multiple_of(i * PANEL, 16 * PANEL), 16 * PANEL)]
            at = pl.multiple_of(leaves[0] * PANEL, 16 * PANEL)
            out_ref[:, pl.ds(at, 16 * PANEL)] = jnp.concatenate(out, axis=1) + near


def far_field(slots, types, pieces, extra, turned, row_basis, down_leaf, near, node_local):
    smem = pl.BlockSpec(memory_space=pltpu.SMEM)
    vmem = pl.BlockSpec(memory_space=pltpu.VMEM)
    hbm = pl.BlockSpec(memory_space=pl.ANY)
    return pl.pallas_call(
        far_kernel,
        in_specs=[vmem, smem] + [hbm] * 7 + [vmem] * 6,
        out_specs=vmem,
        out_shape=jax.ShapeDtypeStruct((16, LEAVES * PANEL), jnp.float32),
        scratch_shapes=[
            pltpu.VMEM((26 * BLOCK, 128), jnp.bfloat16),
            pltpu.VMEM((8, 128), jnp.int32),
            pltpu.SMEM((8, 128), jnp.int32),
            pltpu.SemaphoreType.DMA((7,)),
            pltpu.SemaphoreType.DMA,
        ],
        compiler_params=pltpu.CompilerParams(vmem_limit_bytes=16 << 20),
        cost_estimate=pl.CostEstimate(flops=1000, bytes_accessed=1000, transcendentals=0),
        name="far_field",
    )(slots, types, *pieces, extra, turned, row_basis, down_leaf, *near, node_local)


def per_device(
    loads,
    col_basis,
    row_basis,
    near_blocks,
    near_src,
    up_leaf,
    down_leaf,
    up_node,
    down_node,
    up_group,
    down_group,
    up_top,
    downward_top_transfer,
    coupling,
    send_table,
    distant_leaf_slot_index,
    far_leaf_type,
    far_group_src,
    far_group_type,
    far_top_src,
    far_top_type,
):
    own, to_first, to_second = up_sweep(
        loads, jnp.swapaxes(col_basis, 1, 2), up_leaf, up_node, up_group[0], jnp.swapaxes(send_table, 0, 1)
    )
    along_x = {d: moved(own, flipped(d)) for d in (3, 1, 2)}
    halo0, halo1 = moved(to_first, line_swap(1, 0)), moved(to_second, line_swap(1, 1))
    x1, x2, x3, halo0, halo1, coupling = lax.optimization_barrier(
        (along_x[1], along_x[2], along_x[3], halo0, halo1, coupling)
    )
    mine, group = joined(own, x1, x2, x3)
    along_z = [moved(group, flipped(8 * d)) for d in (1, 2, 3)]
    *along_z, mine = lax.optimization_barrier((*along_z, mine))
    theirs = moved(mine, CORE_SWAP)
    extra = moved(mine[2 * BLOCK :], two_blocks_away())
    z0, z1 = moved(mine, line_swap(8, 0)), moved(mine, line_swap(8, 1))
    column = jnp.concatenate([group] + along_z)
    y1 = moved(column, flipped(32))
    theirs, halo0, halo1, coupling = lax.optimization_barrier((theirs, halo0, halo1, coupling))
    near0 = near_field(near_src.T, halo0, loads, halo1, near_blocks, 0, LEAVES // 2)
    y1, near0, halo0 = lax.optimization_barrier((y1, near0, halo0))
    column = jnp.concatenate([column, y1])
    y2 = moved(column, flipped(64))
    near1 = near_field(near_src.T, halo0, loads, halo1, near_blocks, LEAVES // 2, LEAVES // 2)
    y2, near1, coupling = lax.optimization_barrier((y2, near1, coupling))
    turned = turned_couplings(jnp.transpose(coupling, (1, 2, 0)).reshape(2, HALF * RANK, TYPES))
    y2, turned, z0, z1, extra = lax.optimization_barrier((y2, turned, z0, z1, extra))
    other_core = moved(jnp.concatenate([column, y2]), CORE_SWAP)
    swapped = [moved(z0, CORE_SWAP), moved(z1, CORE_SWAP)]
    node_local = down_sweep(
        far_group_src,
        far_group_type,
        far_top_src,
        far_top_type,
        [column, y2, other_core],
        up_top.reshape(8, 4 * RANK, RANK),
        downward_top_transfer,
        turned,
        down_group[0],
        down_node,
    )
    pieces = [mine, theirs, z0, swapped[0], z1, swapped[1]]
    return far_field(
        distant_leaf_slot_index.T,
        far_leaf_type.T,
        pieces,
        extra,
        turned,
        jnp.swapaxes(row_basis, 1, 2),
        down_leaf,
        [near0, near1],
        node_local,
    )


def solution(mesh):
    whole, split = P(), P(AXES)
    return jax.shard_map(
        per_device,
        mesh=mesh,
        in_specs=(
            P(None, AXES),
            split, split, split, split, split, split, split, split, split, split,
            whole, whole, whole,
            split, split, split,
            P("leaf"), P("leaf"),
            whole, whole,
        ),
        out_specs=P(None, AXES),
        check_vma=False,
    )
```

time: 87.6 us -> 76 us (0.87)
  the two profiles are of different devices: /device:TPU:8 before, /device:TPU:1 now
where the time goes in v3:
time: 76 us; the launch traced here: 75.7 us
  starting transfers between devices  35.7 us (47%)
  Pallas kernels  28.6 us (38%)
  waiting for transfers between devices  7.7 us (10%)
  local copies, waits for them, and re-layouts  3.28 us (4%)
    ppermute x17, starting transfers between devices, moved(): return lax.ppermute(value, AXES, pairs)  35.7 us
    pallas_call x2, Pallas kernels, near_field(): pl.pallas_call(functools.partial(near_kernel, first), in_specs=[pl.BlockS...  10.6 us
    pallas_call x1, Pallas kernels, far_field(): pl.pallas_call(far_kernel, in_specs=[vmem, smem] + [hbm] * 7 + [vmem] * 6...  8.24 us
    ppermute x17, waiting for transfers between devices, moved(): return lax.ppermute(value, AXES, pairs)  7.7 us
    pallas_call x1, Pallas kernels, up_sweep(): pl.pallas_call(up_kernel, in_specs=[hbm] * 5 + [vmem], out_specs=[vmem] *...  4.95 us
    pallas_call x1, Pallas kernels, turned_couplings(): pl.pallas_call(turn_kernel, grid=(steps,), in_specs=[pl.BlockSpec((2, HAL...  2.76 us
    unnamed x49, local copies, waits for them, and re-layouts  2.54 us
    pallas_call x1, Pallas kernels, down_sweep(): pl.pallas_call(down_kernel, in_specs=[smem] * 4 + [vmem] * 4 + [hbm] * 2...  1.99 us
  transfers between devices with their start and end apart: 17, of which 6 were waited for; matrix products, arithmetic and copies ran while one was open for 1% of the time, Pallas kernels for 20%

profile of v3, /device:TPU:1, one launch (start us, length us, event | category | flops | bytes accessed | tf_op | source)
XLA Modules:
  0.0 75.7 jit_solution(15074445840937105820)
XLA Ops:
  0.0 4.9 %up_sweep.1 = (bf16[560,128]{1,0:T(8,128)(2,1)}, bf16[16,4096]{1,0:T(8,128)(2,1)}, bf16[16,4096]{1,0:T(8,128)(2,1)}) custom-call(bf16[16,8192]{1,0:T(8,128)(2,1)} %own_ref.3, bf16[64,64,128]{2,1,0:T(8,128)(2,1)} %bitcast.18, bf16[64,64,64]{2,1,0:T(8,128)(2,1)} %ul_hbm.1, bf16[8,64,64]{2,1,0:T(8,128)(2,1)} %un_hbm.1, bf16[64,64]{1,0:T(8,128)(2,1)} %bitcast.19, ...), custom_call_target="tpu_custom_call" | custom-call | flops 1000 | bytes 1000 | tf_op jit(solution)/shard_map/up_sweep/pallas_call | solution.py:138
  5.0 3.4 %collective-permute-start.2 = (bf16[560,128]{1,0:T(8,128)(2,1)}, bf16[560,128]{1,0:T(8,128)(2,1)S(1)}, u32[]{:S(2)}, u32[]{:S(2)}) collective-permute-start(bf16[560,128]{1,0:T(8,128)(2,1)} %get-tuple-element.35.own), channel_id=1, source_target_pairs={{0,3},{1,2},{2,1},{3,0},{4,7},{5,6},{6,5},{7,4},{8,11},{9,10},{10,... | collective-permute-start | bytes 430088 | tf_op jit(solution)/shard_map/ppermute | solution.py:49
  8.3 0.5 collective-permute-start.1
  8.9 0.1 collective-permute-start
  9.0 1.3 %collective-permute-start.3 = (bf16[16,4096]{1,0:T(8,128)(2,1)}, bf16[16,4096]{1,0:T(8,128)(2,1)S(1)}, u32[]{:S(2)}, u32[]{:S(2)}) collective-permute-start(bf16[16,4096]{1,0:T(8,128)(2,1)} %get-tuple-element.36), channel_id=1, source_target_pairs={{0,1},{2,3},{4,5},{6,7},{8,9},{10,11},{12,13},{14,15},{16,17},{18,... | collective-permute-start | bytes 393224 | tf_op jit(solution)/shard_map/ppermute | solution.py:49
  10.3 5.4 %collective-permute-start.4 = (bf16[16,4096]{1,0:T(8,128)(2,1)}, bf16[16,4096]{1,0:T(8,128)(2,1)S(1)}, u32[]{:S(2)}, u32[]{:S(2)}) collective-permute-start(bf16[16,4096]{1,0:T(8,128)(2,1)} %get-tuple-element.37), channel_id=1, source_target_pairs={{1,2},{3,4},{5,6},{7,8},{9,10},{11,12},{13,14},{15,16},{17,18},{19... | collective-permute-start | bytes 393224 | tf_op jit(solution)/shard_map/ppermute | solution.py:49
  15.7 2.3 %collective-permute-done.3.halo0 = bf16[16,4096]{1,0:T(8,128)(2,1)S(1)} collective-permute-done((bf16[16,4096]{1,0:T(8,128)(2,1)}, bf16[16,4096]{1,0:T(8,128)(2,1)S(1)}, u32[]{:S(2)}, u32[]{:S(2)}) %collective-permute-start.3) | collective-permute-done | bytes 131104 | tf_op jit(solution)/shard_map/ppermute | solution.py:49
  18.0 0.6 collective-permute-done.4.halo1
  18.6 0.0 collective-permute-done.2.x3
  18.6 0.0 collective-permute-done.1.x2
  18.6 0.0 collective-permute-done.x1
  18.6 0.0 copy-start.9
  18.6 0.9 %copy-done.9 = bf16[560,128]{1,0:T(8,128)(2,1)S(1)} copy-done((bf16[560,128]{1,0:T(8,128)(2,1)S(1)}, bf16[560,128]{1,0:T(8,128)(2,1)}, u32[]{:S(2)}) %copy-start.9) | copy-done | bytes 143384
  19.6 0.1 join_blocks.1
  19.6 5.3 %collective-permute-start.7 = (bf16[16,128]{1,0:T(8,128)(2,1)S(1)}, bf16[16,128]{1,0:T(8,128)(2,1)S(1)}, u32[]{:S(2)}, u32[]{:S(2)}) collective-permute-start(bf16[16,128]{1,0:T(8,128)(2,1)S(1)} %get-tuple-element.41), channel_id=1, source_target_pairs={{0,24},{1,25},{2,26},{3,27},{4,28},{5,29},{6,30},{7,31},{8,16},{9,... | collective-permute-start | bytes 12296 | tf_op jit(solution)/shard_map/ppermute | solution.py:49
  24.9 0.0 collective-permute-start.6
  24.9 0.7 collective-permute-start.5
  25.6 0.3 collective-permute-done.7
  25.9 3.0 %collective-permute-done.6 = bf16[16,128]{1,0:T(8,128)(2,1)S(1)} collective-permute-done((bf16[16,128]{1,0:T(8,128)(2,1)S(1)}, bf16[16,128]{1,0:T(8,128)(2,1)S(1)}, u32[]{:S(2)}, u32[]{:S(2)}) %collective-permute-start.6) | collective-permute-done | bytes 4128 | tf_op jit(solution)/shard_map/ppermute | solution.py:49
  28.9 0.0 collective-permute-done.5
  28.9 2.1 %collective-permute-start.8 = (bf16[2240,128]{1,0:T(8,128)(2,1)S(1)}, bf16[2240,128]{1,0:T(8,128)(2,1)S(1)}, u32[]{:S(2)}, u32[]{:S(2)}) collective-permute-start(bf16[2240,128]{1,0:T(8,128)(2,1)S(1)} %get-tuple-element.43.g0), channel_id=1, source_target_pairs={{0,4},{1,5},{2,6},{3,7},{4,0},{5,1},{6,2},{7,3},{8,12},{9,13},{10,... | collective-permute-start | bytes 1720328 | tf_op jit(solution)/shard_map/ppermute | solution.py:49
  31.0 0.7 slice.3
  31.7 1.5 %collective-permute-start.12 = (bf16[2240,128]{1,0:T(8,128)(2,1)S(1)}, bf16[2240,128]{1,0:T(8,128)(2,1)}, u32[]{:S(2)}, u32[]{:S(2)}) collective-permute-start(bf16[2240,128]{1,0:T(8,128)(2,1)S(1)} %get-tuple-element.43.g0), channel_id=1, source_target_pairs={{8,16},{9,17},{10,18},{11,19},{12,20},{13,21},{14,22},{15,23},{24,... | collective-permute-start | bytes 1720328 | tf_op jit(solution)/shard_map/ppermute | solution.py:49
  33.2 1.9 %collective-permute-start.11 = (bf16[2240,128]{1,0:T(8,128)(2,1)S(1)}, bf16[2240,128]{1,0:T(8,128)(2,1)}, u32[]{:S(2)}, u32[]{:S(2)}) collective-permute-start(bf16[2240,128]{1,0:T(8,128)(2,1)S(1)} %get-tuple-element.43.g0), channel_id=1, source_target_pairs={{0,8},{1,9},{2,10},{3,11},{4,12},{5,13},{6,14},{7,15},{16,24},{17,... | collective-permute-start | bytes 1720328 | tf_op jit(solution)/shard_map/ppermute | solution.py:49
  35.1 1.5 %collective-permute-start.9 = (bf16[64,128]{1,0:T(8,128)(2,1)S(1)}, bf16[64,128]{1,0:T(8,128)(2,1)S(1)}, u32[]{:S(2)}, u32[]{:S(2)}) collective-permute-start(bf16[64,128]{1,0:T(8,128)(2,1)S(1)} %pad_maximum_fusion), channel_id=1, source_target_pairs={{0,32},{1,33},{2,34},{3,35},{4,36},{5,37},{6,38},{7,39},{8,40},{9,... | collective-permute-start | bytes 49160 | tf_op jit(solution)/shard_map/ppermute | solution.py:49
  36.6 5.9 %collective-permute-start.13 = (bf16[1120,128]{1,0:T(8,128)(2,1)}, bf16[1120,128]{1,0:T(8,128)(2,1)S(1)}, u32[]{:S(2)}, u32[]{:S(2)}) collective-permute-start(bf16[1120,128]{1,0:T(8,128)(2,1)} %slice.3), channel_id=1, source_target_pairs={{4,16},{5,17},{12,24},{13,25},{18,6},{19,7},{20,32},{21,33},{26,14... | collective-permute-start | bytes 860168 | tf_op jit(solution)/shard_map/ppermute | solution.py:49
  42.6 0.0 collective-permute-done.8.g1
  42.6 0.0 copy-start.5
  42.6 0.8 %copy-done.5 = bf16[2240,128]{1,0:T(8,128)(2,1)} copy-done((bf16[2240,128]{1,0:T(8,128)(2,1)}, bf16[2240,128]{1,0:T(8,128)(2,1)S(1)}, u32[]{:S(2)}) %copy-start.5) | copy-done | bytes 573464
  43.4 5.3 %near_field.2.near0 = f32[16,4096]{1,0:T(8,128)} custom-call(s32[6,64]{1,0:T(8,128)} %bitcast.20, bf16[16,4096]{1,0:T(8,128)(2,1)} %copy-done.18, bf16[16,8192]{1,0:T(8,128)(2,1)} %own_ref.3, bf16[16,4096]{1,0:T(8,128)(2,1)} %copy-done.19, bf16[64,6,128,128]{3,2,1,0:T(8,128)(2,1)} %blocks_hbm.3), custom_call_target="tpu_custom_call" | custom-call | flops 1000 | bytes 1000 | tf_op jit(solution)/shard_map/near_field/pallas_call | solution.py:233
  48.7 0.3 collective-permute-done.9
  49.1 0.6 copy-done.20
  49.7 4.5 %collective-permute-start.10 = (bf16[128,128]{1,0:T(8,128)(2,1)S(1)}, bf16[128,128]{1,0:T(8,128)(2,1)S(1)}, u32[]{:S(2)}, u32[]{:S(2)}) collective-permute-start(bf16[128,128]{1,0:T(8,128)(2,1)S(1)} %get-tuple-element.66.c0), channel_id=1, source_target_pairs={{0,64},{1,65},{2,66},{3,67},{4,68},{5,69},{6,70},{7,71},{8,72},{9,... | collective-permute-start | bytes 98312 | tf_op jit(solution)/shard_map/ppermute | solution.py:49
  54.2 5.3 %near_field.3.near1 = f32[16,4096]{1,0:T(8,128)} custom-call(s32[6,64]{1,0:T(8,128)} %bitcast.21, bf16[16,4096]{1,0:T(8,128)(2,1)} %copy-done.18, bf16[16,8192]{1,0:T(8,128)(2,1)} %own_ref.3, bf16[16,4096]{1,0:T(8,128)(2,1)} %copy-done.19, bf16[64,6,128,128]{3,2,1,0:T(8,128)(2,1)} %blocks_hbm.3), custom_call_target="tpu_custom_call" | custom-call | flops 1000 | bytes 1000 | tf_op jit(solution)/shard_map/near_field/pallas_call | solution.py:233
  59.5 0.0 copy-start.7
  59.5 0.0 copy-start.8
  59.5 0.0 copy-start.10
  59.5 0.0 copy-start.11
  59.5 0.0 copy-start.14
  59.5 0.0 copy-start.15
  59.5 0.0 copy-start.16
  59.6 0.0 copy-start.17
  59.6 0.0 collective-permute-done.10.c1
  59.6 0.0 copy-done
  59.6 2.8 %turn_couplings.1.turned_ref.turned = bf16[10112,128]{1,0:T(8,128)(2,1)S(1)} custom-call(bf16[2,2048,316]{2,1,0:T(8,128)(2,1)S(1)} %bitcast.12), custom_call_target="tpu_custom_call" | custom-call | flops 1000 | bytes 1000 | tf_op jit(solution)/shard_map/turn_couplings/pallas_call | solution.py:181
  62.4 0.0 copy-start.1
  62.4 0.0 copy-start.2
  62.4 0.0 copy-start.3
  62.4 0.0 copy-start.4
  62.4 0.0 copy-start.6
  62.4 0.0 copy-start.12
  62.4 0.0 copy-start.13
  62.4 0.0 collective-permute-done.13.e0
  62.5 0.0 collective-permute-done.12.z2
  62.5 0.0 collective-permute-done.11.z0
  62.5 1.0 %collective-permute-start.14 = (bf16[2240,128]{1,0:T(8,128)(2,1)}, bf16[2240,128]{1,0:T(8,128)(2,1)S(1)}, u32[]{:S(2)}, u32[]{:S(2)}) collective-permute-start(bf16[2240,128]{1,0:T(8,128)(2,1)} %collective-permute-done.11.z0), channel_id=1, source_target_pairs={{0,4},{1,5},{2,6},{3,7},{4,0},{5,1},{6,2},{7,3},{8,12},{9,13},{10,... | collective-permute-start | bytes 1720328 | tf_op jit(solution)/shard_map/ppermute | solution.py:49
  63.5 0.1 collective-permute-start.15
  63.6 0.5 collective-permute-start.16
  64.1 1.2 %collective-permute-done.16.other_core = bf16[256,128]{1,0:T(8,128)(2,1)S(1)} collective-permute-done((bf16[256,128]{1,0:T(8,128)(2,1)S(1)}, bf16[256,128]{1,0:T(8,128)(2,1)S(1)}, u32[]{:S(2)}, u32[]{:S(2)}) %collective-permute-start.16) | collective-permute-done | bytes 65568 | tf_op jit(solution)/shard_map/ppermute | solution.py:49
  65.3 0.0 copy-done.8
  65.4 2.0 %down_sweep.1.node_ref = bf16[128,64]{1,0:T(8,128)(2,1)S(1)} custom-call(s32[1,8]{1,0:T(1,128)S(1)} %copy-done.16, s32[1,8]{1,0:T(1,128)S(1)} %copy-done.17, s32[8,8]{1,0:T(8,128)S(1)} %copy-done.14, s32[8,8]{1,0:T(8,128)S(1)} %copy-done.15, bf16[128,128]{1,0:T(8,128)(2,1)S(1)} %get-tuple-element.66.c0, bf16[128,128]{1,0:T(8,128)(2,1)S(1)} %collective-permute-done.10.c1, ...), custom_call_target="tpu_custom_call" | custom-call | flops 1000 | bytes 1000 | tf_op jit(solution)/shard_map/down_sweep/pallas_call | solution.py:335
  67.4 0.0 collective-permute-done.14.z1
  67.4 0.0 collective-permute-done.15.z3
  67.4 8.2 %far_field.1 = f32[16,8192]{1,0:T(8,128)} custom-call(s32[8,64]{1,0:T(8,128)S(1)} %bitcast.16, s32[8,64]{1,0:T(8,128)S(1)} %bitcast.17, bf16[2240,128]{1,0:T(8,128)(2,1)S(1)} %get-tuple-element.43.g0, bf16[2240,128]{1,0:T(8,128)(2,1)S(1)} %copy-done.6, bf16[2240,128]{1,0:T(8,128)(2,1)} %collective-permute-done.11.z0, ...), custom_call_target="tpu_custom_call" | custom-call | flops 1000 | bytes 1000 | tf_op jit(solution)/shard_map/far_field/pallas_call | solution.py:441
  (29 shorter events, 0.1 us)
Async XLA Ops:
  5.0 13.6 %collective-permute-start.2 = (bf16[560,128]{1,0:T(8,128)(2,1)}, bf16[560,128]{1,0:T(8,128)(2,1)S(1)}, u32[]{:S(2)}, u32[]{:S(2)}) collective-permute-start(bf16[560,128]{1,0:T(8,128)(2,1)} %get-tuple-element.35.own), channel_id=1, source_target_pairs={{0,3},{1,2},{2,1},{3,0},{4,7},{5,6},{6,5},{7,4},{8,11},{9,10},{10,... | collective-permute-start | bytes 430088 | tf_op jit(solution)/shard_map/ppermute | solution.py:49
  8.3 10.2 %collective-permute-start.1 = (bf16[560,128]{1,0:T(8,128)(2,1)}, bf16[560,128]{1,0:T(8,128)(2,1)S(1)}, u32[]{:S(2)}, u32[]{:S(2)}) collective-permute-start(bf16[560,128]{1,0:T(8,128)(2,1)} %get-tuple-element.35.own), channel_id=1, source_target_pairs={{0,2},{1,3},{2,0},{3,1},{4,6},{5,7},{6,4},{7,5},{8,10},{9,11},{10,... | collective-permute-start | bytes 430088 | tf_op jit(solution)/shard_map/ppermute | solution.py:49
  8.9 9.7 %collective-permute-start = (bf16[560,128]{1,0:T(8,128)(2,1)}, bf16[560,128]{1,0:T(8,128)(2,1)S(1)}, u32[]{:S(2)}, u32[]{:S(2)}) collective-permute-start(bf16[560,128]{1,0:T(8,128)(2,1)} %get-tuple-element.35.own), channel_id=1, source_target_pairs={{0,1},{1,0},{2,3},{3,2},{4,5},{5,4},{6,7},{7,6},{8,9},{9,8},{10,11... | collective-permute-start | bytes 430088 | tf_op jit(solution)/shard_map/ppermute | solution.py:49
  9.0 9.0 %collective-permute-start.3 = (bf16[16,4096]{1,0:T(8,128)(2,1)}, bf16[16,4096]{1,0:T(8,128)(2,1)S(1)}, u32[]{:S(2)}, u32[]{:S(2)}) collective-permute-start(bf16[16,4096]{1,0:T(8,128)(2,1)} %get-tuple-element.36), channel_id=1, source_target_pairs={{0,1},{2,3},{4,5},{6,7},{8,9},{10,11},{12,13},{14,15},{16,17},{18,... | collective-permute-start | bytes 393224 | tf_op jit(solution)/shard_map/ppermute | solution.py:49
  10.3 8.2 %collective-permute-start.4 = (bf16[16,4096]{1,0:T(8,128)(2,1)}, bf16[16,4096]{1,0:T(8,128)(2,1)S(1)}, u32[]{:S(2)}, u32[]{:S(2)}) collective-permute-start(bf16[16,4096]{1,0:T(8,128)(2,1)} %get-tuple-element.37), channel_id=1, source_target_pairs={{1,2},{3,4},{5,6},{7,8},{9,10},{11,12},{13,14},{15,16},{17,18},{19... | collective-permute-start | bytes 393224 | tf_op jit(solution)/shard_map/ppermute | solution.py:49
  18.0 25.4 %copy-start.18 = (bf16[16,4096]{1,0:T(8,128)(2,1)}, bf16[16,4096]{1,0:T(8,128)(2,1)S(1)}, u32[]{:S(2)}) copy-start(bf16[16,4096]{1,0:T(8,128)(2,1)S(1)} %collective-permute-done.3.halo0) | copy-start | bytes 393220
  18.6 24.8 %copy-start.19 = (bf16[16,4096]{1,0:T(8,128)(2,1)}, bf16[16,4096]{1,0:T(8,128)(2,1)S(1)}, u32[]{:S(2)}) copy-start(bf16[16,4096]{1,0:T(8,128)(2,1)S(1)} %collective-permute-done.4.halo1) | copy-start | bytes 393220
  18.6 1.0 %copy-start.9 = (bf16[560,128]{1,0:T(8,128)(2,1)S(1)}, bf16[560,128]{1,0:T(8,128)(2,1)}, u32[]{:S(2)}) copy-start(bf16[560,128]{1,0:T(8,128)(2,1)} %get-tuple-element.35.own) | copy-start | bytes 430084
  19.6 6.3 %collective-permute-start.7 = (bf16[16,128]{1,0:T(8,128)(2,1)S(1)}, bf16[16,128]{1,0:T(8,128)(2,1)S(1)}, u32[]{:S(2)}, u32[]{:S(2)}) collective-permute-start(bf16[16,128]{1,0:T(8,128)(2,1)S(1)} %get-tuple-element.41), channel_id=1, source_target_pairs={{0,24},{1,25},{2,26},{3,27},{4,28},{5,29},{6,30},{7,31},{8,16},{9,... | collective-permute-start | bytes 12296 | tf_op jit(solution)/shard_map/ppermute | solution.py:49
  24.9 4.0 %collective-permute-start.6 = (bf16[16,128]{1,0:T(8,128)(2,1)S(1)}, bf16[16,128]{1,0:T(8,128)(2,1)S(1)}, u32[]{:S(2)}, u32[]{:S(2)}) collective-permute-start(bf16[16,128]{1,0:T(8,128)(2,1)S(1)} %get-tuple-element.41), channel_id=1, source_target_pairs={{0,16},{1,17},{2,18},{3,19},{4,20},{5,21},{6,22},{7,23},{8,24},{9,... | collective-permute-start | bytes 12296 | tf_op jit(solution)/shard_map/ppermute | solution.py:49
  24.9 4.0 %collective-permute-start.5 = (bf16[16,128]{1,0:T(8,128)(2,1)S(1)}, bf16[16,128]{1,0:T(8,128)(2,1)S(1)}, u32[]{:S(2)}, u32[]{:S(2)}) collective-permute-start(bf16[16,128]{1,0:T(8,128)(2,1)S(1)} %get-tuple-element.41), channel_id=1, source_target_pairs={{0,8},{1,9},{2,10},{3,11},{4,12},{5,13},{6,14},{7,15},{8,0},{9,1},... | collective-permute-start | bytes 12296 | tf_op jit(solution)/shard_map/ppermute | solution.py:49
  28.9 13.7 %collective-permute-start.8 = (bf16[2240,128]{1,0:T(8,128)(2,1)S(1)}, bf16[2240,128]{1,0:T(8,128)(2,1)S(1)}, u32[]{:S(2)}, u32[]{:S(2)}) collective-permute-start(bf16[2240,128]{1,0:T(8,128)(2,1)S(1)} %get-tuple-element.43.g0), channel_id=1, source_target_pairs={{0,4},{1,5},{2,6},{3,7},{4,0},{5,1},{6,2},{7,3},{8,12},{9,13},{10,... | collective-permute-start | bytes 1720328 | tf_op jit(solution)/shard_map/ppermute | solution.py:49
  31.7 30.7 %collective-permute-start.12 = (bf16[2240,128]{1,0:T(8,128)(2,1)S(1)}, bf16[2240,128]{1,0:T(8,128)(2,1)}, u32[]{:S(2)}, u32[]{:S(2)}) collective-permute-start(bf16[2240,128]{1,0:T(8,128)(2,1)S(1)} %get-tuple-element.43.g0), channel_id=1, source_target_pairs={{8,16},{9,17},{10,18},{11,19},{12,20},{13,21},{14,22},{15,23},{24,... | collective-permute-start | bytes 1720328 | tf_op jit(solution)/shard_map/ppermute | solution.py:49
  33.2 29.3 %collective-permute-start.11 = (bf16[2240,128]{1,0:T(8,128)(2,1)S(1)}, bf16[2240,128]{1,0:T(8,128)(2,1)}, u32[]{:S(2)}, u32[]{:S(2)}) collective-permute-start(bf16[2240,128]{1,0:T(8,128)(2,1)S(1)} %get-tuple-element.43.g0), channel_id=1, source_target_pairs={{0,8},{1,9},{2,10},{3,11},{4,12},{5,13},{6,14},{7,15},{16,24},{17,... | collective-permute-start | bytes 1720328 | tf_op jit(solution)/shard_map/ppermute | solution.py:49
  35.1 13.9 %collective-permute-start.9 = (bf16[64,128]{1,0:T(8,128)(2,1)S(1)}, bf16[64,128]{1,0:T(8,128)(2,1)S(1)}, u32[]{:S(2)}, u32[]{:S(2)}) collective-permute-start(bf16[64,128]{1,0:T(8,128)(2,1)S(1)} %pad_maximum_fusion), channel_id=1, source_target_pairs={{0,32},{1,33},{2,34},{3,35},{4,36},{5,37},{6,38},{7,39},{8,40},{9,... | collective-permute-start | bytes 49160 | tf_op jit(solution)/shard_map/ppermute | solution.py:49
  36.6 25.8 %collective-permute-start.13 = (bf16[1120,128]{1,0:T(8,128)(2,1)}, bf16[1120,128]{1,0:T(8,128)(2,1)S(1)}, u32[]{:S(2)}, u32[]{:S(2)}) collective-permute-start(bf16[1120,128]{1,0:T(8,128)(2,1)} %slice.3), channel_id=1, source_target_pairs={{4,16},{5,17},{12,24},{13,25},{18,6},{19,7},{20,32},{21,33},{26,14... | collective-permute-start | bytes 860168 | tf_op jit(solution)/shard_map/ppermute | solution.py:49
  42.6 0.8 %copy-start.5 = (bf16[2240,128]{1,0:T(8,128)(2,1)}, bf16[2240,128]{1,0:T(8,128)(2,1)S(1)}, u32[]{:S(2)}) copy-start(bf16[2240,128]{1,0:T(8,128)(2,1)S(1)} %collective-permute-done.8.g1) | copy-start | bytes 1720324
  49.1 0.6 copy-start.20
  49.7 9.9 %copy-start = (bf16[316,64,64]{0,2,1:T(8,128)(2,1)S(1)}, bf16[316,64,64]{0,2,1:T(8,128)(2,1)}, u32[]{:S(2)}) copy-start(bf16[316,64,64]{0,2,1:T(8,128)(2,1)} %param.34) | copy-start | bytes 7766020
  49.7 9.9 %collective-permute-start.10 = (bf16[128,128]{1,0:T(8,128)(2,1)S(1)}, bf16[128,128]{1,0:T(8,128)(2,1)S(1)}, u32[]{:S(2)}, u32[]{:S(2)}) collective-permute-start(bf16[128,128]{1,0:T(8,128)(2,1)S(1)} %get-tuple-element.66.c0), channel_id=1, source_target_pairs={{0,64},{1,65},{2,66},{3,67},{4,68},{5,69},{6,70},{7,71},{8,72},{9,... | collective-permute-start | bytes 98312 | tf_op jit(solution)/shard_map/ppermute | solution.py:49
  59.5 4.1 %copy-start.21 = (bf16[256,128]{1,0:T(8,128)(2,1)S(1)}, bf16[256,128]{1,0:T(8,128)(2,1)}, u32[]{:S(2)}) copy-start(bf16[256,128]{1,0:T(8,128)(2,1)} %copy-done.20) | copy-start | bytes 196612
  59.5 5.8 %copy-start.7 = (bf16[32,64,64]{2,1,0:T(8,128)(2,1)S(1)}, bf16[32,64,64]{2,1,0:T(8,128)(2,1)}, u32[]{:S(2)}) copy-start(bf16[32,64,64]{2,1,0:T(8,128)(2,1)} %param.32) | copy-start | bytes 786436
  59.5 5.8 %copy-start.8 = (bf16[32,64,64]{2,1,0:T(8,128)(2,1)S(1)}, bf16[32,64,64]{2,1,0:T(8,128)(2,1)}, u32[]{:S(2)}) copy-start(bf16[32,64,64]{2,1,0:T(8,128)(2,1)} %dt_ref.1) | copy-start | bytes 786436
  59.5 5.8 %copy-start.10 = (bf16[8,64,64]{2,1,0:T(8,128)(2,1)S(1)}, bf16[8,64,64]{2,1,0:T(8,128)(2,1)}, u32[]{:S(2)}) copy-start(bf16[8,64,64]{2,1,0:T(8,128)(2,1)} %dn_ref.1) | copy-start | bytes 196612
  59.5 5.8 %copy-start.11 = (bf16[1,64,64]{2,1,0:T(8,128)(2,1)S(1)}, bf16[1,64,64]{2,1,0:T(8,128)(2,1)}, u32[]{:S(2)}) copy-start(bf16[1,64,64]{2,1,0:T(8,128)(2,1)} %param.31) | copy-start | bytes 24580
  59.5 5.8 %copy-start.14 = (s32[8,8]{1,0:T(8,128)S(1)}, s32[8,8]{1,0:T(8,128)}, u32[]{:S(2)}) copy-start(s32[8,8]{1,0:T(8,128)} %top_src.1) | copy-start | bytes 772
  59.5 5.8 %copy-start.15 = (s32[8,8]{1,0:T(8,128)S(1)}, s32[8,8]{1,0:T(8,128)}, u32[]{:S(2)}) copy-start(s32[8,8]{1,0:T(8,128)} %top_type.1) | copy-start | bytes 772
  59.5 5.8 %copy-start.16 = (s32[1,8]{1,0:T(1,128)S(1)}, s32[1,8]{1,0:T(1,128)}, u32[]{:S(2)}) copy-start(s32[1,8]{1,0:T(1,128)} %far_src.1) | copy-start | bytes 100
  59.6 5.8 %copy-start.17 = (s32[1,8]{1,0:T(1,128)S(1)}, s32[1,8]{1,0:T(1,128)}, u32[]{:S(2)}) copy-start(s32[1,8]{1,0:T(1,128)} %far_type.1) | copy-start | bytes 100
  62.4 5.0 %copy-start.1 = (bf16[64,128,64]{1,2,0:T(8,128)(2,1)S(1)}, bf16[64,128,64]{1,2,0:T(8,128)(2,1)}, u32[]{:S(2)}) copy-start(bf16[64,128,64]{1,2,0:T(8,128)(2,1)} %param.23) | copy-start | bytes 3145732
  62.4 5.0 %copy-start.2 = (bf16[64,64,64]{2,1,0:T(8,128)(2,1)S(1)}, bf16[64,64,64]{2,1,0:T(8,128)(2,1)}, u32[]{:S(2)}) copy-start(bf16[64,64,64]{2,1,0:T(8,128)(2,1)} %down_buf.1) | copy-start | bytes 1572868
  62.4 5.0 %copy-start.3 = (f32[16,4096]{1,0:T(8,128)S(1)}, f32[16,4096]{1,0:T(8,128)}, u32[]{:S(2)}) copy-start(f32[16,4096]{1,0:T(8,128)} %near_field.2.near0) | copy-start | bytes 786436
  62.4 5.0 %copy-start.4 = (f32[16,4096]{1,0:T(8,128)S(1)}, f32[16,4096]{1,0:T(8,128)}, u32[]{:S(2)}) copy-start(f32[16,4096]{1,0:T(8,128)} %near_field.3.near1) | copy-start | bytes 786436
  62.4 5.0 %copy-start.6 = (bf16[2240,128]{1,0:T(8,128)(2,1)S(1)}, bf16[2240,128]{1,0:T(8,128)(2,1)}, u32[]{:S(2)}) copy-start(bf16[2240,128]{1,0:T(8,128)(2,1)} %copy-done.5) | copy-start | bytes 1720324
  62.4 5.0 %copy-start.12 = (s32[64,8]{0,1:T(8,128)S(1)}, s32[64,8]{0,1:T(8,128)}, u32[]{:S(2)}) copy-start(s32[64,8]{0,1:T(8,128)} %param.36) | copy-start | bytes 6148
  62.4 5.0 %copy-start.13 = (s32[64,8]{0,1:T(8,128)S(1)}, s32[64,8]{0,1:T(8,128)}, u32[]{:S(2)}) copy-start(s32[64,8]{0,1:T(8,128)} %param.37) | copy-start | bytes 6148
  62.5 4.9 %collective-permute-start.14 = (bf16[2240,128]{1,0:T(8,128)(2,1)}, bf16[2240,128]{1,0:T(8,128)(2,1)S(1)}, u32[]{:S(2)}, u32[]{:S(2)}) collective-permute-start(bf16[2240,128]{1,0:T(8,128)(2,1)} %collective-permute-done.11.z0), channel_id=1, source_target_pairs={{0,4},{1,5},{2,6},{3,7},{4,0},{5,1},{6,2},{7,3},{8,12},{9,13},{10,... | collective-permute-start | bytes 1720328 | tf_op jit(solution)/shard_map/ppermute | solution.py:49
  63.5 3.9 %collective-permute-start.15 = (bf16[2240,128]{1,0:T(8,128)(2,1)}, bf16[2240,128]{1,0:T(8,128)(2,1)S(1)}, u32[]{:S(2)}, u32[]{:S(2)}) collective-permute-start(bf16[2240,128]{1,0:T(8,128)(2,1)} %collective-permute-done.12.z2), channel_id=1, source_target_pairs={{0,4},{1,5},{2,6},{3,7},{4,0},{5,1},{6,2},{7,3},{8,12},{9,13},{10,... | collective-permute-start | bytes 1720328 | tf_op jit(solution)/shard_map/ppermute | solution.py:49
  63.6 1.7 %collective-permute-start.16 = (bf16[256,128]{1,0:T(8,128)(2,1)S(1)}, bf16[256,128]{1,0:T(8,128)(2,1)S(1)}, u32[]{:S(2)}, u32[]{:S(2)}) collective-permute-start(bf16[256,128]{1,0:T(8,128)(2,1)S(1)} %constant_dynamic-update-slice_fusion.5), channel_id=1, source_target_pairs={{0,4},{1,5},{2,6},{3,7},{4,0},{5,1},{6,2},{7,3},{8,12},{9,13},{10,... | collective-permute-start | bytes 196616 | tf_op jit(solution)/shard_map/ppermute | solution.py:49

commit v4 on v3

--- a/solution.py
+++ b/solution.py
@@ -240,16 +240,18 @@
             pltpu.VMEM((count, NEAR, PANEL, PANEL), jnp.bfloat16),
             pltpu.SemaphoreType.DMA((chunks,)),
         ],
-        compiler_params=pltpu.CompilerParams(vmem_limit_bytes=60 << 20),
+        compiler_params=pltpu.CompilerParams(vmem_limit_bytes=52 << 20),
         cost_estimate=pl.CostEstimate(flops=1000, bytes_accessed=1000, transcendentals=0),
         name="near_field",
     )(src, halo0, own, halo1, blocks)
 
 
-def join_kernel(own, x1, x2, x3, mine_ref, group_ref):
+def join_kernel(own, x1, x2, x3, mine_ref, group_ref, tail_ref):
     total = jnp.zeros((16, 128), jnp.float32)
     for d, ref in enumerate((own, x1, x2, x3)):
         mine_ref[d * BLOCK : (d + 1) * BLOCK, :] = ref[...]
+        if d >= 2:
+            tail_ref[(d - 2) * BLOCK : (d - 1) * BLOCK, :] = ref[...]
         total = total + ref[TERM_ROW : TERM_ROW + 16, :].astype(jnp.float32)
     group_ref[...] = (total + pltpu.roll(total, RANK, 1)).astype(jnp.bfloat16)
 
@@ -259,10 +261,11 @@
     return pl.pallas_call(
         join_kernel,
         in_specs=[vmem] * 4,
-        out_specs=[vmem] * 2,
+        out_specs=[vmem] * 3,
         out_shape=[
             jax.ShapeDtypeStruct((4 * BLOCK, 128), jnp.bfloat16),
             jax.ShapeDtypeStruct((16, 128), jnp.bfloat16),
+            jax.ShapeDtypeStruct((2 * BLOCK, 128), jnp.bfloat16),
         ],
         compiler_params=pltpu.CompilerParams(vmem_limit_bytes=8 << 20),
         cost_estimate=pl.CostEstimate(flops=1000, bytes_accessed=1000, transcendentals=0),
@@ -271,16 +274,18 @@
 
 
 def down_kernel(
-    far_src, far_type, top_src, top_type, c0, c1, other_core, ut_ref, dt_ref, turned_ref, dg_ref, dn_ref, out_ref,
+    far_src, far_type, top_src, top_type, c0, c1, ut_ref, dt_ref, turned_ref, dg_ref, dn_ref, out_ref,
     groups, tops, couplings, own_dt, sems,
 ):
     group, _ = place()
     y, z, parent = group >> 3, (group >> 1) & 3, group >> 2
-    left = lax.broadcasted_iota(jnp.int32, (128, 128), 1) < RANK
-    first_core = jnp.full((128, 128), group & 1, jnp.int32) == 0
-    for j, ref in enumerate((c0, c1)):
-        rows = slice(j * 128, (j + 1) * 128)
-        groups[rows, :] = jnp.where(left == first_core, ref[...], other_core[rows, :])
+    left = lax.broadcasted_iota(jnp.int32, (64, 128), 1) < RANK
+    first_core = jnp.full((64, 128), group & 1, jnp.int32) == 0
+    for j in range(4):
+        ref = (c0, c1)[j // 2]
+        at = (j % 2) * 128
+        own, other = ref[at : at + 64, :], ref[at + 64 : at + 128, :]
+        groups[j * 64 : (j + 1) * 64, :] = jnp.where(left == first_core, own, other)
 
     def block(yy, zz):
         at = (y ^ yy) * 4 + (z ^ zz)
@@ -334,7 +339,7 @@
     hbm = pl.BlockSpec(memory_space=pl.ANY)
     return pl.pallas_call(
         down_kernel,
-        in_specs=[smem] * 4 + [vmem] * 4 + [hbm] * 2 + [vmem] * 2,
+        in_specs=[smem] * 4 + [vmem] * 3 + [hbm] * 2 + [vmem] * 2,
         out_specs=vmem,
         out_shape=jax.ShapeDtypeStruct((128, RANK), jnp.bfloat16),
         scratch_shapes=[
@@ -484,34 +489,34 @@
     )
     along_x = {d: moved(own, flipped(d)) for d in (3, 1, 2)}
     halo0, halo1 = moved(to_first, line_swap(1, 0)), moved(to_second, line_swap(1, 1))
-    x1, x2, x3, halo0, halo1, coupling = lax.optimization_barrier(
-        (along_x[1], along_x[2], along_x[3], halo0, halo1, coupling)
+    turned = turned_couplings(jnp.transpose(coupling, (1, 2, 0)).reshape(2, HALF * RANK, TYPES))
+    x1, x2, x3, turned, halo0, halo1 = lax.optimization_barrier(
+        (along_x[1], along_x[2], along_x[3], turned, halo0, halo1)
     )
-    mine, group = joined(own, x1, x2, x3)
+    mine, group, tail = joined(own, x1, x2, x3)
     along_z = [moved(group, flipped(8 * d)) for d in (1, 2, 3)]
-    *along_z, mine = lax.optimization_barrier((*along_z, mine))
-    theirs = moved(mine, CORE_SWAP)
-    extra = moved(mine[2 * BLOCK :], two_blocks_away())
+    *along_z, mine, tail = lax.optimization_barrier((*along_z, mine, tail))
+    extra = [moved(tail, two_blocks_away())]
     z0, z1 = moved(mine, line_swap(8, 0)), moved(mine, line_swap(8, 1))
     column = jnp.concatenate([group] + along_z)
+    column = jnp.concatenate([column, moved(column, CORE_SWAP)])
     y1 = moved(column, flipped(32))
-    theirs, halo0, halo1, coupling = lax.optimization_barrier((theirs, halo0, halo1, coupling))
+    column, halo0, halo1 = lax.optimization_barrier((column, halo0, halo1))
     near0 = near_field(near_src.T, halo0, loads, halo1, near_blocks, 0, LEAVES // 2)
     y1, near0, halo0 = lax.optimization_barrier((y1, near0, halo0))
     column = jnp.concatenate([column, y1])
     y2 = moved(column, flipped(64))
     near1 = near_field(near_src.T, halo0, loads, halo1, near_blocks, LEAVES // 2, LEAVES // 2)
-    y2, near1, coupling = lax.optimization_barrier((y2, near1, coupling))
-    turned = turned_couplings(jnp.transpose(coupling, (1, 2, 0)).reshape(2, HALF * RANK, TYPES))
-    y2, turned, z0, z1, extra = lax.optimization_barrier((y2, turned, z0, z1, extra))
-    other_core = moved(jnp.concatenate([column, y2]), CORE_SWAP)
+    y2, near1, z0, z1, *extra = lax.optimization_barrier((y2, near1, z0, z1, *extra))
+    theirs = moved(mine, CORE_SWAP)
     swapped = [moved(z0, CORE_SWAP), moved(z1, CORE_SWAP)]
+    (extra,) = extra
     node_local = down_sweep(
         far_group_src,
         far_group_type,
         far_top_src,
         far_top_type,
-        [column, y2, other_core],
+        [column, y2],
         up_top.reshape(8, 4 * RANK, RANK),
         downward_top_transfer,
         turned,

time: 76 us -> 70.3 us (0.925)
  the two profiles are of different devices: /device:TPU:1 before, /device:TPU:7 now
where the time goes in v4:
time: 70.3 us; the launch traced here: 70 us
  starting transfers between devices  32.3 us (46%)
  Pallas kernels  25.5 us (36%)
  waiting for transfers between devices  9.85 us (14%)
  local copies, waits for them, and re-layouts  2.01 us (3%)
    ppermute x17, starting transfers between devices, moved(): return lax.ppermute(value, AXES, pairs)  32.3 us
    ppermute x17, waiting for transfers between devices, moved(): return lax.ppermute(value, AXES, pairs)  9.85 us
    pallas_call x2, Pallas kernels, near_field(): pl.pallas_call(functools.partial(near_kernel, first), in_specs=[pl.BlockS...  8.28 us
    pallas_call x1, Pallas kernels, far_field(): pl.pallas_call(far_kernel, in_specs=[vmem, smem] + [hbm] * 7 + [vmem] * 6...  7.47 us
    pallas_call x1, Pallas kernels, up_sweep(): pl.pallas_call(up_kernel, in_specs=[hbm] * 5 + [vmem], out_specs=[vmem] *...  4.95 us
    pallas_call x1, Pallas kernels, turned_couplings(): pl.pallas_call(turn_kernel, grid=(steps,), in_specs=[pl.BlockSpec((2, HAL...  2.75 us
    unnamed x37, local copies, waits for them, and re-layouts  2 us
    pallas_call x1, Pallas kernels, down_sweep(): pl.pallas_call(down_kernel, in_specs=[smem] * 4 + [vmem] * 3 + [hbm] * 2...  1.99 us
  transfers between devices with their start and end apart: 17, of which 4 were waited for; matrix products, arithmetic and copies ran while one was open for 0% of the time, Pallas kernels for 19%

profile of v4, /device:TPU:7, one launch (start us, length us, event | category | flops | bytes accessed | tf_op | source)
XLA Modules:
  0.0 70.0 jit_solution(12849926377041070168)
XLA Ops:
  0.0 4.9 %up_sweep.1 = (bf16[560,128]{1,0:T(8,128)(2,1)}, bf16[16,4096]{1,0:T(8,128)(2,1)}, bf16[16,4096]{1,0:T(8,128)(2,1)}) custom-call(bf16[16,8192]{1,0:T(8,128)(2,1)} %own_ref.3, bf16[64,64,128]{2,1,0:T(8,128)(2,1)} %bitcast.20, bf16[64,64,64]{2,1,0:T(8,128)(2,1)} %ul_hbm.1, bf16[8,64,64]{2,1,0:T(8,128)(2,1)} %un_hbm.1, bf16[64,64]{1,0:T(8,128)(2,1)} %bitcast.21, ...), custom_call_target="tpu_custom_call" | custom-call | flops 1000 | bytes 1000 | tf_op jit(solution)/shard_map/up_sweep/pallas_call | solution.py:138
  5.0 0.1 collective-permute-start.2
  5.0 2.3 %collective-permute-start.1 = (bf16[560,128]{1,0:T(8,128)(2,1)}, bf16[560,128]{1,0:T(8,128)(2,1)S(1)}, u32[]{:S(2)}, u32[]{:S(2)}) collective-permute-start(bf16[560,128]{1,0:T(8,128)(2,1)} %get-tuple-element.33.own), channel_id=1, source_target_pairs={{0,2},{1,3},{2,0},{3,1},{4,6},{5,7},{6,4},{7,5},{8,10},{9,11},{10,... | collective-permute-start | bytes 430088 | tf_op jit(solution)/shard_map/ppermute | solution.py:49
  7.4 0.9 %collective-permute-start = (bf16[560,128]{1,0:T(8,128)(2,1)}, bf16[560,128]{1,0:T(8,128)(2,1)S(1)}, u32[]{:S(2)}, u32[]{:S(2)}) collective-permute-start(bf16[560,128]{1,0:T(8,128)(2,1)} %get-tuple-element.33.own), channel_id=1, source_target_pairs={{0,1},{1,0},{2,3},{3,2},{4,5},{5,4},{6,7},{7,6},{8,9},{9,8},{10,11... | collective-permute-start | bytes 430088 | tf_op jit(solution)/shard_map/ppermute | solution.py:49
  8.3 0.5 collective-permute-start.3
  8.8 5.8 %collective-permute-start.4 = (bf16[16,4096]{1,0:T(8,128)(2,1)}, bf16[16,4096]{1,0:T(8,128)(2,1)S(1)}, u32[]{:S(2)}, u32[]{:S(2)}) collective-permute-start(bf16[16,4096]{1,0:T(8,128)(2,1)} %get-tuple-element.35), channel_id=1, source_target_pairs={{1,2},{3,4},{5,6},{7,8},{9,10},{11,12},{13,14},{15,16},{17,18},{19... | collective-permute-start | bytes 393224 | tf_op jit(solution)/shard_map/ppermute | solution.py:49
  14.6 0.0 copy-start
  14.7 1.9 %copy-done = bf16[316,64,64]{0,2,1:T(8,128)(2,1)S(1)} copy-done((bf16[316,64,64]{0,2,1:T(8,128)(2,1)S(1)}, bf16[316,64,64]{0,2,1:T(8,128)(2,1)}, u32[]{:S(2)}) %copy-start) | copy-done | bytes 2588696
  16.5 2.8 %turn_couplings.1.turned_ref.turned = bf16[10112,128]{1,0:T(8,128)(2,1)S(1)} custom-call(bf16[2,2048,316]{2,1,0:T(8,128)(2,1)S(1)} %bitcast.12), custom_call_target="tpu_custom_call" | custom-call | flops 1000 | bytes 1000 | tf_op jit(solution)/shard_map/turn_couplings/pallas_call | solution.py:181
  19.3 0.0 collective-permute-done.3.halo0
  19.3 0.0 collective-permute-done.4.halo1
  19.3 0.0 collective-permute-done.2.x3
  19.3 0.0 collective-permute-done.1.x2
  19.3 0.0 collective-permute-done.x1
  19.3 0.0 copy-done.6
  19.4 0.1 join_blocks.1
  19.5 4.0 %collective-permute-start.7 = (bf16[16,128]{1,0:T(8,128)(2,1)S(1)}, bf16[16,128]{1,0:T(8,128)(2,1)S(1)}, u32[]{:S(2)}, u32[]{:S(2)}) collective-permute-start(bf16[16,128]{1,0:T(8,128)(2,1)S(1)} %get-tuple-element.39), channel_id=1, source_target_pairs={{0,24},{1,25},{2,26},{3,27},{4,28},{5,29},{6,30},{7,31},{8,16},{9,... | collective-permute-start | bytes 12296 | tf_op jit(solution)/shard_map/ppermute | solution.py:49
  23.5 0.0 collective-permute-start.6
  23.5 0.7 collective-permute-start.5
  24.2 0.4 collective-permute-done.7
  24.6 2.9 %collective-permute-done.6 = bf16[16,128]{1,0:T(8,128)(2,1)S(1)} collective-permute-done((bf16[16,128]{1,0:T(8,128)(2,1)S(1)}, bf16[16,128]{1,0:T(8,128)(2,1)S(1)}, u32[]{:S(2)}, u32[]{:S(2)}) %collective-permute-start.6) | collective-permute-done | bytes 4128 | tf_op jit(solution)/shard_map/ppermute | solution.py:49
  27.5 0.0 collective-permute-done.5
  27.5 0.7 collective-permute-start.13
  28.2 2.4 %collective-permute-start.12 = (bf16[2240,128]{1,0:T(8,128)(2,1)S(1)}, bf16[2240,128]{1,0:T(8,128)(2,1)S(1)}, u32[]{:S(2)}, u32[]{:S(2)}) collective-permute-start(bf16[2240,128]{1,0:T(8,128)(2,1)S(1)} %get-tuple-element.42.g0), channel_id=1, source_target_pairs={{0,8},{1,9},{2,10},{3,11},{4,12},{5,13},{6,14},{7,15},{16,24},{17,... | collective-permute-start | bytes 1720328 | tf_op jit(solution)/shard_map/ppermute | solution.py:49
  30.6 1.9 %collective-permute-start.9 = (bf16[64,128]{1,0:T(8,128)(2,1)S(1)}, bf16[64,128]{1,0:T(8,128)(2,1)S(1)}, u32[]{:S(2)}, u32[]{:S(2)}) collective-permute-start(bf16[64,128]{1,0:T(8,128)(2,1)S(1)} %pad_maximum_fusion), channel_id=1, source_target_pairs={{0,4},{1,5},{2,6},{3,7},{4,0},{5,1},{6,2},{7,3},{8,12},{9,13},{10,... | collective-permute-start | bytes 49160 | tf_op jit(solution)/shard_map/ppermute | solution.py:49
  32.5 1.3 %collective-permute-start.14 = (bf16[1120,128]{1,0:T(8,128)(2,1)S(1)}, bf16[1120,128]{1,0:T(8,128)(2,1)S(1)}, u32[]{:S(2)}, u32[]{:S(2)}) collective-permute-start(bf16[1120,128]{1,0:T(8,128)(2,1)S(1)} %get-tuple-element.53), channel_id=1, source_target_pairs={{4,16},{5,17},{12,24},{13,25},{18,6},{19,7},{20,32},{21,33},{26,14... | collective-permute-start | bytes 860168 | tf_op jit(solution)/shard_map/ppermute | solution.py:49
  33.8 0.0 collective-permute-done.9
  33.8 1.4 %collective-permute-start.10 = (bf16[128,128]{1,0:T(8,128)(2,1)S(1)}, bf16[128,128]{1,0:T(8,128)(2,1)S(1)}, u32[]{:S(2)}, u32[]{:S(2)}) collective-permute-start(bf16[128,128]{1,0:T(8,128)(2,1)S(1)} %constant_dynamic-update-slice_fusion), channel_id=1, source_target_pairs={{0,32},{1,33},{2,34},{3,35},{4,36},{5,37},{6,38},{7,39},{8,40},{9,... | collective-permute-start | bytes 98312 | tf_op jit(solution)/shard_map/ppermute | solution.py:49
  35.2 0.0 copy-done.1
  35.2 0.0 copy-done.9
  35.2 4.1 %near_field.2.near0 = f32[16,4096]{1,0:T(8,128)S(1)} custom-call(s32[6,64]{1,0:T(8,128)S(1)} %bitcast.16, bf16[16,4096]{1,0:T(8,128)(2,1)S(1)} %collective-permute-done.3.halo0, bf16[16,8192]{1,0:T(8,128)(2,1)S(1)} %copy-done.1, bf16[16,4096]{1,0:T(8,128)(2,1)S(1)} %collective-permute-done.4.halo1, bf16[64,6,128,128]{3,2,1,0:T(8,128)(2,1)} %blocks_hbm.3), custom_call_target="tpu_custom_call" | custom-call | flops 1000 | bytes 1000 | tf_op jit(solution)/shard_map/near_field/pallas_call | solution.py:233
  39.4 6.3 %collective-permute-done.10 = bf16[128,128]{1,0:T(8,128)(2,1)S(1)} collective-permute-done((bf16[128,128]{1,0:T(8,128)(2,1)S(1)}, bf16[128,128]{1,0:T(8,128)(2,1)S(1)}, u32[]{:S(2)}, u32[]{:S(2)}) %collective-permute-start.10) | collective-permute-done | bytes 32800 | tf_op jit(solution)/shard_map/ppermute | solution.py:49
  45.7 0.0 copy-start.5
  45.7 0.0 copy-start.7
  45.7 0.0 copy-start.8
  45.7 0.0 copy-start.12
  45.7 0.0 copy-start.13
  45.7 0.0 copy-start.14
  45.7 0.0 copy-start.15
  45.8 3.4 %collective-permute-start.11 = (bf16[256,128]{1,0:T(8,128)(2,1)S(1)}, bf16[256,128]{1,0:T(8,128)(2,1)S(1)}, u32[]{:S(2)}, u32[]{:S(2)}) collective-permute-start(bf16[256,128]{1,0:T(8,128)(2,1)S(1)} %constant_dynamic-update-slice_fusion.5.c0), channel_id=1, source_target_pairs={{0,64},{1,65},{2,66},{3,67},{4,68},{5,69},{6,70},{7,71},{8,72},{9,... | collective-permute-start | bytes 196616 | tf_op jit(solution)/shard_map/ppermute | solution.py:49
  49.1 6.3 %collective-permute-start.8 = (bf16[2240,128]{1,0:T(8,128)(2,1)S(1)}, bf16[2240,128]{1,0:T(8,128)(2,1)S(1)}, u32[]{:S(2)}, u32[]{:S(2)}) collective-permute-start(bf16[2240,128]{1,0:T(8,128)(2,1)S(1)} %get-tuple-element.42.g0), channel_id=1, source_target_pairs={{0,4},{1,5},{2,6},{3,7},{4,0},{5,1},{6,2},{7,3},{8,12},{9,13},{10,... | collective-permute-start | bytes 1720328 | tf_op jit(solution)/shard_map/ppermute | solution.py:49
  55.4 4.1 %near_field.3.near1 = f32[16,4096]{1,0:T(8,128)S(1)} custom-call(s32[6,64]{1,0:T(8,128)S(1)} %bitcast.17, bf16[16,4096]{1,0:T(8,128)(2,1)S(1)} %collective-permute-done.3.halo0, bf16[16,8192]{1,0:T(8,128)(2,1)S(1)} %copy-done.1, bf16[16,4096]{1,0:T(8,128)(2,1)S(1)} %collective-permute-done.4.halo1, bf16[64,6,128,128]{3,2,1,0:T(8,128)(2,1)} %blocks_hbm.3), custom_call_target="tpu_custom_call" | custom-call | flops 1000 | bytes 1000 | tf_op jit(solution)/shard_map/near_field/pallas_call | solution.py:233
  59.6 0.0 copy-start.2
  59.6 0.0 copy-start.3
  59.6 0.0 copy-start.10
  59.6 0.0 copy-start.11
  59.6 0.0 collective-permute-done.11.c1
  59.6 0.0 collective-permute-done.14.e0
  59.6 0.0 collective-permute-done.13.z2
  59.7 0.0 collective-permute-done.12.z0
  59.7 0.1 collective-permute-start.15
  59.8 0.5 collective-permute-start.16
  60.3 0.0 copy-done.4
  60.3 0.0 copy-done.5
  60.3 0.0 copy-done.7
  60.3 0.0 copy-done.8
  60.3 0.0 copy-done.12
  60.3 0.0 copy-done.13
  60.3 0.0 copy-done.14
  60.3 2.0 %down_sweep.1.node_ref = bf16[128,64]{1,0:T(8,128)(2,1)S(1)} custom-call(s32[1,8]{1,0:T(1,128)S(1)} %copy-done.14, s32[1,8]{1,0:T(1,128)S(1)} %copy-done.15, s32[8,8]{1,0:T(8,128)S(1)} %copy-done.12, s32[8,8]{1,0:T(8,128)S(1)} %copy-done.13, bf16[256,128]{1,0:T(8,128)(2,1)S(1)} %constant_dynamic-update-slice_fusion.5.c0, ...), custom_call_target="tpu_custom_call" | custom-call | flops 1000 | bytes 1000 | tf_op jit(solution)/shard_map/down_sweep/pallas_call | solution.py:340
  62.3 0.0 collective-permute-done.8.g1
  62.3 0.0 collective-permute-done.15.z1
  62.3 0.2 collective-permute-done.16.z3
  62.6 7.5 %far_field.1 = f32[16,8192]{1,0:T(8,128)} custom-call(s32[8,64]{1,0:T(8,128)S(1)} %bitcast.18, s32[8,64]{1,0:T(8,128)S(1)} %bitcast.19, bf16[2240,128]{1,0:T(8,128)(2,1)S(1)} %get-tuple-element.42.g0, bf16[2240,128]{1,0:T(8,128)(2,1)S(1)} %collective-permute-done.8.g1, bf16[2240,128]{1,0:T(8,128)(2,1)S(1)} %collective-permute-done.12.z0, ...), custom_call_target="tpu_custom_call" | custom-call | flops 1000 | bytes 1000 | tf_op jit(solution)/shard_map/far_field/pallas_call | solution.py:446
  (17 shorter events, 0.1 us)
Async XLA Ops:
  5.0 14.4 %collective-permute-start.2 = (bf16[560,128]{1,0:T(8,128)(2,1)}, bf16[560,128]{1,0:T(8,128)(2,1)S(1)}, u32[]{:S(2)}, u32[]{:S(2)}) collective-permute-start(bf16[560,128]{1,0:T(8,128)(2,1)} %get-tuple-element.33.own), channel_id=1, source_target_pairs={{0,3},{1,2},{2,1},{3,0},{4,7},{5,6},{6,5},{7,4},{8,11},{9,10},{10,... | collective-permute-start | bytes 430088 | tf_op jit(solution)/shard_map/ppermute | solution.py:49
  5.0 14.3 %collective-permute-start.1 = (bf16[560,128]{1,0:T(8,128)(2,1)}, bf16[560,128]{1,0:T(8,128)(2,1)S(1)}, u32[]{:S(2)}, u32[]{:S(2)}) collective-permute-start(bf16[560,128]{1,0:T(8,128)(2,1)} %get-tuple-element.33.own), channel_id=1, source_target_pairs={{0,2},{1,3},{2,0},{3,1},{4,6},{5,7},{6,4},{7,5},{8,10},{9,11},{10,... | collective-permute-start | bytes 430088 | tf_op jit(solution)/shard_map/ppermute | solution.py:49
  7.4 12.0 %collective-permute-start = (bf16[560,128]{1,0:T(8,128)(2,1)}, bf16[560,128]{1,0:T(8,128)(2,1)S(1)}, u32[]{:S(2)}, u32[]{:S(2)}) collective-permute-start(bf16[560,128]{1,0:T(8,128)(2,1)} %get-tuple-element.33.own), channel_id=1, source_target_pairs={{0,1},{1,0},{2,3},{3,2},{4,5},{5,4},{6,7},{7,6},{8,9},{9,8},{10,11... | collective-permute-start | bytes 430088 | tf_op jit(solution)/shard_map/ppermute | solution.py:49
  8.3 11.0 %collective-permute-start.3 = (bf16[16,4096]{1,0:T(8,128)(2,1)}, bf16[16,4096]{1,0:T(8,128)(2,1)S(1)}, u32[]{:S(2)}, u32[]{:S(2)}) collective-permute-start(bf16[16,4096]{1,0:T(8,128)(2,1)} %get-tuple-element.34), channel_id=1, source_target_pairs={{0,1},{2,3},{4,5},{6,7},{8,9},{10,11},{12,13},{14,15},{16,17},{18,... | collective-permute-start | bytes 393224 | tf_op jit(solution)/shard_map/ppermute | solution.py:49
  8.8 10.5 %collective-permute-start.4 = (bf16[16,4096]{1,0:T(8,128)(2,1)}, bf16[16,4096]{1,0:T(8,128)(2,1)S(1)}, u32[]{:S(2)}, u32[]{:S(2)}) collective-permute-start(bf16[16,4096]{1,0:T(8,128)(2,1)} %get-tuple-element.35), channel_id=1, source_target_pairs={{1,2},{3,4},{5,6},{7,8},{9,10},{11,12},{13,14},{15,16},{17,18},{19... | collective-permute-start | bytes 393224 | tf_op jit(solution)/shard_map/ppermute | solution.py:49
  14.6 1.9 %copy-start = (bf16[316,64,64]{0,2,1:T(8,128)(2,1)S(1)}, bf16[316,64,64]{0,2,1:T(8,128)(2,1)}, u32[]{:S(2)}) copy-start(bf16[316,64,64]{0,2,1:T(8,128)(2,1)} %param.34) | copy-start | bytes 7766020
  16.5 2.8 %copy-start.6 = (bf16[560,128]{1,0:T(8,128)(2,1)S(1)}, bf16[560,128]{1,0:T(8,128)(2,1)}, u32[]{:S(2)}) copy-start(bf16[560,128]{1,0:T(8,128)(2,1)} %get-tuple-element.33.own) | copy-start | bytes 430084
  16.5 18.7 %copy-start.1 = (bf16[16,8192]{1,0:T(8,128)(2,1)S(1)}, bf16[16,8192]{1,0:T(8,128)(2,1)}, u32[]{:S(2)}) copy-start(bf16[16,8192]{1,0:T(8,128)(2,1)} %own_ref.3) | copy-start | bytes 786436
  16.5 18.7 %copy-start.9 = (s32[64,6]{0,1:T(8,128)S(1)}, s32[64,6]{0,1:T(8,128)}, u32[]{:S(2)}) copy-start(s32[64,6]{0,1:T(8,128)} %param.25) | copy-start | bytes 4612
  19.5 5.1 %collective-permute-start.7 = (bf16[16,128]{1,0:T(8,128)(2,1)S(1)}, bf16[16,128]{1,0:T(8,128)(2,1)S(1)}, u32[]{:S(2)}, u32[]{:S(2)}) collective-permute-start(bf16[16,128]{1,0:T(8,128)(2,1)S(1)} %get-tuple-element.39), channel_id=1, source_target_pairs={{0,24},{1,25},{2,26},{3,27},{4,28},{5,29},{6,30},{7,31},{8,16},{9,... | collective-permute-start | bytes 12296 | tf_op jit(solution)/shard_map/ppermute | solution.py:49
  23.5 4.0 %collective-permute-start.6 = (bf16[16,128]{1,0:T(8,128)(2,1)S(1)}, bf16[16,128]{1,0:T(8,128)(2,1)S(1)}, u32[]{:S(2)}, u32[]{:S(2)}) collective-permute-start(bf16[16,128]{1,0:T(8,128)(2,1)S(1)} %get-tuple-element.39), channel_id=1, source_target_pairs={{0,16},{1,17},{2,18},{3,19},{4,20},{5,21},{6,22},{7,23},{8,24},{9,... | collective-permute-start | bytes 12296 | tf_op jit(solution)/shard_map/ppermute | solution.py:49
  23.5 4.0 %collective-permute-start.5 = (bf16[16,128]{1,0:T(8,128)(2,1)S(1)}, bf16[16,128]{1,0:T(8,128)(2,1)S(1)}, u32[]{:S(2)}, u32[]{:S(2)}) collective-permute-start(bf16[16,128]{1,0:T(8,128)(2,1)S(1)} %get-tuple-element.39), channel_id=1, source_target_pairs={{0,8},{1,9},{2,10},{3,11},{4,12},{5,13},{6,14},{7,15},{8,0},{9,1},... | collective-permute-start | bytes 12296 | tf_op jit(solution)/shard_map/ppermute | solution.py:49
  27.5 32.2 %collective-permute-start.13 = (bf16[2240,128]{1,0:T(8,128)(2,1)S(1)}, bf16[2240,128]{1,0:T(8,128)(2,1)S(1)}, u32[]{:S(2)}, u32[]{:S(2)}) collective-permute-start(bf16[2240,128]{1,0:T(8,128)(2,1)S(1)} %get-tuple-element.42.g0), channel_id=1, source_target_pairs={{8,16},{9,17},{10,18},{11,19},{12,20},{13,21},{14,22},{15,23},{24,... | collective-permute-start | bytes 1720328 | tf_op jit(solution)/shard_map/ppermute | solution.py:49
  28.2 31.5 %collective-permute-start.12 = (bf16[2240,128]{1,0:T(8,128)(2,1)S(1)}, bf16[2240,128]{1,0:T(8,128)(2,1)S(1)}, u32[]{:S(2)}, u32[]{:S(2)}) collective-permute-start(bf16[2240,128]{1,0:T(8,128)(2,1)S(1)} %get-tuple-element.42.g0), channel_id=1, source_target_pairs={{0,8},{1,9},{2,10},{3,11},{4,12},{5,13},{6,14},{7,15},{16,24},{17,... | collective-permute-start | bytes 1720328 | tf_op jit(solution)/shard_map/ppermute | solution.py:49
  30.6 3.2 %collective-permute-start.9 = (bf16[64,128]{1,0:T(8,128)(2,1)S(1)}, bf16[64,128]{1,0:T(8,128)(2,1)S(1)}, u32[]{:S(2)}, u32[]{:S(2)}) collective-permute-start(bf16[64,128]{1,0:T(8,128)(2,1)S(1)} %pad_maximum_fusion), channel_id=1, source_target_pairs={{0,4},{1,5},{2,6},{3,7},{4,0},{5,1},{6,2},{7,3},{8,12},{9,13},{10,... | collective-permute-start | bytes 49160 | tf_op jit(solution)/shard_map/ppermute | solution.py:49
  32.5 27.1 %collective-permute-start.14 = (bf16[1120,128]{1,0:T(8,128)(2,1)S(1)}, bf16[1120,128]{1,0:T(8,128)(2,1)S(1)}, u32[]{:S(2)}, u32[]{:S(2)}) collective-permute-start(bf16[1120,128]{1,0:T(8,128)(2,1)S(1)} %get-tuple-element.53), channel_id=1, source_target_pairs={{4,16},{5,17},{12,24},{13,25},{18,6},{19,7},{20,32},{21,33},{26,14... | collective-permute-start | bytes 860168 | tf_op jit(solution)/shard_map/ppermute | solution.py:49
  33.8 11.8 %collective-permute-start.10 = (bf16[128,128]{1,0:T(8,128)(2,1)S(1)}, bf16[128,128]{1,0:T(8,128)(2,1)S(1)}, u32[]{:S(2)}, u32[]{:S(2)}) collective-permute-start(bf16[128,128]{1,0:T(8,128)(2,1)S(1)} %constant_dynamic-update-slice_fusion), channel_id=1, source_target_pairs={{0,32},{1,33},{2,34},{3,35},{4,36},{5,37},{6,38},{7,39},{8,40},{9,... | collective-permute-start | bytes 98312 | tf_op jit(solution)/shard_map/ppermute | solution.py:49
  45.7 14.6 %copy-start.4 = (bf16[32,64,64]{2,1,0:T(8,128)(2,1)S(1)}, bf16[32,64,64]{2,1,0:T(8,128)(2,1)}, u32[]{:S(2)}) copy-start(bf16[32,64,64]{2,1,0:T(8,128)(2,1)} %param.32) | copy-start | bytes 786436
  45.7 14.6 %copy-start.5 = (bf16[32,64,64]{2,1,0:T(8,128)(2,1)S(1)}, bf16[32,64,64]{2,1,0:T(8,128)(2,1)}, u32[]{:S(2)}) copy-start(bf16[32,64,64]{2,1,0:T(8,128)(2,1)} %dt_ref.1) | copy-start | bytes 786436
  45.7 14.6 %copy-start.7 = (bf16[8,64,64]{2,1,0:T(8,128)(2,1)S(1)}, bf16[8,64,64]{2,1,0:T(8,128)(2,1)}, u32[]{:S(2)}) copy-start(bf16[8,64,64]{2,1,0:T(8,128)(2,1)} %dn_ref.1) | copy-start | bytes 196612
  45.7 14.6 %copy-start.8 = (bf16[1,64,64]{2,1,0:T(8,128)(2,1)S(1)}, bf16[1,64,64]{2,1,0:T(8,128)(2,1)}, u32[]{:S(2)}) copy-start(bf16[1,64,64]{2,1,0:T(8,128)(2,1)} %param.31) | copy-start | bytes 24580
  45.7 14.6 %copy-start.12 = (s32[8,8]{1,0:T(8,128)S(1)}, s32[8,8]{1,0:T(8,128)}, u32[]{:S(2)}) copy-start(s32[8,8]{1,0:T(8,128)} %top_src.1) | copy-start | bytes 772
  45.7 14.6 %copy-start.13 = (s32[8,8]{1,0:T(8,128)S(1)}, s32[8,8]{1,0:T(8,128)}, u32[]{:S(2)}) copy-start(s32[8,8]{1,0:T(8,128)} %top_type.1) | copy-start | bytes 772
  45.7 14.6 %copy-start.14 = (s32[1,8]{1,0:T(1,128)S(1)}, s32[1,8]{1,0:T(1,128)}, u32[]{:S(2)}) copy-start(s32[1,8]{1,0:T(1,128)} %far_src.1) | copy-start | bytes 100
  45.7 14.6 %copy-start.15 = (s32[1,8]{1,0:T(1,128)S(1)}, s32[1,8]{1,0:T(1,128)}, u32[]{:S(2)}) copy-start(s32[1,8]{1,0:T(1,128)} %far_type.1) | copy-start | bytes 100
  45.8 13.9 %collective-permute-start.11 = (bf16[256,128]{1,0:T(8,128)(2,1)S(1)}, bf16[256,128]{1,0:T(8,128)(2,1)S(1)}, u32[]{:S(2)}, u32[]{:S(2)}) collective-permute-start(bf16[256,128]{1,0:T(8,128)(2,1)S(1)} %constant_dynamic-update-slice_fusion.5.c0), channel_id=1, source_target_pairs={{0,64},{1,65},{2,66},{3,67},{4,68},{5,69},{6,70},{7,71},{8,72},{9,... | collective-permute-start | bytes 196616 | tf_op jit(solution)/shard_map/ppermute | solution.py:49
  49.1 13.2 %collective-permute-start.8 = (bf16[2240,128]{1,0:T(8,128)(2,1)S(1)}, bf16[2240,128]{1,0:T(8,128)(2,1)S(1)}, u32[]{:S(2)}, u32[]{:S(2)}) collective-permute-start(bf16[2240,128]{1,0:T(8,128)(2,1)S(1)} %get-tuple-element.42.g0), channel_id=1, source_target_pairs={{0,4},{1,5},{2,6},{3,7},{4,0},{5,1},{6,2},{7,3},{8,12},{9,13},{10,... | collective-permute-start | bytes 1720328 | tf_op jit(solution)/shard_map/ppermute | solution.py:49
  59.6 3.0 %copy-start.2 = (bf16[64,128,64]{1,2,0:T(8,128)(2,1)S(1)}, bf16[64,128,64]{1,2,0:T(8,128)(2,1)}, u32[]{:S(2)}) copy-start(bf16[64,128,64]{1,2,0:T(8,128)(2,1)} %param.23) | copy-start | bytes 3145732
  59.6 3.0 %copy-start.3 = (bf16[64,64,64]{2,1,0:T(8,128)(2,1)S(1)}, bf16[64,64,64]{2,1,0:T(8,128)(2,1)}, u32[]{:S(2)}) copy-start(bf16[64,64,64]{2,1,0:T(8,128)(2,1)} %down_buf.1) | copy-start | bytes 1572868
  59.6 3.0 %copy-start.10 = (s32[64,8]{0,1:T(8,128)S(1)}, s32[64,8]{0,1:T(8,128)}, u32[]{:S(2)}) copy-start(s32[64,8]{0,1:T(8,128)} %param.36) | copy-start | bytes 6148
  59.6 2.9 %copy-start.11 = (s32[64,8]{0,1:T(8,128)S(1)}, s32[64,8]{0,1:T(8,128)}, u32[]{:S(2)}) copy-start(s32[64,8]{0,1:T(8,128)} %param.37) | copy-start | bytes 6148
  59.7 2.7 %collective-permute-start.15 = (bf16[2240,128]{1,0:T(8,128)(2,1)S(1)}, bf16[2240,128]{1,0:T(8,128)(2,1)S(1)}, u32[]{:S(2)}, u32[]{:S(2)}) collective-permute-start(bf16[2240,128]{1,0:T(8,128)(2,1)S(1)} %collective-permute-done.12.z0), channel_id=1, source_target_pairs={{0,4},{1,5},{2,6},{3,7},{4,0},{5,1},{6,2},{7,3},{8,12},{9,13},{10,... | collective-permute-start | bytes 1720328 | tf_op jit(solution)/shard_map/ppermute | solution.py:49
  59.8 2.8 %collective-permute-start.16 = (bf16[2240,128]{1,0:T(8,128)(2,1)S(1)}, bf16[2240,128]{1,0:T(8,128)(2,1)S(1)}, u32[]{:S(2)}, u32[]{:S(2)}) collective-permute-start(bf16[2240,128]{1,0:T(8,128)(2,1)S(1)} %collective-permute-done.13.z2), channel_id=1, source_target_pairs={{0,4},{1,5},{2,6},{3,7},{4,0},{5,1},{6,2},{7,3},{8,12},{9,13},{10,... | collective-permute-start | bytes 1720328 | tf_op jit(solution)/shard_map/ppermute | solution.py:49

commit v5 on v4

--- a/solution.py
+++ b/solution.py
@@ -66,7 +66,7 @@
     for p in range(DEVICES):
         x, core = p & 3, (p >> 2) & 1
         target = p + 12 if core == 1 else p - 12
-        if (x < 2) == (core == 1) and 0 <= target < DEVICES:
+        if (x < 2) == (core == 0) and 0 <= target < DEVICES:
             pairs.append((p, target))
     return pairs
 
@@ -246,12 +246,10 @@
     )(src, halo0, own, halo1, blocks)
 
 
-def join_kernel(own, x1, x2, x3, mine_ref, group_ref, tail_ref):
+def join_kernel(own, x1, x2, x3, mine_ref, group_ref):
     total = jnp.zeros((16, 128), jnp.float32)
     for d, ref in enumerate((own, x1, x2, x3)):
         mine_ref[d * BLOCK : (d + 1) * BLOCK, :] = ref[...]
-        if d >= 2:
-            tail_ref[(d - 2) * BLOCK : (d - 1) * BLOCK, :] = ref[...]
         total = total + ref[TERM_ROW : TERM_ROW + 16, :].astype(jnp.float32)
     group_ref[...] = (total + pltpu.roll(total, RANK, 1)).astype(jnp.bfloat16)
 
@@ -261,11 +259,10 @@
     return pl.pallas_call(
         join_kernel,
         in_specs=[vmem] * 4,
-        out_specs=[vmem] * 3,
+        out_specs=[vmem] * 2,
         out_shape=[
             jax.ShapeDtypeStruct((4 * BLOCK, 128), jnp.bfloat16),
             jax.ShapeDtypeStruct((16, 128), jnp.bfloat16),
-            jax.ShapeDtypeStruct((2 * BLOCK, 128), jnp.bfloat16),
         ],
         compiler_params=pltpu.CompilerParams(vmem_limit_bytes=8 << 20),
         cost_estimate=pl.CostEstimate(flops=1000, bytes_accessed=1000, transcendentals=0),
@@ -356,13 +353,14 @@
 
 
 def far_kernel(
-    slot_ref, type_ref, g0, g1, z0, z1, z2, z3, e0, turned, rows_buf, down_buf, near0, near1, node_ref,
+    slot_ref, type_ref, g0, g1, z0, z1, z2, z3, e0, e1, turned, rows_buf, down_buf, near0, near1, node_ref,
     out_ref, table, found, scalars, sems, scalar_sem,
 ):
     copies = []
     for j, ref in enumerate((g0, g1, z0, z1, z2, z3)):
         copies.append((ref, table.at[pl.ds(j * 4 * BLOCK, 4 * BLOCK), :]))
-    copies.append((e0, table.at[pl.ds(24 * BLOCK, 2 * BLOCK), :]))
+    for j, ref in enumerate((e0, e1)):
+        copies.append((ref, table.at[pl.ds((24 + j) * BLOCK, BLOCK), :]))
     copies = [pltpu.make_async_copy(source, target, sems.at[j]) for j, (source, target) in enumerate(copies)]
     for c in copies:
         c.start()
@@ -445,20 +443,20 @@
     hbm = pl.BlockSpec(memory_space=pl.ANY)
     return pl.pallas_call(
         far_kernel,
-        in_specs=[vmem, smem] + [hbm] * 7 + [vmem] * 6,
+        in_specs=[vmem, smem] + [hbm] * 8 + [vmem] * 6,
         out_specs=vmem,
         out_shape=jax.ShapeDtypeStruct((16, LEAVES * PANEL), jnp.float32),
         scratch_shapes=[
             pltpu.VMEM((26 * BLOCK, 128), jnp.bfloat16),
             pltpu.VMEM((8, 128), jnp.int32),
             pltpu.SMEM((8, 128), jnp.int32),
-            pltpu.SemaphoreType.DMA((7,)),
+            pltpu.SemaphoreType.DMA((8,)),
             pltpu.SemaphoreType.DMA,
         ],
         compiler_params=pltpu.CompilerParams(vmem_limit_bytes=16 << 20),
         cost_estimate=pl.CostEstimate(flops=1000, bytes_accessed=1000, transcendentals=0),
         name="far_field",
-    )(slots, types, *pieces, extra, turned, row_basis, down_leaf, *near, node_local)
+    )(slots, types, *pieces, *extra, turned, row_basis, down_leaf, *near, node_local)
 
 
 def per_device(
@@ -489,28 +487,26 @@
     )
     along_x = {d: moved(own, flipped(d)) for d in (3, 1, 2)}
     halo0, halo1 = moved(to_first, line_swap(1, 0)), moved(to_second, line_swap(1, 1))
-    turned = turned_couplings(jnp.transpose(coupling, (1, 2, 0)).reshape(2, HALF * RANK, TYPES))
-    x1, x2, x3, turned, halo0, halo1 = lax.optimization_barrier(
-        (along_x[1], along_x[2], along_x[3], turned, halo0, halo1)
-    )
-    mine, group, tail = joined(own, x1, x2, x3)
+    x1, x2, x3, coupling = lax.optimization_barrier((along_x[1], along_x[2], along_x[3], coupling))
+    tail = moved(own, two_blocks_away())
+    mine, group = joined(own, x1, x2, x3)
     along_z = [moved(group, flipped(8 * d)) for d in (1, 2, 3)]
-    *along_z, mine, tail = lax.optimization_barrier((*along_z, mine, tail))
-    extra = [moved(tail, two_blocks_away())]
+    *along_z, mine, tail, halo0, halo1 = lax.optimization_barrier((*along_z, mine, tail, halo0, halo1))
     z0, z1 = moved(mine, line_swap(8, 0)), moved(mine, line_swap(8, 1))
     column = jnp.concatenate([group] + along_z)
     column = jnp.concatenate([column, moved(column, CORE_SWAP)])
     y1 = moved(column, flipped(32))
-    column, halo0, halo1 = lax.optimization_barrier((column, halo0, halo1))
+    column, halo0, halo1, tail = lax.optimization_barrier((column, halo0, halo1, tail))
+    extra = [moved(tail, flipped(2)), moved(tail, flipped(3))]
     near0 = near_field(near_src.T, halo0, loads, halo1, near_blocks, 0, LEAVES // 2)
-    y1, near0, halo0 = lax.optimization_barrier((y1, near0, halo0))
+    near1 = near_field(near_src.T, halo0, loads, halo1, near_blocks, LEAVES // 2, LEAVES // 2)
+    y1, near0, near1, coupling = lax.optimization_barrier((y1, near0, near1, coupling))
+    turned = turned_couplings(jnp.transpose(coupling, (1, 2, 0)).reshape(2, HALF * RANK, TYPES))
     column = jnp.concatenate([column, y1])
     y2 = moved(column, flipped(64))
-    near1 = near_field(near_src.T, halo0, loads, halo1, near_blocks, LEAVES // 2, LEAVES // 2)
-    y2, near1, z0, z1, *extra = lax.optimization_barrier((y2, near1, z0, z1, *extra))
+    y2, turned, mine, z0, z1, *extra = lax.optimization_barrier((y2, turned, mine, z0, z1, *extra))
     theirs = moved(mine, CORE_SWAP)
     swapped = [moved(z0, CORE_SWAP), moved(z1, CORE_SWAP)]
-    (extra,) = extra
     node_local = down_sweep(
         far_group_src,
         far_group_type,

time: 70.3 us -> 65.9 us (0.937)
  the two profiles are of different devices: /device:TPU:7 before, /device:TPU:1 now
where the time goes in v5:
time: 65.9 us; the launch traced here: 64.9 us
  starting transfers between devices  29.5 us (45%)
  Pallas kernels  26.2 us (40%)
  waiting for transfers between devices  7.84 us (12%)
  local copies, waits for them, and re-layouts  1.04 us (2%)
    ppermute x19, starting transfers between devices, moved(): return lax.ppermute(value, AXES, pairs)  29.5 us
    pallas_call x2, Pallas kernels, near_field(): pl.pallas_call(functools.partial(near_kernel, first), in_specs=[pl.BlockS...  8.58 us
    ppermute x19, waiting for transfers between devices, moved(): return lax.ppermute(value, AXES, pairs)  7.84 us
    pallas_call x1, Pallas kernels, far_field(): pl.pallas_call(far_kernel, in_specs=[vmem, smem] + [hbm] * 8 + [vmem] * 6...  7.79 us
    pallas_call x1, Pallas kernels, up_sweep(): pl.pallas_call(up_kernel, in_specs=[hbm] * 5 + [vmem], out_specs=[vmem] *...  4.99 us
    pallas_call x1, Pallas kernels, turned_couplings(): pl.pallas_call(turn_kernel, grid=(steps,), in_specs=[pl.BlockSpec((2, HAL...  2.75 us
    pallas_call x1, Pallas kernels, down_sweep(): pl.pallas_call(down_kernel, in_specs=[smem] * 4 + [vmem] * 3 + [hbm] * 2...  1.99 us
  transfers between devices with their start and end apart: 19, of which 5 were waited for; matrix products, arithmetic and copies ran while one was open for 0% of the time, Pallas kernels for 21%

profile of v5, /device:TPU:1, one launch (start us, length us, event | category | flops | bytes accessed | tf_op | source)
XLA Modules:
  0.0 64.9 jit_solution(6100987175800384019)
XLA Ops:
  0.0 5.0 %up_sweep.1 = (bf16[560,128]{1,0:T(8,128)(2,1)}, bf16[16,4096]{1,0:T(8,128)(2,1)}, bf16[16,4096]{1,0:T(8,128)(2,1)}) custom-call(bf16[16,8192]{1,0:T(8,128)(2,1)} %own_ref.3, bf16[64,64,128]{2,1,0:T(8,128)(2,1)} %bitcast.20, bf16[64,64,64]{2,1,0:T(8,128)(2,1)} %ul_hbm.1, bf16[8,64,64]{2,1,0:T(8,128)(2,1)} %un_hbm.1, bf16[64,64]{1,0:T(8,128)(2,1)} %bitcast.21, ...), custom_call_target="tpu_custom_call" | custom-call | flops 1000 | bytes 1000 | tf_op jit(solution)/shard_map/up_sweep/pallas_call | solution.py:138
  5.0 3.4 %collective-permute-start.2 = (bf16[560,128]{1,0:T(8,128)(2,1)}, bf16[560,128]{1,0:T(8,128)(2,1)S(1)}, u32[]{:S(2)}, u32[]{:S(2)}) collective-permute-start(bf16[560,128]{1,0:T(8,128)(2,1)} %get-tuple-element.36.own), channel_id=1, source_target_pairs={{0,3},{1,2},{2,1},{3,0},{4,7},{5,6},{6,5},{7,4},{8,11},{9,10},{10,... | collective-permute-start | bytes 430088 | tf_op jit(solution)/shard_map/ppermute | solution.py:49
  8.4 0.5 collective-permute-start.1
  8.9 0.1 collective-permute-start
  9.1 1.3 %collective-permute-start.7 = (bf16[16,4096]{1,0:T(8,128)(2,1)}, bf16[16,4096]{1,0:T(8,128)(2,1)S(1)}, u32[]{:S(2)}, u32[]{:S(2)}) collective-permute-start(bf16[16,4096]{1,0:T(8,128)(2,1)} %get-tuple-element.42), channel_id=1, source_target_pairs={{0,1},{2,3},{4,5},{6,7},{8,9},{10,11},{12,13},{14,15},{16,17},{18,... | collective-permute-start | bytes 393224 | tf_op jit(solution)/shard_map/ppermute | solution.py:49
  10.4 1.3 %collective-permute-start.6 = (bf16[560,128]{1,0:T(8,128)(2,1)}, bf16[560,128]{1,0:T(8,128)(2,1)S(1)}, u32[]{:S(2)}, u32[]{:S(2)}) collective-permute-start(bf16[560,128]{1,0:T(8,128)(2,1)} %get-tuple-element.36.own), channel_id=1, source_target_pairs={{6,18},{7,19},{14,26},{15,27},{16,4},{17,5},{22,34},{23,35},{24,12... | collective-permute-start | bytes 430088 | tf_op jit(solution)/shard_map/ppermute | solution.py:49
  11.7 3.0 %collective-permute-done.2.x3 = bf16[560,128]{1,0:T(8,128)(2,1)S(1)} collective-permute-done((bf16[560,128]{1,0:T(8,128)(2,1)}, bf16[560,128]{1,0:T(8,128)(2,1)S(1)}, u32[]{:S(2)}, u32[]{:S(2)}) %collective-permute-start.2) | collective-permute-done | bytes 143392 | tf_op jit(solution)/shard_map/ppermute | solution.py:49
  14.7 6.1 %collective-permute-start.8 = (bf16[16,4096]{1,0:T(8,128)(2,1)}, bf16[16,4096]{1,0:T(8,128)(2,1)S(1)}, u32[]{:S(2)}, u32[]{:S(2)}) collective-permute-start(bf16[16,4096]{1,0:T(8,128)(2,1)} %get-tuple-element.43), channel_id=1, source_target_pairs={{1,2},{3,4},{5,6},{7,8},{9,10},{11,12},{13,14},{15,16},{17,18},{19... | collective-permute-start | bytes 393224 | tf_op jit(solution)/shard_map/ppermute | solution.py:49
  20.8 0.0 collective-permute-done.1.x2
  20.9 0.0 collective-permute-done.x1
  20.9 0.0 copy-start.6
  20.9 0.9 %copy-done.6 = bf16[560,128]{1,0:T(8,128)(2,1)S(1)} copy-done((bf16[560,128]{1,0:T(8,128)(2,1)S(1)}, bf16[560,128]{1,0:T(8,128)(2,1)}, u32[]{:S(2)}) %copy-start.6) | copy-done | bytes 143384
  21.8 0.1 join_blocks.1
  21.9 3.8 %collective-permute-start.5 = (bf16[16,128]{1,0:T(8,128)(2,1)S(1)}, bf16[16,128]{1,0:T(8,128)(2,1)S(1)}, u32[]{:S(2)}, u32[]{:S(2)}) collective-permute-start(bf16[16,128]{1,0:T(8,128)(2,1)S(1)} %get-tuple-element.40), channel_id=1, source_target_pairs={{0,24},{1,25},{2,26},{3,27},{4,28},{5,29},{6,30},{7,31},{8,16},{9,... | collective-permute-start | bytes 12296 | tf_op jit(solution)/shard_map/ppermute | solution.py:49
  25.7 0.0 collective-permute-start.4
  25.7 0.0 collective-permute-done.7.halo0
  25.7 0.7 %collective-permute-start.3 = (bf16[16,128]{1,0:T(8,128)(2,1)S(1)}, bf16[16,128]{1,0:T(8,128)(2,1)S(1)}, u32[]{:S(2)}, u32[]{:S(2)}) collective-permute-start(bf16[16,128]{1,0:T(8,128)(2,1)S(1)} %get-tuple-element.40), channel_id=1, source_target_pairs={{0,8},{1,9},{2,10},{3,11},{4,12},{5,13},{6,14},{7,15},{8,0},{9,1},... | collective-permute-start | bytes 12296 | tf_op jit(solution)/shard_map/ppermute | solution.py:49
  26.3 0.0 collective-permute-done.8.halo1
  26.3 0.0 collective-permute-done.6
  26.4 0.3 collective-permute-done.5
  26.7 3.0 %collective-permute-done.4 = bf16[16,128]{1,0:T(8,128)(2,1)S(1)} collective-permute-done((bf16[16,128]{1,0:T(8,128)(2,1)S(1)}, bf16[16,128]{1,0:T(8,128)(2,1)S(1)}, u32[]{:S(2)}, u32[]{:S(2)}) %collective-permute-start.4) | collective-permute-done | bytes 4128 | tf_op jit(solution)/shard_map/ppermute | solution.py:49
  29.6 0.0 collective-permute-done.3
  29.6 0.7 %collective-permute-start.13 = (bf16[2240,128]{1,0:T(8,128)(2,1)S(1)}, bf16[2240,128]{1,0:T(8,128)(2,1)S(1)}, u32[]{:S(2)}, u32[]{:S(2)}) collective-permute-start(bf16[2240,128]{1,0:T(8,128)(2,1)S(1)} %get-tuple-element.58.g0), channel_id=1, source_target_pairs={{8,16},{9,17},{10,18},{11,19},{12,20},{13,21},{14,22},{15,23},{24,... | collective-permute-start | bytes 1720328 | tf_op jit(solution)/shard_map/ppermute | solution.py:49
  30.3 2.4 %collective-permute-start.12 = (bf16[2240,128]{1,0:T(8,128)(2,1)S(1)}, bf16[2240,128]{1,0:T(8,128)(2,1)S(1)}, u32[]{:S(2)}, u32[]{:S(2)}) collective-permute-start(bf16[2240,128]{1,0:T(8,128)(2,1)S(1)} %get-tuple-element.58.g0), channel_id=1, source_target_pairs={{0,8},{1,9},{2,10},{3,11},{4,12},{5,13},{6,14},{7,15},{16,24},{17,... | collective-permute-start | bytes 1720328 | tf_op jit(solution)/shard_map/ppermute | solution.py:49
  32.8 1.6 %collective-permute-start.9 = (bf16[64,128]{1,0:T(8,128)(2,1)S(1)}, bf16[64,128]{1,0:T(8,128)(2,1)S(1)}, u32[]{:S(2)}, u32[]{:S(2)}) collective-permute-start(bf16[64,128]{1,0:T(8,128)(2,1)S(1)} %pad_maximum_fusion), channel_id=1, source_target_pairs={{0,4},{1,5},{2,6},{3,7},{4,0},{5,1},{6,2},{7,3},{8,12},{9,13},{10,... | collective-permute-start | bytes 49160 | tf_op jit(solution)/shard_map/ppermute | solution.py:49
  34.4 0.8 %collective-permute-done.9 = bf16[64,128]{1,0:T(8,128)(2,1)S(1)} collective-permute-done((bf16[64,128]{1,0:T(8,128)(2,1)S(1)}, bf16[64,128]{1,0:T(8,128)(2,1)S(1)}, u32[]{:S(2)}, u32[]{:S(2)}) %collective-permute-start.9) | collective-permute-done | bytes 16416 | tf_op jit(solution)/shard_map/ppermute | solution.py:49
  35.2 1.4 %collective-permute-start.10 = (bf16[128,128]{1,0:T(8,128)(2,1)S(1)}, bf16[128,128]{1,0:T(8,128)(2,1)S(1)}, u32[]{:S(2)}, u32[]{:S(2)}) collective-permute-start(bf16[128,128]{1,0:T(8,128)(2,1)S(1)} %constant_dynamic-update-slice_fusion), channel_id=1, source_target_pairs={{0,32},{1,33},{2,34},{3,35},{4,36},{5,37},{6,38},{7,39},{8,40},{9,... | collective-permute-start | bytes 98312 | tf_op jit(solution)/shard_map/ppermute | solution.py:49
  36.6 0.8 %collective-permute-start.15 = (bf16[560,128]{1,0:T(8,128)(2,1)S(1)}, bf16[560,128]{1,0:T(8,128)(2,1)S(1)}, u32[]{:S(2)}, u32[]{:S(2)}) collective-permute-start(bf16[560,128]{1,0:T(8,128)(2,1)S(1)} %collective-permute-done.6), channel_id=1, source_target_pairs={{0,3},{1,2},{2,1},{3,0},{4,7},{5,6},{6,5},{7,4},{8,11},{9,10},{10,... | collective-permute-start | bytes 430088 | tf_op jit(solution)/shard_map/ppermute | solution.py:49
  37.4 0.5 collective-permute-start.14
  37.9 0.0 copy-done.1
  37.9 4.1 %near_field.3.near1 = f32[16,4096]{1,0:T(8,128)S(1)} custom-call(s32[6,64]{1,0:T(8,128)S(1)} %bitcast.16, bf16[16,4096]{1,0:T(8,128)(2,1)S(1)} %collective-permute-done.7.halo0, bf16[16,8192]{1,0:T(8,128)(2,1)S(1)} %copy-done.1, bf16[16,4096]{1,0:T(8,128)(2,1)S(1)} %collective-permute-done.8.halo1, bf16[64,6,128,128]{3,2,1,0:T(8,128)(2,1)} %blocks_hbm.3), custom_call_target="tpu_custom_call" | custom-call | flops 1000 | bytes 1000 | tf_op jit(solution)/shard_map/near_field/pallas_call | solution.py:233
  42.1 0.0 copy-start
  42.1 4.4 %near_field.2.near0 = f32[16,4096]{1,0:T(8,128)S(1)} custom-call(s32[6,64]{1,0:T(8,128)S(1)} %bitcast.17, bf16[16,4096]{1,0:T(8,128)(2,1)S(1)} %collective-permute-done.7.halo0, bf16[16,8192]{1,0:T(8,128)(2,1)S(1)} %copy-done.1, bf16[16,4096]{1,0:T(8,128)(2,1)S(1)} %collective-permute-done.8.halo1, bf16[64,6,128,128]{3,2,1,0:T(8,128)(2,1)} %blocks_hbm.3), custom_call_target="tpu_custom_call" | custom-call | flops 1000 | bytes 1000 | tf_op jit(solution)/shard_map/near_field/pallas_call | solution.py:233
  46.6 0.0 copy-start.4
  46.6 0.0 copy-start.5
  46.6 0.0 copy-start.7
  46.6 0.0 copy-start.8
  46.6 0.0 copy-start.12
  46.6 0.0 copy-start.13
  46.6 0.0 copy-start.14
  46.6 0.0 copy-start.15
  46.7 0.0 collective-permute-done.10
  46.7 2.7 %collective-permute-start.11 = (bf16[256,128]{1,0:T(8,128)(2,1)S(1)}, bf16[256,128]{1,0:T(8,128)(2,1)S(1)}, u32[]{:S(2)}, u32[]{:S(2)}) collective-permute-start(bf16[256,128]{1,0:T(8,128)(2,1)S(1)} %constant_dynamic-update-slice_fusion.5.c0), channel_id=1, source_target_pairs={{0,64},{1,65},{2,66},{3,67},{4,68},{5,69},{6,70},{7,71},{8,72},{9,... | collective-permute-start | bytes 196616 | tf_op jit(solution)/shard_map/ppermute | solution.py:49
  49.4 0.0 copy-done
  49.4 2.8 %turn_couplings.1.turned_ref.turned = bf16[10112,128]{1,0:T(8,128)(2,1)S(1)} custom-call(bf16[2,2048,316]{2,1,0:T(8,128)(2,1)S(1)} %bitcast.12), custom_call_target="tpu_custom_call" | custom-call | flops 1000 | bytes 1000 | tf_op jit(solution)/shard_map/turn_couplings/pallas_call | solution.py:181
  52.1 0.0 copy-start.2
  52.2 0.0 copy-start.3
  52.2 0.0 copy-start.10
  52.2 0.0 copy-start.11
  52.2 0.0 collective-permute-done.11.c1
  52.2 0.0 collective-permute-done.15.e1
  52.2 0.0 collective-permute-done.14.e0
  52.2 0.0 collective-permute-done.13.z2
  52.2 0.0 collective-permute-done.12.z0
  52.2 1.6 %collective-permute-start.16 = (bf16[2240,128]{1,0:T(8,128)(2,1)S(1)}, bf16[2240,128]{1,0:T(8,128)(2,1)S(1)}, u32[]{:S(2)}, u32[]{:S(2)}) collective-permute-start(bf16[2240,128]{1,0:T(8,128)(2,1)S(1)} %get-tuple-element.58.g0), channel_id=1, source_target_pairs={{0,4},{1,5},{2,6},{3,7},{4,0},{5,1},{6,2},{7,3},{8,12},{9,13},{10,... | collective-permute-start | bytes 1720328 | tf_op jit(solution)/shard_map/ppermute | solution.py:49
  53.9 0.1 collective-permute-start.17
  54.0 0.4 collective-permute-start.18
  54.4 0.0 copy-done.8
  54.4 2.0 %down_sweep.1.node_ref = bf16[128,64]{1,0:T(8,128)(2,1)S(1)} custom-call(s32[1,8]{1,0:T(1,128)S(1)} %copy-done.14, s32[1,8]{1,0:T(1,128)S(1)} %copy-done.15, s32[8,8]{1,0:T(8,128)S(1)} %copy-done.12, s32[8,8]{1,0:T(8,128)S(1)} %copy-done.13, bf16[256,128]{1,0:T(8,128)(2,1)S(1)} %constant_dynamic-update-slice_fusion.5.c0, ...), custom_call_target="tpu_custom_call" | custom-call | flops 1000 | bytes 1000 | tf_op jit(solution)/shard_map/down_sweep/pallas_call | solution.py:337
  56.4 0.0 collective-permute-done.16.g1
  56.5 0.0 collective-permute-done.17.z1
  56.5 0.7 %collective-permute-done.18.z3 = bf16[2240,128]{1,0:T(8,128)(2,1)S(1)} collective-permute-done((bf16[2240,128]{1,0:T(8,128)(2,1)S(1)}, bf16[2240,128]{1,0:T(8,128)(2,1)S(1)}, u32[]{:S(2)}, u32[]{:S(2)}) %collective-permute-start.18) | collective-permute-done | bytes 573472 | tf_op jit(solution)/shard_map/ppermute | solution.py:49
  57.1 0.0 copy-done.3
  57.1 7.8 %far_field.1 = f32[16,8192]{1,0:T(8,128)} custom-call(s32[8,64]{1,0:T(8,128)S(1)} %bitcast.18, s32[8,64]{1,0:T(8,128)S(1)} %bitcast.19, bf16[2240,128]{1,0:T(8,128)(2,1)S(1)} %get-tuple-element.58.g0, bf16[2240,128]{1,0:T(8,128)(2,1)S(1)} %collective-permute-done.16.g1, bf16[2240,128]{1,0:T(8,128)(2,1)S(1)} %collective-permute-done.12.z0, ...), custom_call_target="tpu_custom_call" | custom-call | flops 1000 | bytes 1000 | tf_op jit(solution)/shard_map/far_field/pallas_call | solution.py:444
  (21 shorter events, 0.1 us)
Async XLA Ops:
  0.0 37.9 %copy-start.1 = (bf16[16,8192]{1,0:T(8,128)(2,1)S(1)}, bf16[16,8192]{1,0:T(8,128)(2,1)}, u32[]{:S(2)}) copy-start(bf16[16,8192]{1,0:T(8,128)(2,1)} %own_ref.3) | copy-start | bytes 786436
  0.0 37.9 %copy-start.9 = (s32[64,6]{0,1:T(8,128)S(1)}, s32[64,6]{0,1:T(8,128)}, u32[]{:S(2)}) copy-start(s32[64,6]{0,1:T(8,128)} %param.25) | copy-start | bytes 4612
  5.0 9.7 %collective-permute-start.2 = (bf16[560,128]{1,0:T(8,128)(2,1)}, bf16[560,128]{1,0:T(8,128)(2,1)S(1)}, u32[]{:S(2)}, u32[]{:S(2)}) collective-permute-start(bf16[560,128]{1,0:T(8,128)(2,1)} %get-tuple-element.36.own), channel_id=1, source_target_pairs={{0,3},{1,2},{2,1},{3,0},{4,7},{5,6},{6,5},{7,4},{8,11},{9,10},{10,... | collective-permute-start | bytes 430088 | tf_op jit(solution)/shard_map/ppermute | solution.py:49
  8.4 12.5 %collective-permute-start.1 = (bf16[560,128]{1,0:T(8,128)(2,1)}, bf16[560,128]{1,0:T(8,128)(2,1)S(1)}, u32[]{:S(2)}, u32[]{:S(2)}) collective-permute-start(bf16[560,128]{1,0:T(8,128)(2,1)} %get-tuple-element.36.own), channel_id=1, source_target_pairs={{0,2},{1,3},{2,0},{3,1},{4,6},{5,7},{6,4},{7,5},{8,10},{9,11},{10,... | collective-permute-start | bytes 430088 | tf_op jit(solution)/shard_map/ppermute | solution.py:49
  8.9 12.0 %collective-permute-start = (bf16[560,128]{1,0:T(8,128)(2,1)}, bf16[560,128]{1,0:T(8,128)(2,1)S(1)}, u32[]{:S(2)}, u32[]{:S(2)}) collective-permute-start(bf16[560,128]{1,0:T(8,128)(2,1)} %get-tuple-element.36.own), channel_id=1, source_target_pairs={{0,1},{1,0},{2,3},{3,2},{4,5},{5,4},{6,7},{7,6},{8,9},{9,8},{10,11... | collective-permute-start | bytes 430088 | tf_op jit(solution)/shard_map/ppermute | solution.py:49
  9.1 16.6 %collective-permute-start.7 = (bf16[16,4096]{1,0:T(8,128)(2,1)}, bf16[16,4096]{1,0:T(8,128)(2,1)S(1)}, u32[]{:S(2)}, u32[]{:S(2)}) collective-permute-start(bf16[16,4096]{1,0:T(8,128)(2,1)} %get-tuple-element.42), channel_id=1, source_target_pairs={{0,1},{2,3},{4,5},{6,7},{8,9},{10,11},{12,13},{14,15},{16,17},{18,... | collective-permute-start | bytes 393224 | tf_op jit(solution)/shard_map/ppermute | solution.py:49
  10.4 16.0 %collective-permute-start.6 = (bf16[560,128]{1,0:T(8,128)(2,1)}, bf16[560,128]{1,0:T(8,128)(2,1)S(1)}, u32[]{:S(2)}, u32[]{:S(2)}) collective-permute-start(bf16[560,128]{1,0:T(8,128)(2,1)} %get-tuple-element.36.own), channel_id=1, source_target_pairs={{6,18},{7,19},{14,26},{15,27},{16,4},{17,5},{22,34},{23,35},{24,12... | collective-permute-start | bytes 430088 | tf_op jit(solution)/shard_map/ppermute | solution.py:49
  14.7 11.6 %collective-permute-start.8 = (bf16[16,4096]{1,0:T(8,128)(2,1)}, bf16[16,4096]{1,0:T(8,128)(2,1)S(1)}, u32[]{:S(2)}, u32[]{:S(2)}) collective-permute-start(bf16[16,4096]{1,0:T(8,128)(2,1)} %get-tuple-element.43), channel_id=1, source_target_pairs={{1,2},{3,4},{5,6},{7,8},{9,10},{11,12},{13,14},{15,16},{17,18},{19... | collective-permute-start | bytes 393224 | tf_op jit(solution)/shard_map/ppermute | solution.py:49
  20.9 0.9 %copy-start.6 = (bf16[560,128]{1,0:T(8,128)(2,1)S(1)}, bf16[560,128]{1,0:T(8,128)(2,1)}, u32[]{:S(2)}) copy-start(bf16[560,128]{1,0:T(8,128)(2,1)} %get-tuple-element.36.own) | copy-start | bytes 430084
  21.9 4.8 %collective-permute-start.5 = (bf16[16,128]{1,0:T(8,128)(2,1)S(1)}, bf16[16,128]{1,0:T(8,128)(2,1)S(1)}, u32[]{:S(2)}, u32[]{:S(2)}) collective-permute-start(bf16[16,128]{1,0:T(8,128)(2,1)S(1)} %get-tuple-element.40), channel_id=1, source_target_pairs={{0,24},{1,25},{2,26},{3,27},{4,28},{5,29},{6,30},{7,31},{8,16},{9,... | collective-permute-start | bytes 12296 | tf_op jit(solution)/shard_map/ppermute | solution.py:49
  25.7 4.0 %collective-permute-start.4 = (bf16[16,128]{1,0:T(8,128)(2,1)S(1)}, bf16[16,128]{1,0:T(8,128)(2,1)S(1)}, u32[]{:S(2)}, u32[]{:S(2)}) collective-permute-start(bf16[16,128]{1,0:T(8,128)(2,1)S(1)} %get-tuple-element.40), channel_id=1, source_target_pairs={{0,16},{1,17},{2,18},{3,19},{4,20},{5,21},{6,22},{7,23},{8,24},{9,... | collective-permute-start | bytes 12296 | tf_op jit(solution)/shard_map/ppermute | solution.py:49
  25.7 4.0 %collective-permute-start.3 = (bf16[16,128]{1,0:T(8,128)(2,1)S(1)}, bf16[16,128]{1,0:T(8,128)(2,1)S(1)}, u32[]{:S(2)}, u32[]{:S(2)}) collective-permute-start(bf16[16,128]{1,0:T(8,128)(2,1)S(1)} %get-tuple-element.40), channel_id=1, source_target_pairs={{0,8},{1,9},{2,10},{3,11},{4,12},{5,13},{6,14},{7,15},{8,0},{9,1},... | collective-permute-start | bytes 12296 | tf_op jit(solution)/shard_map/ppermute | solution.py:49
  29.6 22.6 %collective-permute-start.13 = (bf16[2240,128]{1,0:T(8,128)(2,1)S(1)}, bf16[2240,128]{1,0:T(8,128)(2,1)S(1)}, u32[]{:S(2)}, u32[]{:S(2)}) collective-permute-start(bf16[2240,128]{1,0:T(8,128)(2,1)S(1)} %get-tuple-element.58.g0), channel_id=1, source_target_pairs={{8,16},{9,17},{10,18},{11,19},{12,20},{13,21},{14,22},{15,23},{24,... | collective-permute-start | bytes 1720328 | tf_op jit(solution)/shard_map/ppermute | solution.py:49
  30.3 21.9 %collective-permute-start.12 = (bf16[2240,128]{1,0:T(8,128)(2,1)S(1)}, bf16[2240,128]{1,0:T(8,128)(2,1)S(1)}, u32[]{:S(2)}, u32[]{:S(2)}) collective-permute-start(bf16[2240,128]{1,0:T(8,128)(2,1)S(1)} %get-tuple-element.58.g0), channel_id=1, source_target_pairs={{0,8},{1,9},{2,10},{3,11},{4,12},{5,13},{6,14},{7,15},{16,24},{17,... | collective-permute-start | bytes 1720328 | tf_op jit(solution)/shard_map/ppermute | solution.py:49
  32.8 2.5 %collective-permute-start.9 = (bf16[64,128]{1,0:T(8,128)(2,1)S(1)}, bf16[64,128]{1,0:T(8,128)(2,1)S(1)}, u32[]{:S(2)}, u32[]{:S(2)}) collective-permute-start(bf16[64,128]{1,0:T(8,128)(2,1)S(1)} %pad_maximum_fusion), channel_id=1, source_target_pairs={{0,4},{1,5},{2,6},{3,7},{4,0},{5,1},{6,2},{7,3},{8,12},{9,13},{10,... | collective-permute-start | bytes 49160 | tf_op jit(solution)/shard_map/ppermute | solution.py:49
  35.2 11.4 %collective-permute-start.10 = (bf16[128,128]{1,0:T(8,128)(2,1)S(1)}, bf16[128,128]{1,0:T(8,128)(2,1)S(1)}, u32[]{:S(2)}, u32[]{:S(2)}) collective-permute-start(bf16[128,128]{1,0:T(8,128)(2,1)S(1)} %constant_dynamic-update-slice_fusion), channel_id=1, source_target_pairs={{0,32},{1,33},{2,34},{3,35},{4,36},{5,37},{6,38},{7,39},{8,40},{9,... | collective-permute-start | bytes 98312 | tf_op jit(solution)/shard_map/ppermute | solution.py:49
  36.6 15.6 %collective-permute-start.15 = (bf16[560,128]{1,0:T(8,128)(2,1)S(1)}, bf16[560,128]{1,0:T(8,128)(2,1)S(1)}, u32[]{:S(2)}, u32[]{:S(2)}) collective-permute-start(bf16[560,128]{1,0:T(8,128)(2,1)S(1)} %collective-permute-done.6), channel_id=1, source_target_pairs={{0,3},{1,2},{2,1},{3,0},{4,7},{5,6},{6,5},{7,4},{8,11},{9,10},{10,... | collective-permute-start | bytes 430088 | tf_op jit(solution)/shard_map/ppermute | solution.py:49
  37.4 14.8 %collective-permute-start.14 = (bf16[560,128]{1,0:T(8,128)(2,1)S(1)}, bf16[560,128]{1,0:T(8,128)(2,1)S(1)}, u32[]{:S(2)}, u32[]{:S(2)}) collective-permute-start(bf16[560,128]{1,0:T(8,128)(2,1)S(1)} %collective-permute-done.6), channel_id=1, source_target_pairs={{0,2},{1,3},{2,0},{3,1},{4,6},{5,7},{6,4},{7,5},{8,10},{9,11},{10,... | collective-permute-start | bytes 430088 | tf_op jit(solution)/shard_map/ppermute | solution.py:49
  42.1 7.3 %copy-start = (bf16[316,64,64]{0,2,1:T(8,128)(2,1)S(1)}, bf16[316,64,64]{0,2,1:T(8,128)(2,1)}, u32[]{:S(2)}) copy-start(bf16[316,64,64]{0,2,1:T(8,128)(2,1)} %param.34) | copy-start | bytes 7766020
  46.6 7.8 %copy-start.4 = (bf16[32,64,64]{2,1,0:T(8,128)(2,1)S(1)}, bf16[32,64,64]{2,1,0:T(8,128)(2,1)}, u32[]{:S(2)}) copy-start(bf16[32,64,64]{2,1,0:T(8,128)(2,1)} %param.32) | copy-start | bytes 786436
  46.6 7.8 %copy-start.5 = (bf16[32,64,64]{2,1,0:T(8,128)(2,1)S(1)}, bf16[32,64,64]{2,1,0:T(8,128)(2,1)}, u32[]{:S(2)}) copy-start(bf16[32,64,64]{2,1,0:T(8,128)(2,1)} %dt_ref.1) | copy-start | bytes 786436
  46.6 7.8 %copy-start.7 = (bf16[8,64,64]{2,1,0:T(8,128)(2,1)S(1)}, bf16[8,64,64]{2,1,0:T(8,128)(2,1)}, u32[]{:S(2)}) copy-start(bf16[8,64,64]{2,1,0:T(8,128)(2,1)} %dn_ref.1) | copy-start | bytes 196612
  46.6 7.8 %copy-start.8 = (bf16[1,64,64]{2,1,0:T(8,128)(2,1)S(1)}, bf16[1,64,64]{2,1,0:T(8,128)(2,1)}, u32[]{:S(2)}) copy-start(bf16[1,64,64]{2,1,0:T(8,128)(2,1)} %param.31) | copy-start | bytes 24580
  46.6 7.8 %copy-start.12 = (s32[8,8]{1,0:T(8,128)S(1)}, s32[8,8]{1,0:T(8,128)}, u32[]{:S(2)}) copy-start(s32[8,8]{1,0:T(8,128)} %top_src.1) | copy-start | bytes 772
  46.6 7.8 %copy-start.13 = (s32[8,8]{1,0:T(8,128)S(1)}, s32[8,8]{1,0:T(8,128)}, u32[]{:S(2)}) copy-start(s32[8,8]{1,0:T(8,128)} %top_type.1) | copy-start | bytes 772
  46.6 7.8 %copy-start.14 = (s32[1,8]{1,0:T(1,128)S(1)}, s32[1,8]{1,0:T(1,128)}, u32[]{:S(2)}) copy-start(s32[1,8]{1,0:T(1,128)} %far_src.1) | copy-start | bytes 100
  46.6 7.8 %copy-start.15 = (s32[1,8]{1,0:T(1,128)S(1)}, s32[1,8]{1,0:T(1,128)}, u32[]{:S(2)}) copy-start(s32[1,8]{1,0:T(1,128)} %far_type.1) | copy-start | bytes 100
  46.7 5.5 %collective-permute-start.11 = (bf16[256,128]{1,0:T(8,128)(2,1)S(1)}, bf16[256,128]{1,0:T(8,128)(2,1)S(1)}, u32[]{:S(2)}, u32[]{:S(2)}) collective-permute-start(bf16[256,128]{1,0:T(8,128)(2,1)S(1)} %constant_dynamic-update-slice_fusion.5.c0), channel_id=1, source_target_pairs={{0,64},{1,65},{2,66},{3,67},{4,68},{5,69},{6,70},{7,71},{8,72},{9,... | collective-permute-start | bytes 196616 | tf_op jit(solution)/shard_map/ppermute | solution.py:49
  52.1 5.0 %copy-start.2 = (bf16[64,128,64]{1,2,0:T(8,128)(2,1)S(1)}, bf16[64,128,64]{1,2,0:T(8,128)(2,1)}, u32[]{:S(2)}) copy-start(bf16[64,128,64]{1,2,0:T(8,128)(2,1)} %param.23) | copy-start | bytes 3145732
  52.2 5.0 %copy-start.3 = (bf16[64,64,64]{2,1,0:T(8,128)(2,1)S(1)}, bf16[64,64,64]{2,1,0:T(8,128)(2,1)}, u32[]{:S(2)}) copy-start(bf16[64,64,64]{2,1,0:T(8,128)(2,1)} %down_buf.1) | copy-start | bytes 1572868
  52.2 5.0 %copy-start.10 = (s32[64,8]{0,1:T(8,128)S(1)}, s32[64,8]{0,1:T(8,128)}, u32[]{:S(2)}) copy-start(s32[64,8]{0,1:T(8,128)} %param.36) | copy-start | bytes 6148
  52.2 5.0 %copy-start.11 = (s32[64,8]{0,1:T(8,128)S(1)}, s32[64,8]{0,1:T(8,128)}, u32[]{:S(2)}) copy-start(s32[64,8]{0,1:T(8,128)} %param.37) | copy-start | bytes 6148
  52.2 4.2 %collective-permute-start.16 = (bf16[2240,128]{1,0:T(8,128)(2,1)S(1)}, bf16[2240,128]{1,0:T(8,128)(2,1)S(1)}, u32[]{:S(2)}, u32[]{:S(2)}) collective-permute-start(bf16[2240,128]{1,0:T(8,128)(2,1)S(1)} %get-tuple-element.58.g0), channel_id=1, source_target_pairs={{0,4},{1,5},{2,6},{3,7},{4,0},{5,1},{6,2},{7,3},{8,12},{9,13},{10,... | collective-permute-start | bytes 1720328 | tf_op jit(solution)/shard_map/ppermute | solution.py:49
  53.9 2.6 %collective-permute-start.17 = (bf16[2240,128]{1,0:T(8,128)(2,1)S(1)}, bf16[2240,128]{1,0:T(8,128)(2,1)S(1)}, u32[]{:S(2)}, u32[]{:S(2)}) collective-permute-start(bf16[2240,128]{1,0:T(8,128)(2,1)S(1)} %collective-permute-done.12.z0), channel_id=1, source_target_pairs={{0,4},{1,5},{2,6},{3,7},{4,0},{5,1},{6,2},{7,3},{8,12},{9,13},{10,... | collective-permute-start | bytes 1720328 | tf_op jit(solution)/shard_map/ppermute | solution.py:49
  54.0 3.2 %collective-permute-start.18 = (bf16[2240,128]{1,0:T(8,128)(2,1)S(1)}, bf16[2240,128]{1,0:T(8,128)(2,1)S(1)}, u32[]{:S(2)}, u32[]{:S(2)}) collective-permute-start(bf16[2240,128]{1,0:T(8,128)(2,1)S(1)} %collective-permute-done.13.z2), channel_id=1, source_target_pairs={{0,4},{1,5},{2,6},{3,7},{4,0},{5,1},{6,2},{7,3},{8,12},{9,13},{10,... | collective-permute-start | bytes 1720328 | tf_op jit(solution)/shard_map/ppermute | solution.py:49

commit v6 on v5

--- a/solution.py
+++ b/solution.py
@@ -423,18 +423,18 @@
 
     for j, near_ref in enumerate((near0, near1)):
 
-        @pl.loop(0, LEAVES // 2, step=16)
+        @pl.loop(0, LEAVES // 2, step=32)
         def _(i):
-            leaves = [j * (LEAVES // 2) + i + u for u in range(16)]
+            leaves = [j * (LEAVES // 2) + i + u for u in range(32)]
             lefts = [left_side(t) for t in leaves]
             both = [dot(x, right_side(t)) for x, t in zip(lefts, leaves)]
             nodes = [node_ref[pl.ds(pl.multiple_of((t >> 3) * 16, 16), 16), :] for t in leaves[::8]]
             inherited = [dot(nodes[u // 8], down_buf[t]) for u, t in enumerate(leaves)]
             total = [(p[:16] + pltpu.roll(p[16:], RANK, 1))[:, :RANK] + q for p, q in zip(both, inherited)]
             out = [dot(p.astype(jnp.bfloat16), rows_buf[t]) for p, t in zip(total, leaves)]
-            near = near_ref[:, pl.ds(pl.multiple_of(i * PANEL, 16 * PANEL), 16 * PANEL)]
-            at = pl.multiple_of(leaves[0] * PANEL, 16 * PANEL)
-            out_ref[:, pl.ds(at, 16 * PANEL)] = jnp.concatenate(out, axis=1) + near
+            near = near_ref[:, pl.ds(pl.multiple_of(i * PANEL, 32 * PANEL), 32 * PANEL)]
+            at = pl.multiple_of(leaves[0] * PANEL, 32 * PANEL)
+            out_ref[:, pl.ds(at, 32 * PANEL)] = jnp.concatenate(out, axis=1) + near
 
 
 def far_field(slots, types, pieces, extra, turned, row_basis, down_leaf, near, node_local):

time: 65.9 us -> 64.1 us (0.973)
  Pallas kernels: 26.2 us -> 24.4 us
    pallas_call x1, Pallas kernels: 7.79 us -> 6.02 us  [far_field(): pl.pallas_call(far_kernel, in_specs=[vmem, smem] + [hbm] * 8 + [vmem] * 6...]
where the time goes in v6:
time: 64.1 us; the launch traced here: 63.2 us
  starting transfers between devices  29.5 us (46%)
  Pallas kernels  24.4 us (38%)
  waiting for transfers between devices  7.84 us (12%)
  local copies, waits for them, and re-layouts  1.04 us (2%)
    ppermute x19, starting transfers between devices, moved(): return lax.ppermute(value, AXES, pairs)  29.5 us
    pallas_call x2, Pallas kernels, near_field(): pl.pallas_call(functools.partial(near_kernel, first), in_specs=[pl.BlockS...  8.58 us
    ppermute x19, waiting for transfers between devices, moved(): return lax.ppermute(value, AXES, pairs)  7.84 us
    pallas_call x1, Pallas kernels, far_field(): pl.pallas_call(far_kernel, in_specs=[vmem, smem] + [hbm] * 8 + [vmem] * 6...  6.02 us
    pallas_call x1, Pallas kernels, up_sweep(): pl.pallas_call(up_kernel, in_specs=[hbm] * 5 + [vmem], out_specs=[vmem] *...  4.99 us
    pallas_call x1, Pallas kernels, turned_couplings(): pl.pallas_call(turn_kernel, grid=(steps,), in_specs=[pl.BlockSpec((2, HAL...  2.75 us
    pallas_call x1, Pallas kernels, down_sweep(): pl.pallas_call(down_kernel, in_specs=[smem] * 4 + [vmem] * 3 + [hbm] * 2...  1.99 us
  transfers between devices with their start and end apart: 19, of which 5 were waited for; matrix products, arithmetic and copies ran while one was open for 0% of the time, Pallas kernels for 21%

profile of v6, /device:TPU:1, one launch (start us, length us, event | category | flops | bytes accessed | tf_op | source)
XLA Modules:
  0.0 63.2 jit_solution(12031990681491726195)
XLA Ops:
  0.0 5.0 %up_sweep.1 = (bf16[560,128]{1,0:T(8,128)(2,1)}, bf16[16,4096]{1,0:T(8,128)(2,1)}, bf16[16,4096]{1,0:T(8,128)(2,1)}) custom-call(bf16[16,8192]{1,0:T(8,128)(2,1)} %own_ref.3, bf16[64,64,128]{2,1,0:T(8,128)(2,1)} %bitcast.20, bf16[64,64,64]{2,1,0:T(8,128)(2,1)} %ul_hbm.1, bf16[8,64,64]{2,1,0:T(8,128)(2,1)} %un_hbm.1, bf16[64,64]{1,0:T(8,128)(2,1)} %bitcast.21, ...), custom_call_target="tpu_custom_call" | custom-call | flops 1000 | bytes 1000 | tf_op jit(solution)/shard_map/up_sweep/pallas_call | solution.py:138
  5.0 3.4 %collective-permute-start.2 = (bf16[560,128]{1,0:T(8,128)(2,1)}, bf16[560,128]{1,0:T(8,128)(2,1)S(1)}, u32[]{:S(2)}, u32[]{:S(2)}) collective-permute-start(bf16[560,128]{1,0:T(8,128)(2,1)} %get-tuple-element.36.own), channel_id=1, source_target_pairs={{0,3},{1,2},{2,1},{3,0},{4,7},{5,6},{6,5},{7,4},{8,11},{9,10},{10,... | collective-permute-start | bytes 430088 | tf_op jit(solution)/shard_map/ppermute | solution.py:49
  8.4 0.5 collective-permute-start.1
  8.9 0.1 collective-permute-start
  9.1 1.3 %collective-permute-start.7 = (bf16[16,4096]{1,0:T(8,128)(2,1)}, bf16[16,4096]{1,0:T(8,128)(2,1)S(1)}, u32[]{:S(2)}, u32[]{:S(2)}) collective-permute-start(bf16[16,4096]{1,0:T(8,128)(2,1)} %get-tuple-element.42), channel_id=1, source_target_pairs={{0,1},{2,3},{4,5},{6,7},{8,9},{10,11},{12,13},{14,15},{16,17},{18,... | collective-permute-start | bytes 393224 | tf_op jit(solution)/shard_map/ppermute | solution.py:49
  10.4 1.3 %collective-permute-start.6 = (bf16[560,128]{1,0:T(8,128)(2,1)}, bf16[560,128]{1,0:T(8,128)(2,1)S(1)}, u32[]{:S(2)}, u32[]{:S(2)}) collective-permute-start(bf16[560,128]{1,0:T(8,128)(2,1)} %get-tuple-element.36.own), channel_id=1, source_target_pairs={{6,18},{7,19},{14,26},{15,27},{16,4},{17,5},{22,34},{23,35},{24,12... | collective-permute-start | bytes 430088 | tf_op jit(solution)/shard_map/ppermute | solution.py:49
  11.7 3.0 %collective-permute-done.2.x3 = bf16[560,128]{1,0:T(8,128)(2,1)S(1)} collective-permute-done((bf16[560,128]{1,0:T(8,128)(2,1)}, bf16[560,128]{1,0:T(8,128)(2,1)S(1)}, u32[]{:S(2)}, u32[]{:S(2)}) %collective-permute-start.2) | collective-permute-done | bytes 143392 | tf_op jit(solution)/shard_map/ppermute | solution.py:49
  14.7 6.1 %collective-permute-start.8 = (bf16[16,4096]{1,0:T(8,128)(2,1)}, bf16[16,4096]{1,0:T(8,128)(2,1)S(1)}, u32[]{:S(2)}, u32[]{:S(2)}) collective-permute-start(bf16[16,4096]{1,0:T(8,128)(2,1)} %get-tuple-element.43), channel_id=1, source_target_pairs={{1,2},{3,4},{5,6},{7,8},{9,10},{11,12},{13,14},{15,16},{17,18},{19... | collective-permute-start | bytes 393224 | tf_op jit(solution)/shard_map/ppermute | solution.py:49
  20.8 0.0 collective-permute-done.1.x2
  20.9 0.0 collective-permute-done.x1
  20.9 0.0 copy-start.6
  20.9 0.9 %copy-done.6 = bf16[560,128]{1,0:T(8,128)(2,1)S(1)} copy-done((bf16[560,128]{1,0:T(8,128)(2,1)S(1)}, bf16[560,128]{1,0:T(8,128)(2,1)}, u32[]{:S(2)}) %copy-start.6) | copy-done | bytes 143384
  21.8 0.1 join_blocks.1
  21.9 3.8 %collective-permute-start.5 = (bf16[16,128]{1,0:T(8,128)(2,1)S(1)}, bf16[16,128]{1,0:T(8,128)(2,1)S(1)}, u32[]{:S(2)}, u32[]{:S(2)}) collective-permute-start(bf16[16,128]{1,0:T(8,128)(2,1)S(1)} %get-tuple-element.40), channel_id=1, source_target_pairs={{0,24},{1,25},{2,26},{3,27},{4,28},{5,29},{6,30},{7,31},{8,16},{9,... | collective-permute-start | bytes 12296 | tf_op jit(solution)/shard_map/ppermute | solution.py:49
  25.7 0.0 collective-permute-start.4
  25.7 0.0 collective-permute-done.7.halo0
  25.7 0.7 %collective-permute-start.3 = (bf16[16,128]{1,0:T(8,128)(2,1)S(1)}, bf16[16,128]{1,0:T(8,128)(2,1)S(1)}, u32[]{:S(2)}, u32[]{:S(2)}) collective-permute-start(bf16[16,128]{1,0:T(8,128)(2,1)S(1)} %get-tuple-element.40), channel_id=1, source_target_pairs={{0,8},{1,9},{2,10},{3,11},{4,12},{5,13},{6,14},{7,15},{8,0},{9,1},... | collective-permute-start | bytes 12296 | tf_op jit(solution)/shard_map/ppermute | solution.py:49
  26.3 0.0 collective-permute-done.8.halo1
  26.3 0.0 collective-permute-done.6
  26.4 0.3 collective-permute-done.5
  26.7 3.0 %collective-permute-done.4 = bf16[16,128]{1,0:T(8,128)(2,1)S(1)} collective-permute-done((bf16[16,128]{1,0:T(8,128)(2,1)S(1)}, bf16[16,128]{1,0:T(8,128)(2,1)S(1)}, u32[]{:S(2)}, u32[]{:S(2)}) %collective-permute-start.4) | collective-permute-done | bytes 4128 | tf_op jit(solution)/shard_map/ppermute | solution.py:49
  29.6 0.0 collective-permute-done.3
  29.6 0.7 %collective-permute-start.13 = (bf16[2240,128]{1,0:T(8,128)(2,1)S(1)}, bf16[2240,128]{1,0:T(8,128)(2,1)S(1)}, u32[]{:S(2)}, u32[]{:S(2)}) collective-permute-start(bf16[2240,128]{1,0:T(8,128)(2,1)S(1)} %get-tuple-element.58.g0), channel_id=1, source_target_pairs={{8,16},{9,17},{10,18},{11,19},{12,20},{13,21},{14,22},{15,23},{24,... | collective-permute-start | bytes 1720328 | tf_op jit(solution)/shard_map/ppermute | solution.py:49
  30.3 2.4 %collective-permute-start.12 = (bf16[2240,128]{1,0:T(8,128)(2,1)S(1)}, bf16[2240,128]{1,0:T(8,128)(2,1)S(1)}, u32[]{:S(2)}, u32[]{:S(2)}) collective-permute-start(bf16[2240,128]{1,0:T(8,128)(2,1)S(1)} %get-tuple-element.58.g0), channel_id=1, source_target_pairs={{0,8},{1,9},{2,10},{3,11},{4,12},{5,13},{6,14},{7,15},{16,24},{17,... | collective-permute-start | bytes 1720328 | tf_op jit(solution)/shard_map/ppermute | solution.py:49
  32.8 1.6 %collective-permute-start.9 = (bf16[64,128]{1,0:T(8,128)(2,1)S(1)}, bf16[64,128]{1,0:T(8,128)(2,1)S(1)}, u32[]{:S(2)}, u32[]{:S(2)}) collective-permute-start(bf16[64,128]{1,0:T(8,128)(2,1)S(1)} %pad_maximum_fusion), channel_id=1, source_target_pairs={{0,4},{1,5},{2,6},{3,7},{4,0},{5,1},{6,2},{7,3},{8,12},{9,13},{10,... | collective-permute-start | bytes 49160 | tf_op jit(solution)/shard_map/ppermute | solution.py:49
  34.4 0.8 %collective-permute-done.9 = bf16[64,128]{1,0:T(8,128)(2,1)S(1)} collective-permute-done((bf16[64,128]{1,0:T(8,128)(2,1)S(1)}, bf16[64,128]{1,0:T(8,128)(2,1)S(1)}, u32[]{:S(2)}, u32[]{:S(2)}) %collective-permute-start.9) | collective-permute-done | bytes 16416 | tf_op jit(solution)/shard_map/ppermute | solution.py:49
  35.2 1.4 %collective-permute-start.10 = (bf16[128,128]{1,0:T(8,128)(2,1)S(1)}, bf16[128,128]{1,0:T(8,128)(2,1)S(1)}, u32[]{:S(2)}, u32[]{:S(2)}) collective-permute-start(bf16[128,128]{1,0:T(8,128)(2,1)S(1)} %constant_dynamic-update-slice_fusion), channel_id=1, source_target_pairs={{0,32},{1,33},{2,34},{3,35},{4,36},{5,37},{6,38},{7,39},{8,40},{9,... | collective-permute-start | bytes 98312 | tf_op jit(solution)/shard_map/ppermute | solution.py:49
  36.6 0.8 %collective-permute-start.15 = (bf16[560,128]{1,0:T(8,128)(2,1)S(1)}, bf16[560,128]{1,0:T(8,128)(2,1)S(1)}, u32[]{:S(2)}, u32[]{:S(2)}) collective-permute-start(bf16[560,128]{1,0:T(8,128)(2,1)S(1)} %collective-permute-done.6), channel_id=1, source_target_pairs={{0,3},{1,2},{2,1},{3,0},{4,7},{5,6},{6,5},{7,4},{8,11},{9,10},{10,... | collective-permute-start | bytes 430088 | tf_op jit(solution)/shard_map/ppermute | solution.py:49
  37.4 0.5 collective-permute-start.14
  37.9 0.0 copy-done.1
  37.9 0.0 copy-done.9
  37.9 4.1 %near_field.3.near1 = f32[16,4096]{1,0:T(8,128)S(1)} custom-call(s32[6,64]{1,0:T(8,128)S(1)} %bitcast.16, bf16[16,4096]{1,0:T(8,128)(2,1)S(1)} %collective-permute-done.7.halo0, bf16[16,8192]{1,0:T(8,128)(2,1)S(1)} %copy-done.1, bf16[16,4096]{1,0:T(8,128)(2,1)S(1)} %collective-permute-done.8.halo1, bf16[64,6,128,128]{3,2,1,0:T(8,128)(2,1)} %blocks_hbm.3), custom_call_target="tpu_custom_call" | custom-call | flops 1000 | bytes 1000 | tf_op jit(solution)/shard_map/near_field/pallas_call | solution.py:233
  42.1 0.0 copy-start
  42.1 4.4 %near_field.2.near0 = f32[16,4096]{1,0:T(8,128)S(1)} custom-call(s32[6,64]{1,0:T(8,128)S(1)} %bitcast.17, bf16[16,4096]{1,0:T(8,128)(2,1)S(1)} %collective-permute-done.7.halo0, bf16[16,8192]{1,0:T(8,128)(2,1)S(1)} %copy-done.1, bf16[16,4096]{1,0:T(8,128)(2,1)S(1)} %collective-permute-done.8.halo1, bf16[64,6,128,128]{3,2,1,0:T(8,128)(2,1)} %blocks_hbm.3), custom_call_target="tpu_custom_call" | custom-call | flops 1000 | bytes 1000 | tf_op jit(solution)/shard_map/near_field/pallas_call | solution.py:233
  46.6 0.0 copy-start.4
  46.6 0.0 copy-start.5
  46.6 0.0 copy-start.7
  46.6 0.0 copy-start.8
  46.6 0.0 copy-start.12
  46.6 0.0 copy-start.13
  46.6 0.0 copy-start.14
  46.6 0.0 copy-start.15
  46.7 0.0 collective-permute-done.10
  46.7 2.7 %collective-permute-start.11 = (bf16[256,128]{1,0:T(8,128)(2,1)S(1)}, bf16[256,128]{1,0:T(8,128)(2,1)S(1)}, u32[]{:S(2)}, u32[]{:S(2)}) collective-permute-start(bf16[256,128]{1,0:T(8,128)(2,1)S(1)} %constant_dynamic-update-slice_fusion.5.c0), channel_id=1, source_target_pairs={{0,64},{1,65},{2,66},{3,67},{4,68},{5,69},{6,70},{7,71},{8,72},{9,... | collective-permute-start | bytes 196616 | tf_op jit(solution)/shard_map/ppermute | solution.py:49
  49.4 0.0 copy-done
  49.4 2.8 %turn_couplings.1.turned_ref.turned = bf16[10112,128]{1,0:T(8,128)(2,1)S(1)} custom-call(bf16[2,2048,316]{2,1,0:T(8,128)(2,1)S(1)} %bitcast.12), custom_call_target="tpu_custom_call" | custom-call | flops 1000 | bytes 1000 | tf_op jit(solution)/shard_map/turn_couplings/pallas_call | solution.py:181
  52.1 0.0 copy-start.2
  52.2 0.0 copy-start.3
  52.2 0.0 copy-start.10
  52.2 0.0 copy-start.11
  52.2 0.0 collective-permute-done.11.c1
  52.2 0.0 collective-permute-done.15.e1
  52.2 0.0 collective-permute-done.14.e0
  52.2 0.0 collective-permute-done.13.z2
  52.2 0.0 collective-permute-done.12.z0
  52.2 1.6 %collective-permute-start.16 = (bf16[2240,128]{1,0:T(8,128)(2,1)S(1)}, bf16[2240,128]{1,0:T(8,128)(2,1)S(1)}, u32[]{:S(2)}, u32[]{:S(2)}) collective-permute-start(bf16[2240,128]{1,0:T(8,128)(2,1)S(1)} %get-tuple-element.58.g0), channel_id=1, source_target_pairs={{0,4},{1,5},{2,6},{3,7},{4,0},{5,1},{6,2},{7,3},{8,12},{9,13},{10,... | collective-permute-start | bytes 1720328 | tf_op jit(solution)/shard_map/ppermute | solution.py:49
  53.9 0.1 collective-permute-start.17
  54.0 0.4 collective-permute-start.18
  54.4 2.0 %down_sweep.1.node_ref = bf16[128,64]{1,0:T(8,128)(2,1)S(1)} custom-call(s32[1,8]{1,0:T(1,128)S(1)} %copy-done.14, s32[1,8]{1,0:T(1,128)S(1)} %copy-done.15, s32[8,8]{1,0:T(8,128)S(1)} %copy-done.12, s32[8,8]{1,0:T(8,128)S(1)} %copy-done.13, bf16[256,128]{1,0:T(8,128)(2,1)S(1)} %constant_dynamic-update-slice_fusion.5.c0, ...), custom_call_target="tpu_custom_call" | custom-call | flops 1000 | bytes 1000 | tf_op jit(solution)/shard_map/down_sweep/pallas_call | solution.py:337
  56.4 0.0 collective-permute-done.16.g1
  56.5 0.0 collective-permute-done.17.z1
  56.5 0.7 %collective-permute-done.18.z3 = bf16[2240,128]{1,0:T(8,128)(2,1)S(1)} collective-permute-done((bf16[2240,128]{1,0:T(8,128)(2,1)S(1)}, bf16[2240,128]{1,0:T(8,128)(2,1)S(1)}, u32[]{:S(2)}, u32[]{:S(2)}) %collective-permute-start.18) | collective-permute-done | bytes 573472 | tf_op jit(solution)/shard_map/ppermute | solution.py:49
  57.1 0.0 copy-done.10
  57.1 6.0 %far_field.1 = f32[16,8192]{1,0:T(8,128)} custom-call(s32[8,64]{1,0:T(8,128)S(1)} %bitcast.18, s32[8,64]{1,0:T(8,128)S(1)} %bitcast.19, bf16[2240,128]{1,0:T(8,128)(2,1)S(1)} %get-tuple-element.58.g0, bf16[2240,128]{1,0:T(8,128)(2,1)S(1)} %collective-permute-done.16.g1, bf16[2240,128]{1,0:T(8,128)(2,1)S(1)} %collective-permute-done.12.z0, ...), custom_call_target="tpu_custom_call" | custom-call | flops 1000 | bytes 1000 | tf_op jit(solution)/shard_map/far_field/pallas_call | solution.py:444
  (21 shorter events, 0.1 us)
Async XLA Ops:
  0.0 37.9 %copy-start.1 = (bf16[16,8192]{1,0:T(8,128)(2,1)S(1)}, bf16[16,8192]{1,0:T(8,128)(2,1)}, u32[]{:S(2)}) copy-start(bf16[16,8192]{1,0:T(8,128)(2,1)} %own_ref.3) | copy-start | bytes 786436
  0.0 37.9 %copy-start.9 = (s32[64,6]{0,1:T(8,128)S(1)}, s32[64,6]{0,1:T(8,128)}, u32[]{:S(2)}) copy-start(s32[64,6]{0,1:T(8,128)} %param.25) | copy-start | bytes 4612
  5.0 9.7 %collective-permute-start.2 = (bf16[560,128]{1,0:T(8,128)(2,1)}, bf16[560,128]{1,0:T(8,128)(2,1)S(1)}, u32[]{:S(2)}, u32[]{:S(2)}) collective-permute-start(bf16[560,128]{1,0:T(8,128)(2,1)} %get-tuple-element.36.own), channel_id=1, source_target_pairs={{0,3},{1,2},{2,1},{3,0},{4,7},{5,6},{6,5},{7,4},{8,11},{9,10},{10,... | collective-permute-start | bytes 430088 | tf_op jit(solution)/shard_map/ppermute | solution.py:49
  8.4 12.5 %collective-permute-start.1 = (bf16[560,128]{1,0:T(8,128)(2,1)}, bf16[560,128]{1,0:T(8,128)(2,1)S(1)}, u32[]{:S(2)}, u32[]{:S(2)}) collective-permute-start(bf16[560,128]{1,0:T(8,128)(2,1)} %get-tuple-element.36.own), channel_id=1, source_target_pairs={{0,2},{1,3},{2,0},{3,1},{4,6},{5,7},{6,4},{7,5},{8,10},{9,11},{10,... | collective-permute-start | bytes 430088 | tf_op jit(solution)/shard_map/ppermute | solution.py:49
  8.9 12.0 %collective-permute-start = (bf16[560,128]{1,0:T(8,128)(2,1)}, bf16[560,128]{1,0:T(8,128)(2,1)S(1)}, u32[]{:S(2)}, u32[]{:S(2)}) collective-permute-start(bf16[560,128]{1,0:T(8,128)(2,1)} %get-tuple-element.36.own), channel_id=1, source_target_pairs={{0,1},{1,0},{2,3},{3,2},{4,5},{5,4},{6,7},{7,6},{8,9},{9,8},{10,11... | collective-permute-start | bytes 430088 | tf_op jit(solution)/shard_map/ppermute | solution.py:49
  9.1 16.6 %collective-permute-start.7 = (bf16[16,4096]{1,0:T(8,128)(2,1)}, bf16[16,4096]{1,0:T(8,128)(2,1)S(1)}, u32[]{:S(2)}, u32[]{:S(2)}) collective-permute-start(bf16[16,4096]{1,0:T(8,128)(2,1)} %get-tuple-element.42), channel_id=1, source_target_pairs={{0,1},{2,3},{4,5},{6,7},{8,9},{10,11},{12,13},{14,15},{16,17},{18,... | collective-permute-start | bytes 393224 | tf_op jit(solution)/shard_map/ppermute | solution.py:49
  10.4 16.0 %collective-permute-start.6 = (bf16[560,128]{1,0:T(8,128)(2,1)}, bf16[560,128]{1,0:T(8,128)(2,1)S(1)}, u32[]{:S(2)}, u32[]{:S(2)}) collective-permute-start(bf16[560,128]{1,0:T(8,128)(2,1)} %get-tuple-element.36.own), channel_id=1, source_target_pairs={{6,18},{7,19},{14,26},{15,27},{16,4},{17,5},{22,34},{23,35},{24,12... | collective-permute-start | bytes 430088 | tf_op jit(solution)/shard_map/ppermute | solution.py:49
  14.7 11.6 %collective-permute-start.8 = (bf16[16,4096]{1,0:T(8,128)(2,1)}, bf16[16,4096]{1,0:T(8,128)(2,1)S(1)}, u32[]{:S(2)}, u32[]{:S(2)}) collective-permute-start(bf16[16,4096]{1,0:T(8,128)(2,1)} %get-tuple-element.43), channel_id=1, source_target_pairs={{1,2},{3,4},{5,6},{7,8},{9,10},{11,12},{13,14},{15,16},{17,18},{19... | collective-permute-start | bytes 393224 | tf_op jit(solution)/shard_map/ppermute | solution.py:49
  20.9 0.9 %copy-start.6 = (bf16[560,128]{1,0:T(8,128)(2,1)S(1)}, bf16[560,128]{1,0:T(8,128)(2,1)}, u32[]{:S(2)}) copy-start(bf16[560,128]{1,0:T(8,128)(2,1)} %get-tuple-element.36.own) | copy-start | bytes 430084
  21.9 4.8 %collective-permute-start.5 = (bf16[16,128]{1,0:T(8,128)(2,1)S(1)}, bf16[16,128]{1,0:T(8,128)(2,1)S(1)}, u32[]{:S(2)}, u32[]{:S(2)}) collective-permute-start(bf16[16,128]{1,0:T(8,128)(2,1)S(1)} %get-tuple-element.40), channel_id=1, source_target_pairs={{0,24},{1,25},{2,26},{3,27},{4,28},{5,29},{6,30},{7,31},{8,16},{9,... | collective-permute-start | bytes 12296 | tf_op jit(solution)/shard_map/ppermute | solution.py:49
  25.7 4.0 %collective-permute-start.4 = (bf16[16,128]{1,0:T(8,128)(2,1)S(1)}, bf16[16,128]{1,0:T(8,128)(2,1)S(1)}, u32[]{:S(2)}, u32[]{:S(2)}) collective-permute-start(bf16[16,128]{1,0:T(8,128)(2,1)S(1)} %get-tuple-element.40), channel_id=1, source_target_pairs={{0,16},{1,17},{2,18},{3,19},{4,20},{5,21},{6,22},{7,23},{8,24},{9,... | collective-permute-start | bytes 12296 | tf_op jit(solution)/shard_map/ppermute | solution.py:49
  25.7 4.0 %collective-permute-start.3 = (bf16[16,128]{1,0:T(8,128)(2,1)S(1)}, bf16[16,128]{1,0:T(8,128)(2,1)S(1)}, u32[]{:S(2)}, u32[]{:S(2)}) collective-permute-start(bf16[16,128]{1,0:T(8,128)(2,1)S(1)} %get-tuple-element.40), channel_id=1, source_target_pairs={{0,8},{1,9},{2,10},{3,11},{4,12},{5,13},{6,14},{7,15},{8,0},{9,1},... | collective-permute-start | bytes 12296 | tf_op jit(solution)/shard_map/ppermute | solution.py:49
  29.6 22.6 %collective-permute-start.13 = (bf16[2240,128]{1,0:T(8,128)(2,1)S(1)}, bf16[2240,128]{1,0:T(8,128)(2,1)S(1)}, u32[]{:S(2)}, u32[]{:S(2)}) collective-permute-start(bf16[2240,128]{1,0:T(8,128)(2,1)S(1)} %get-tuple-element.58.g0), channel_id=1, source_target_pairs={{8,16},{9,17},{10,18},{11,19},{12,20},{13,21},{14,22},{15,23},{24,... | collective-permute-start | bytes 1720328 | tf_op jit(solution)/shard_map/ppermute | solution.py:49
  30.3 21.9 %collective-permute-start.12 = (bf16[2240,128]{1,0:T(8,128)(2,1)S(1)}, bf16[2240,128]{1,0:T(8,128)(2,1)S(1)}, u32[]{:S(2)}, u32[]{:S(2)}) collective-permute-start(bf16[2240,128]{1,0:T(8,128)(2,1)S(1)} %get-tuple-element.58.g0), channel_id=1, source_target_pairs={{0,8},{1,9},{2,10},{3,11},{4,12},{5,13},{6,14},{7,15},{16,24},{17,... | collective-permute-start | bytes 1720328 | tf_op jit(solution)/shard_map/ppermute | solution.py:49
  32.8 2.5 %collective-permute-start.9 = (bf16[64,128]{1,0:T(8,128)(2,1)S(1)}, bf16[64,128]{1,0:T(8,128)(2,1)S(1)}, u32[]{:S(2)}, u32[]{:S(2)}) collective-permute-start(bf16[64,128]{1,0:T(8,128)(2,1)S(1)} %pad_maximum_fusion), channel_id=1, source_target_pairs={{0,4},{1,5},{2,6},{3,7},{4,0},{5,1},{6,2},{7,3},{8,12},{9,13},{10,... | collective-permute-start | bytes 49160 | tf_op jit(solution)/shard_map/ppermute | solution.py:49
  35.2 11.4 %collective-permute-start.10 = (bf16[128,128]{1,0:T(8,128)(2,1)S(1)}, bf16[128,128]{1,0:T(8,128)(2,1)S(1)}, u32[]{:S(2)}, u32[]{:S(2)}) collective-permute-start(bf16[128,128]{1,0:T(8,128)(2,1)S(1)} %constant_dynamic-update-slice_fusion), channel_id=1, source_target_pairs={{0,32},{1,33},{2,34},{3,35},{4,36},{5,37},{6,38},{7,39},{8,40},{9,... | collective-permute-start | bytes 98312 | tf_op jit(solution)/shard_map/ppermute | solution.py:49
  36.6 15.6 %collective-permute-start.15 = (bf16[560,128]{1,0:T(8,128)(2,1)S(1)}, bf16[560,128]{1,0:T(8,128)(2,1)S(1)}, u32[]{:S(2)}, u32[]{:S(2)}) collective-permute-start(bf16[560,128]{1,0:T(8,128)(2,1)S(1)} %collective-permute-done.6), channel_id=1, source_target_pairs={{0,3},{1,2},{2,1},{3,0},{4,7},{5,6},{6,5},{7,4},{8,11},{9,10},{10,... | collective-permute-start | bytes 430088 | tf_op jit(solution)/shard_map/ppermute | solution.py:49
  37.4 14.8 %collective-permute-start.14 = (bf16[560,128]{1,0:T(8,128)(2,1)S(1)}, bf16[560,128]{1,0:T(8,128)(2,1)S(1)}, u32[]{:S(2)}, u32[]{:S(2)}) collective-permute-start(bf16[560,128]{1,0:T(8,128)(2,1)S(1)} %collective-permute-done.6), channel_id=1, source_target_pairs={{0,2},{1,3},{2,0},{3,1},{4,6},{5,7},{6,4},{7,5},{8,10},{9,11},{10,... | collective-permute-start | bytes 430088 | tf_op jit(solution)/shard_map/ppermute | solution.py:49
  42.1 7.3 %copy-start = (bf16[316,64,64]{0,2,1:T(8,128)(2,1)S(1)}, bf16[316,64,64]{0,2,1:T(8,128)(2,1)}, u32[]{:S(2)}) copy-start(bf16[316,64,64]{0,2,1:T(8,128)(2,1)} %param.34) | copy-start | bytes 7766020
  46.6 7.8 %copy-start.4 = (bf16[32,64,64]{2,1,0:T(8,128)(2,1)S(1)}, bf16[32,64,64]{2,1,0:T(8,128)(2,1)}, u32[]{:S(2)}) copy-start(bf16[32,64,64]{2,1,0:T(8,128)(2,1)} %param.32) | copy-start | bytes 786436
  46.6 7.8 %copy-start.5 = (bf16[32,64,64]{2,1,0:T(8,128)(2,1)S(1)}, bf16[32,64,64]{2,1,0:T(8,128)(2,1)}, u32[]{:S(2)}) copy-start(bf16[32,64,64]{2,1,0:T(8,128)(2,1)} %dt_ref.1) | copy-start | bytes 786436
  46.6 7.8 %copy-start.7 = (bf16[8,64,64]{2,1,0:T(8,128)(2,1)S(1)}, bf16[8,64,64]{2,1,0:T(8,128)(2,1)}, u32[]{:S(2)}) copy-start(bf16[8,64,64]{2,1,0:T(8,128)(2,1)} %dn_ref.1) | copy-start | bytes 196612
  46.6 7.8 %copy-start.8 = (bf16[1,64,64]{2,1,0:T(8,128)(2,1)S(1)}, bf16[1,64,64]{2,1,0:T(8,128)(2,1)}, u32[]{:S(2)}) copy-start(bf16[1,64,64]{2,1,0:T(8,128)(2,1)} %param.31) | copy-start | bytes 24580
  46.6 7.8 %copy-start.12 = (s32[8,8]{1,0:T(8,128)S(1)}, s32[8,8]{1,0:T(8,128)}, u32[]{:S(2)}) copy-start(s32[8,8]{1,0:T(8,128)} %top_src.1) | copy-start | bytes 772
  46.6 7.8 %copy-start.13 = (s32[8,8]{1,0:T(8,128)S(1)}, s32[8,8]{1,0:T(8,128)}, u32[]{:S(2)}) copy-start(s32[8,8]{1,0:T(8,128)} %top_type.1) | copy-start | bytes 772
  46.6 7.8 %copy-start.14 = (s32[1,8]{1,0:T(1,128)S(1)}, s32[1,8]{1,0:T(1,128)}, u32[]{:S(2)}) copy-start(s32[1,8]{1,0:T(1,128)} %far_src.1) | copy-start | bytes 100
  46.6 7.8 %copy-start.15 = (s32[1,8]{1,0:T(1,128)S(1)}, s32[1,8]{1,0:T(1,128)}, u32[]{:S(2)}) copy-start(s32[1,8]{1,0:T(1,128)} %far_type.1) | copy-start | bytes 100
  46.7 5.5 %collective-permute-start.11 = (bf16[256,128]{1,0:T(8,128)(2,1)S(1)}, bf16[256,128]{1,0:T(8,128)(2,1)S(1)}, u32[]{:S(2)}, u32[]{:S(2)}) collective-permute-start(bf16[256,128]{1,0:T(8,128)(2,1)S(1)} %constant_dynamic-update-slice_fusion.5.c0), channel_id=1, source_target_pairs={{0,64},{1,65},{2,66},{3,67},{4,68},{5,69},{6,70},{7,71},{8,72},{9,... | collective-permute-start | bytes 196616 | tf_op jit(solution)/shard_map/ppermute | solution.py:49
  52.1 5.0 %copy-start.2 = (bf16[64,128,64]{1,2,0:T(8,128)(2,1)S(1)}, bf16[64,128,64]{1,2,0:T(8,128)(2,1)}, u32[]{:S(2)}) copy-start(bf16[64,128,64]{1,2,0:T(8,128)(2,1)} %param.23) | copy-start | bytes 3145732
  52.2 5.0 %copy-start.3 = (bf16[64,64,64]{2,1,0:T(8,128)(2,1)S(1)}, bf16[64,64,64]{2,1,0:T(8,128)(2,1)}, u32[]{:S(2)}) copy-start(bf16[64,64,64]{2,1,0:T(8,128)(2,1)} %down_buf.1) | copy-start | bytes 1572868
  52.2 5.0 %copy-start.10 = (s32[64,8]{0,1:T(8,128)S(1)}, s32[64,8]{0,1:T(8,128)}, u32[]{:S(2)}) copy-start(s32[64,8]{0,1:T(8,128)} %param.36) | copy-start | bytes 6148
  52.2 5.0 %copy-start.11 = (s32[64,8]{0,1:T(8,128)S(1)}, s32[64,8]{0,1:T(8,128)}, u32[]{:S(2)}) copy-start(s32[64,8]{0,1:T(8,128)} %param.37) | copy-start | bytes 6148
  52.2 4.2 %collective-permute-start.16 = (bf16[2240,128]{1,0:T(8,128)(2,1)S(1)}, bf16[2240,128]{1,0:T(8,128)(2,1)S(1)}, u32[]{:S(2)}, u32[]{:S(2)}) collective-permute-start(bf16[2240,128]{1,0:T(8,128)(2,1)S(1)} %get-tuple-element.58.g0), channel_id=1, source_target_pairs={{0,4},{1,5},{2,6},{3,7},{4,0},{5,1},{6,2},{7,3},{8,12},{9,13},{10,... | collective-permute-start | bytes 1720328 | tf_op jit(solution)/shard_map/ppermute | solution.py:49
  53.9 2.6 %collective-permute-start.17 = (bf16[2240,128]{1,0:T(8,128)(2,1)S(1)}, bf16[2240,128]{1,0:T(8,128)(2,1)S(1)}, u32[]{:S(2)}, u32[]{:S(2)}) collective-permute-start(bf16[2240,128]{1,0:T(8,128)(2,1)S(1)} %collective-permute-done.12.z0), channel_id=1, source_target_pairs={{0,4},{1,5},{2,6},{3,7},{4,0},{5,1},{6,2},{7,3},{8,12},{9,13},{10,... | collective-permute-start | bytes 1720328 | tf_op jit(solution)/shard_map/ppermute | solution.py:49
  54.0 3.2 %collective-permute-start.18 = (bf16[2240,128]{1,0:T(8,128)(2,1)S(1)}, bf16[2240,128]{1,0:T(8,128)(2,1)S(1)}, u32[]{:S(2)}, u32[]{:S(2)}) collective-permute-start(bf16[2240,128]{1,0:T(8,128)(2,1)S(1)} %collective-permute-done.13.z2), channel_id=1, source_target_pairs={{0,4},{1,5},{2,6},{3,7},{4,0},{5,1},{6,2},{7,3},{8,12},{9,13},{10,... | collective-permute-start | bytes 1720328 | tf_op jit(solution)/shard_map/ppermute | solution.py:49
